TPU v7x, 256 devices: a whole 4x4x8 slice. The times are simulated.
256 devices in a mesh: dp: 32 (over z, x_hi, core), tensor: 8 (over y, x_lo).
Axes of the slice: x: 4 (x_hi: 2, x_lo: 2; x = x_hi * 2 + x_lo), y: 4, z: 8, core: 2. Of those that a mesh axis runs over, the one named last changes fastest.
Arguments:
- tokens: bfloat16 [24576, 5120], P('dp'), may hold values from -6 to 6
- lengths: int32 [32, 8], P('dp'), may hold values from 1 to 384, 768 in all within a row
- qkv_weight: bfloat16 [5120, 10240], P(('dp', 'tensor')), may hold values from -0.056181208 to 0.056181208
- query_norm_gain: float32 [128], replicated, may hold values from 0.6 to 5
- key_norm_gain: float32 [128], replicated, may hold values from 0.6 to 5
Outputs:
- attended: bfloat16 [24576, 8192], P('dp', 'tensor')
All inputs are finite; a program needn't handle non-finite values.
Results may differ from a plain program's by a relative error of at most 0.012.
The roundings to bfloat16 on the way count: a program that leaves them out, or rounds other values in their place, can miss the bound.
Values may be sent and summed in bfloat16 or wider, within the bound.
No kernel may reach another device: no remote copies, remote signals or barrier semaphores. Data moves between devices by JAX's collectives and lax.ppermute only.
A program may use at most 128 MiB of HBM per device.

v0:
```python
import math

import jax
import jax.numpy as jnp
from jax import lax
from jax.sharding import PartitionSpec as P

QUERY_HEADS = 64
KEY_VALUE_HEADS = 8


ROPE_BASE = 1000000.0
NORM_EPS = 1e-06


def request_starts(length_row, row_count):
    ending = jnp.cumsum(length_row)
    offsets = ending - length_row
    row_ids = jnp.arange(row_count, dtype=jnp.int32)
    reached = offsets[None, :] <= row_ids[:, None]
    return jnp.max(jnp.where(reached, offsets[None, :], 0), axis=1)


def head_norm(field, gain):
    return field * lax.rsqrt(jnp.mean(field * field, axis=-1, keepdims=True) + NORM_EPS) * gain


def rotary(field, token_positions):
    head_width = field.shape[-1]
    half_size = head_width // 2
    frequency = ROPE_BASE ** (-jnp.arange(half_size, dtype=jnp.float32) * 2.0 / head_width)
    angles = token_positions[:, None] * frequency[None, :]
    cosine = jnp.concatenate([jnp.cos(angles), jnp.cos(angles)], axis=1)[:, None, :]
    sine_table = jnp.concatenate([jnp.sin(angles), jnp.sin(angles)], axis=1)[:, None, :]
    front_half = field[..., :half_size]
    back_half = field[..., half_size:]
    turned = jnp.concatenate([-back_half, front_half], axis=-1)
    return field * cosine + turned * sine_table


def divide_heads(
    query_key_value, q_heads, kv_heads, query_norm_gain, key_norm_gain, token_positions
):
    row_count = query_key_value.shape[0]
    head_width = query_norm_gain.shape[0]
    q_end = q_heads * head_width
    k_end = q_end + kv_heads * head_width
    query_rows = query_key_value[:, :q_end].reshape(row_count, q_heads, head_width)
    heads_of_keys = query_key_value[:, q_end:k_end].reshape(row_count, kv_heads, head_width)
    query_rows = rotary(head_norm(query_rows, query_norm_gain), token_positions).astype(
        jnp.bfloat16
    )
    heads_of_keys = rotary(head_norm(heads_of_keys, key_norm_gain), token_positions).astype(
        jnp.bfloat16
    )
    value_rows = (
        query_key_value[:, k_end:].reshape(row_count, kv_heads, head_width).astype(jnp.bfloat16)
    )
    heads_per_group = q_heads // kv_heads
    query_rows = query_rows.reshape(row_count, kv_heads, heads_per_group, head_width)
    return (query_rows, heads_of_keys, value_rows)


def join_columns(weight, groups, head_width):
    row_count = weight.shape[0]
    q_total = QUERY_HEADS * head_width
    key_value_total = KEY_VALUE_HEADS * head_width
    query_part = weight[:, :q_total].reshape(row_count, groups, q_total // groups)
    key_part = weight[:, q_total : q_total + key_value_total].reshape(
        row_count, groups, key_value_total // groups
    )
    value_part = weight[:, q_total + key_value_total :].reshape(
        row_count, groups, key_value_total // groups
    )
    return jnp.concatenate([query_part, key_part, value_part], axis=2)


def block_scores(query_rows, heads_of_keys):
    scores = jnp.einsum(
        "qhgd,khd->hgqk", query_rows, heads_of_keys, preferred_element_type=jnp.float32
    )
    return scores * (1.0 / math.sqrt(query_rows.shape[3]))


def softmax_weights(scores, request_start):
    query_count = scores.shape[2]
    key_count = scores.shape[3]
    query_pos = jnp.arange(query_count, dtype=jnp.int32)
    key_pos = jnp.arange(key_count, dtype=jnp.int32)
    allowed = (key_pos[None, :] <= query_pos[:, None]) & (
        key_pos[None, :] >= request_start[:, None]
    )
    masked = jnp.where(allowed[None, None], scores, -1e30)
    row_max = jnp.max(masked, axis=3, keepdims=True)
    exponent = jnp.exp(masked - row_max)
    return (exponent / jnp.sum(exponent, axis=3, keepdims=True)).astype(jnp.bfloat16)


def shards(tokens, lengths, qkv_weight, query_norm_gain, key_norm_gain):
    width_per_tensor = lax.axis_size("tensor")
    replicas = lax.axis_size("dp")
    row_count = tokens.shape[0]
    head_width = query_norm_gain.shape[0]
    q_local = QUERY_HEADS // width_per_tensor
    key_value_local = KEY_VALUE_HEADS // width_per_tensor
    joined_width = (q_local + 2 * key_value_local) * head_width
    piece_rows = qkv_weight.shape[0]
    stacked = lax.all_gather(qkv_weight, "dp", axis=0, tiled=True)
    grouped = join_columns(stacked, width_per_tensor, head_width)
    swapped = lax.all_to_all(grouped, "tensor", split_axis=1, concat_axis=0, tiled=True)
    ordered = swapped.reshape(width_per_tensor, replicas, piece_rows, joined_width)
    ordered = ordered.transpose(1, 0, 2, 3).reshape(-1, joined_width)
    query_key_value = jnp.dot(tokens, ordered, preferred_element_type=jnp.float32)
    request_start = request_starts(lengths[0], row_count)
    token_positions = (jnp.arange(row_count, dtype=jnp.int32) - request_start).astype(jnp.float32)
    query_rows, heads_of_keys, value_rows = divide_heads(
        query_key_value, q_local, key_value_local, query_norm_gain, key_norm_gain, token_positions
    )
    block_rows = min(768, row_count)
    scores = block_scores(query_rows, heads_of_keys)
    weights = softmax_weights(scores, request_start)
    mixed = jnp.einsum("hgqk,khd->qhgd", weights, value_rows, preferred_element_type=jnp.float32)
    outputs = mixed.reshape(block_rows, -1).astype(jnp.bfloat16)
    return outputs


def solution(mesh):
    in_specs = (P("dp", None), P("dp", None), P(("dp", "tensor"), None), P(), P())
    out_specs = P("dp", "tensor")
    return jax.shard_map(shards, mesh=mesh, in_specs=in_specs, out_specs=out_specs, check_vma=False)
```

profile of v0, /device:TPU:1, one launch (start us, length us, event | category | flops | bytes accessed | tf_op | source)
XLA Modules:
  0.0 448.8 jit_solution(7274158806654851332)
XLA Ops:
  6.5 0.0 all-gather.3.cloned.1.call-start
  6.5 0.7 all-gather.3.cloned.1.call-update
  7.3 139.7 %all-gather.3.cloned.1.call-done = bf16[32,20,10240]{2,1,0:T(8,128)(2,1)} async-done(((bf16[1,20,10240]{2,1,0:T(8,128)(2,1)}), bf16[32,20,10240]{2,1,0:T(8,128)(2,1)}) %all-gather.3.cloned.1.call-update) | async-done | bytes 13107216 | tf_op jit(solution)/shard_map/all_gather | solution.py:108
  147.0 16.9 %reshape.159 = bf16[640,10240]{1,0:T(8,128)(2,1)} reshape(bf16[32,20,10240]{2,1,0:T(8,128)(2,1)} %all-gather.3.cloned.1.call-done) | data formatting | bytes 26214400
  163.9 2.3 slice_bitcast_fusion.1
  166.2 9.2 %slice.41 = bf16[640,8192]{1,0:T(8,128)(2,1)} slice(bf16[640,10240]{1,0:T(8,128)(2,1)} %reshape.159), slice={[0:640], [0:8192]} | slice | bytes 20971520 | tf_op jit(solution)/shard_map/slice | solution.py:68
  175.4 9.6 %copy.47 = bf16[80,8,8,1024]{3,2,0,1:T(8,128)(2,1)} copy(bf16[80,8,8,1024]{3,2,1,0:T(8,128)(2,1)} %bitcast.88) | data formatting | bytes 20971520 | tf_op jit(solution)/shard_map/reshape | solution.py:68
  185.1 0.6 copy_bitcast_fusion.1
  185.7 10.1 %pad_maximum_fusion = bf16[640,8,1280]{2,0,1:T(8,128)(2,1)} fusion(bf16[640,8,128]{2,0,1:T(8,128)(2,1)S(1)} %get-tuple-element.15, bf16[640,8,128]{2,0,1:T(8,128)(2,1)S(1)} %get-tuple-element.16, bf16[640,8,1024]{2,0,1:T(8,128)(2,1)} %bitcast.87), kind=kLoop, calls=%fused_computation.5 | loop fusion | flops 39321600 | bytes 26214400 | tf_op jit(solution)/shard_map/concatenate | solution.py:75
  195.9 5.7 %all-to-all-start = ((bf16[640,8,1280]{2,0,1:T(8,128)(2,1)}), bf16[640,8,1280]{2,0,1:T(8,128)(2,1)}, u32[]{:S(2)}, u32[]{:S(2)}) async-start(bf16[640,8,1280]{2,0,1:T(8,128)(2,1)} %pad_maximum_fusion), calls=%async_computation | async-start | bytes 26214400 | tf_op jit(solution)/shard_map/all_to_all | solution.py:110
  201.6 0.2 reduce-window_clone.1
  201.8 0.1 select_reduce_fusion
  201.9 0.8 multiply_cosine_fusion
  202.6 0.1 pad_maximum_fusion.1
  202.7 0.3 fusion.6
  203.0 143.2 %all-to-all-done = bf16[640,8,1280]{2,0,1:T(8,128)(2,1)} async-done(((bf16[640,8,1280]{2,0,1:T(8,128)(2,1)}), bf16[640,8,1280]{2,0,1:T(8,128)(2,1)}, u32[]{:S(2)}, u32[]{:S(2)}) %all-to-all-start) | async-done | bytes 13107232 | tf_op jit(solution)/shard_map/all_to_all | solution.py:110
  346.2 21.6 %copy.31 = bf16[640,8,1280]{2,1,0:T(8,128)(2,1)S(1)} copy(bf16[640,8,1280]{2,0,1:T(8,128)(2,1)} %all-to-all-done) | data formatting | bytes 26214400 | tf_op jit(solution)/shard_map/all_to_all | solution.py:110
  367.8 7.3 %copy.32 = bf16[32,8,20,1280]{3,2,1,0:T(8,128)(2,1)} copy(bf16[32,8,20,1280]{3,1,2,0:T(8,128)(2,1)S(1)} %bitcast.86) | data formatting | bytes 26214400 | tf_op jit(solution)/shard_map/transpose | solution.py:112
  375.1 19.7 %reshape.155 = bf16[5120,1280]{1,0:T(8,128)(2,1)} reshape(bf16[32,8,20,1280]{3,2,1,0:T(8,128)(2,1)} %copy.32) | data formatting | bytes 26214400 | tf_op jit(solution)/shard_map/reshape | solution.py:112
  394.8 14.9 %convolution_bitcast_fusion = f32[768,1280]{0,1:T(8,128)S(1)} fusion(bf16[5120,1280]{1,0:T(8,128)(2,1)} %reshape.155, bf16[768,5120]{1,0:T(8,128)(2,1)} %param.5), kind=kOutput, calls=%fused_computation.9 | convolution fusion | flops 10066329600 | bytes 24903680 | tf_op jit(solution)/shard_map/dot_general | solution.py:113
  409.7 0.2 multiply_reduce_fusion
  410.0 0.5 multiply_multiply_fusion
  410.5 0.0 copy-start.2
  410.5 0.2 slice_negate_fusion
  410.8 0.4 copy-done.2
  411.2 0.1 fusion.12
  411.3 0.2 maximum_multiply_fusion
  411.6 0.7 fusion.4
  412.3 8.4 %fusion.1 = (f32[8,768]{1,0:T(8,128)S(1)}, f32[768,768,8]{1,0,2:T(8,128)}) fusion(pred[768,768]{0,1:T(8,128)(4,1)S(1)} %fusion.6, bf16[768,8,128]{0,2,1:T(8,128)(2,1)S(1)} %bitcast.89, f32[768,64]{0,1:T(8,128)S(1)} %get-tuple-element.10, f32[768,64]{0,1:T(8,128)S(1)} %get-tuple-element.9, f32[128]{0:T(128)S(1)} %copy-done.2, ...), kind=kOutput, calls=%fused_computation.4 | convolution fusion | flops 1222993920 | bytes 22245888 | tf_op jit(solution)/shard_map/qhgd,khd->hgqk/dot_general | solution.py:79
  420.7 10.2 %fusion = f32[8,768]{1,0:T(8,128)S(1)} fusion(f32[768,768,8]{1,0,2:T(8,128)} %get-tuple-element.14, f32[8,768]{1,0:T(8,128)S(1)} %get-tuple-element.13, pred[768,768]{0,1:T(8,128)(4,1)S(1)} %fusion.6), kind=kLoop, calls=%fused_computation.3 | loop fusion | flops 18868224 | bytes 19513344 | tf_op jit(solution)/shard_map/reduce_sum | solution.py:96
  430.9 9.3 %fusion.7 = bf16[128,8,768]{2,0,1:T(8,128)(2,1)S(1)} fusion(f32[8,768]{1,0:T(8,128)S(1)} %fusion, f32[8,768]{1,0:T(8,128)S(1)} %get-tuple-element.13, f32[768,768,8]{1,0,2:T(8,128)} %get-tuple-element.14, pred[768,768]{0,1:T(8,128)(4,1)S(1)} %fusion.6, f32[768,1280]{0,1:T(8,128)} %copy-done), kind=kOutput, calls=%fused_computation.21 | convolution fusion | flops 1232338944 | bytes 21282816 | tf_op jit(solution)/shard_map/hgqk,khd->qhgd/dot_general | solution.py:122
  440.3 1.6 copy.36
  (14 shorter events, 0.1 us)
Async XLA Ops:
  6.5 140.5 %all-gather.3.cloned.1.call-start = ((), (), s32[]{:S(2)}) async-start(), calls=%async_computation.1 | async-start | bytes 16220160 | tf_op jit(solution)/shard_map/all_gather | solution.py:108
  195.9 5.7 %copy-start.3 = (s32[1,8]{1,0:T(1,128)S(1)}, s32[1,8]{1,0:T(1,128)}, u32[]{:S(2)}) copy-start(s32[1,8]{1,0:T(1,128)} %param.6) | copy-start | bytes 100
  195.9 6.8 %copy-start.1 = (f32[128]{0:T(128)S(1)}, f32[128]{0:T(128)}, u32[]{:S(2)}) copy-start(f32[128]{0:T(128)} %param.8) | copy-start | bytes 1540
  195.9 150.4 %all-to-all-start = ((bf16[640,8,1280]{2,0,1:T(8,128)(2,1)}), bf16[640,8,1280]{2,0,1:T(8,128)(2,1)}, u32[]{:S(2)}, u32[]{:S(2)}) async-start(bf16[640,8,1280]{2,0,1:T(8,128)(2,1)} %pad_maximum_fusion), calls=%async_computation | async-start | bytes 26214400 | tf_op jit(solution)/shard_map/all_to_all | solution.py:110
  409.7 2.6 copy-start
  410.5 0.7 copy-start.2
Sparse Core Ops, SparseCore 0:
  10.1 136.8 all-gather.2
where the time goes:
time: 450 us; the launch traced here: 449 us
  waiting for transfers between devices  284 us (63%)
  local copies, waits for them, and re-layouts  89.3 us (20%)
  matrix products  32.7 us (7%)
  other arithmetic  23.8 us (5%)
  between operations  13.6 us (3%)
  starting transfers between devices  5.69 us (1%)
    all_to_all x1, waiting for transfers between devices, shards(): lax.all_to_all(grouped, 'tensor', split_axis=1, concat_axis=0, tiled=True)  143 us
    all_gather x1, waiting for transfers between devices, shards(): stacked = lax.all_gather(qkv_weight, 'dp', axis=0, tiled=True)  140 us
    all_to_all x1, local copies, waits for them, and re-layouts, shards(): lax.all_to_all(grouped, 'tensor', split_axis=1, concat_axis=0, tiled=True)  21.6 us
    reshape x1, local copies, waits for them, and re-layouts, shards(): ordered = ordered.transpose(1, 0, 2, 3).reshape(-1, joined_width)  19.7 us
    unnamed x10, local copies, waits for them, and re-layouts  19.7 us
    dot_general x1, matrix products, shards(): jnp.dot(tokens, ordered, preferred_element_type=jnp.float32)  14.9 us
    reduce_sum x1, other arithmetic, softmax_weights(): jnp.sum(exponent, axis=3, keepdims=True)  10.2 us
    concatenate x1, other arithmetic, join_columns(): return jnp.concatenate([query_part, key_part, value_part], axis=2)  10.1 us
  transfers between devices with their start and end apart: 2, of which 2 were waited for; matrix products, arithmetic and copies ran while one was open for 0% of the time, Pallas kernels for 0%

commit v1 on v0

v1 whole, which is shorter than its diff:
```python
import math

import jax
import jax.numpy as jnp
from jax import lax
from jax.experimental import pallas as pl
from jax.experimental.pallas import tpu as pltpu
from jax.sharding import Mesh, PartitionSpec as P

ROPE_BASE = 1000000.0
NORM_EPS = 1e-06

HEAD = 128
HEADS = 8
ROWS = 768
NZ = 8
GROUP = 320
DEPTH = 2 * GROUP
COLS = 640
TILE = 256
TILES = ROWS // TILE
LONGEST = 384
QBLOCK = 128
TENSOR = ("y", "xl")
UP = [(z, (z + 1) % NZ) for z in range(NZ)]
DOWN = [(z, (z - 1) % NZ) for z in range(NZ)]
SWAP = [(0, 1), (1, 0)]

ANYWHERE = pl.BlockSpec(memory_space=pl.ANY)
VMEM = pl.BlockSpec(memory_space=pltpu.VMEM)
SMEM = pl.BlockSpec(memory_space=pltpu.SMEM)


def request_starts(length_row):
    ending = jnp.cumsum(length_row)
    offsets = ending - length_row
    row_ids = jnp.arange(ROWS, dtype=jnp.int32)
    reached = offsets[None, :] <= row_ids[:, None]
    return jnp.max(jnp.where(reached, offsets[None, :], 0), axis=1)


def rotary_tables(request_start):
    positions = (jnp.arange(ROWS, dtype=jnp.int32) - request_start).astype(jnp.float32)
    half = HEAD // 2
    frequency = ROPE_BASE ** (-jnp.arange(half, dtype=jnp.float32) * 2.0 / HEAD)
    angles = positions[:, None] * frequency[None, :]
    cosine, sine = jnp.cos(angles), jnp.sin(angles)
    return jnp.concatenate([cosine, cosine], axis=1), jnp.concatenate([-sine, sine], axis=1)


def regroup(weight):
    rows = weight.shape[0]
    query = weight[:, :8192].reshape(rows, 8, 2, 512)
    key = weight[:, 8192:9216].reshape(rows, 8, 1, HEAD)
    value = weight[:, 9216:].reshape(rows, 8, 1, HEAD)
    joined = jnp.concatenate([jnp.concatenate([key, value], axis=2), query], axis=3)
    return joined.transpose(2, 1, 0, 3)


def gather_blocks(block, ahead):
    half = GROUP // 2

    def up(array):
        return lax.ppermute(array, "z", UP)

    def down(array):
        return lax.ppermute(array, "z", DOWN)

    def across(array):
        return lax.ppermute(array, "xh", SWAP)

    up1, down1 = up(block), down(block)
    other = across(block)
    up1, down1, ahead = lax.optimization_barrier((up1, down1, ahead))
    up2, down2 = up(up1), down(down1)
    other_up1, other_down1 = across(up1), across(down1)
    up3, down3 = up(up2), down(down2)
    other_up2, other_down2 = up(other_up1), down(other_down1)
    up4, down4 = up(up3[:half]), down(down3[half:])
    other_up4, other_down4 = across(up4), across(down4)
    other_up3, other_down3 = up(other_up2), down(other_down2)
    early = [
        (block, 0, 0, 0), (other, 0, 1, 0),
        (up1, -1, 0, 0), (other_up1, -1, 1, 0), (down1, 1, 0, 0), (other_down1, 1, 1, 0),
        (up2, -2, 0, 0), (other_up2, -2, 1, 0), (down2, 2, 0, 0), (other_down2, 2, 1, 0),
    ]
    late = [
        (up3, -3, 0, 0), (other_up3, -3, 1, 0), (down3, 3, 0, 0), (other_down3, 3, 1, 0),
        (up4, 4, 0, 0), (down4, 4, 0, half), (other_up4, 4, 1, 0), (other_down4, 4, 1, half),
    ]
    return early, late, ahead


def slots_of(pieces):
    offsets = []
    for _, offset, _, _ in pieces:
        if offset not in offsets:
            offsets.append(offset)
    return offsets


def weight_copies(place_ref, pieces, sources, target, sems):
    offsets = slots_of(pieces)
    copies = [[] for _ in offsets]
    for number, (array, offset, flip, first) in enumerate(pieces):
        slot = offsets.index(offset)
        side = lax.rem(place_ref[1] + flip, 2)
        row = pl.multiple_of(side * GROUP + (slot * DEPTH + first), 16)
        where = target.at[pl.ds(row, array.shape[0])]
        copies[slot].append(pltpu.make_async_copy(sources[number], where, sems.at[number]))
    return copies


def slot_of(offset):
    return (offset + NZ) % NZ


def hold_tokens(place, tokens):
    def kernel(place_ref, token_ref, out_ref, sems):
        copies = [
            pltpu.make_async_copy(
                token_ref.at[
                    :, pl.ds(pl.multiple_of(lax.rem(place_ref[0] + slot, NZ) * DEPTH, HEAD), DEPTH)
                ],
                out_ref.at[slot],
                sems.at[slot],
            )
            for slot in range(NZ)
        ]
        for copy in copies:
            copy.start()
        for copy in copies:
            copy.wait()

    return pl.pallas_call(
        kernel,
        out_shape=pltpu.VMEM((NZ, ROWS, DEPTH), jnp.bfloat16),
        in_specs=[SMEM, ANYWHERE],
        out_specs=ANYWHERE,
        scratch_shapes=[pltpu.SemaphoreType.DMA((NZ,))],
        compiler_params=pltpu.CompilerParams(vmem_limit_bytes=4 << 20),
        cost_estimate=pl.CostEstimate(flops=0, bytes_accessed=16 << 20, transcendentals=0),
        name="hold_tokens",
    )(place, pltpu.with_memory_space_constraint(tokens, pltpu.HBM))


def project_early(place, pieces, held_sets):
    offsets = slots_of(pieces)
    count = len(offsets)

    def kernel(place_ref, *refs):
        sources, held_refs = refs[: len(pieces)], refs[len(pieces) : len(pieces) + 2]
        out_refs, (weight, sem_w) = refs[len(pieces) + 2 : len(pieces) + 4], refs[len(pieces) + 4 :]
        weights = weight_copies(place_ref, pieces, sources, weight, sem_w)
        for group in weights:
            for copy in group:
                copy.start()
        for slot, offset in enumerate(offsets):
            for copy in weights[slot]:
                copy.wait()
            for held_ref, out_ref in zip(held_refs, out_refs):
                product = jnp.dot(
                    held_ref[slot_of(offset)],
                    weight[slot * DEPTH : (slot + 1) * DEPTH],
                    preferred_element_type=jnp.float32,
                )
                if slot == 0:
                    out_ref[...] = product
                else:
                    out_ref[...] += product

    shape = pltpu.VMEM((ROWS, COLS), jnp.float32)
    return pl.pallas_call(
        kernel,
        out_shape=(shape, shape),
        in_specs=[SMEM] + [ANYWHERE] * len(pieces) + [VMEM] * 2,
        out_specs=(VMEM, VMEM),
        scratch_shapes=[
            pltpu.VMEM((count * DEPTH, COLS), jnp.bfloat16),
            pltpu.SemaphoreType.DMA((len(pieces),)),
        ],
        compiler_params=pltpu.CompilerParams(vmem_limit_bytes=16 << 20),
        cost_estimate=pl.CostEstimate(
            flops=4 * ROWS * count * DEPTH * COLS, bytes_accessed=18 << 20, transcendentals=0
        ),
        name="project_early",
    )(place, *[piece[0] for piece in pieces], *held_sets)


def project_late(place, pieces, held, partial, cosine, sine, query_gain, key_gain, ready=None):
    offsets = slots_of(pieces)
    count = len(offsets)
    n_in = len(pieces) if ready is None else 1

    def kernel(place_ref, *refs):
        sources = refs[:n_in]
        held_ref, partial_ref, cos_ref, sin_ref, qgain_ref, kgain_ref, out_ref = refs[n_in : n_in + 7]
        core = place_ref[2]
        weights = [[] for _ in offsets]
        if ready is None:
            weight, sem_w = refs[n_in + 7 :]
            weights = weight_copies(place_ref, pieces, sources, weight, sem_w)
        else:
            weight = sources[0]
        for group in weights:
            for copy in group:
                copy.start()

        def normed(field, gain, rows):
            factor = lax.rsqrt(jnp.mean(field * field, axis=1, keepdims=True) + NORM_EPS)
            field = field * factor * gain
            return field * cos_ref[rows] + pltpu.roll(field, HEAD // 2, 1) * sin_ref[rows]

        for tile in range(TILES):
            rows = pl.ds(tile * TILE, TILE)
            result = partial_ref[rows]
            for slot, offset in enumerate(offsets):
                if tile == 0:
                    for copy in weights[slot]:
                        copy.wait()
                result = result + jnp.dot(
                    held_ref[slot_of(offset), rows],
                    weight[slot * DEPTH : (slot + 1) * DEPTH],
                    preferred_element_type=jnp.float32,
                )
            raw = result[:, :HEAD]
            key = normed(raw, kgain_ref[...], rows)
            out_ref[rows, :HEAD] = jnp.where(core == 0, key, raw).astype(jnp.bfloat16)
            for first in range(HEAD, COLS, HEAD):
                field = normed(result[:, first : first + HEAD], qgain_ref[...], rows)
                out_ref[rows, first : first + HEAD] = field.astype(jnp.bfloat16)

    shape = jax.ShapeDtypeStruct((ROWS, COLS), jnp.bfloat16)
    weight_shape = pltpu.VMEM((count * DEPTH, COLS), jnp.bfloat16)
    first = ready is None
    return pl.pallas_call(
        kernel,
        out_shape=(shape, weight_shape) if first else shape,
        in_specs=[SMEM] + ([ANYWHERE] * n_in if first else [VMEM]) + [VMEM] * 6,
        out_specs=(VMEM, VMEM) if first else VMEM,
        scratch_shapes=[pltpu.SemaphoreType.DMA((len(pieces),))] if first else [],
        compiler_params=pltpu.CompilerParams(vmem_limit_bytes=16 << 20),
        cost_estimate=pl.CostEstimate(
            flops=2 * ROWS * count * DEPTH * COLS, bytes_accessed=9 << 20, transcendentals=0
        ),
        name="project_late",
    )(
        place, *([piece[0] for piece in pieces] if first else [ready]), held, partial, cosine, sine,
        query_gain, key_gain,
    )


def attend(place, own, received, request_start):
    scale = math.log2(math.e) / math.sqrt(HEAD)

    def kernel(place_ref, own_ref, received_ref, start_ref, out_ref, key_ref, value_ref):
        core = place_ref[2]
        key_ref[...] = jnp.where(core == 0, own_ref[:, :HEAD], received_ref[:, :HEAD])
        value_ref[:, :HEAD] = jnp.where(core == 0, received_ref[:, :HEAD], own_ref[:, :HEAD])
        value_ref[:, HEAD:] = jnp.ones((ROWS, HEAD), jnp.bfloat16)
        for block in range(ROWS // QBLOCK):
            rows = pl.ds(block * QBLOCK, QBLOCK)
            low = max(0, block * QBLOCK - LONGEST + 1) // QBLOCK * QBLOCK
            count = (block + 1) * QBLOCK - low
            keys, values = key_ref[pl.ds(low, count)], value_ref[pl.ds(low, count)]
            row_ids = block * QBLOCK + lax.broadcasted_iota(jnp.int32, (QBLOCK, count), 0)
            key_ids = low + lax.broadcasted_iota(jnp.int32, (QBLOCK, count), 1)
            allowed = (key_ids <= row_ids) & (key_ids >= start_ref[rows])
            bias = jnp.where(allowed, 0.0, -1e30)
            for side, source in enumerate((own_ref, received_ref)):
                first = pl.multiple_of((core if side == 0 else 1 - core) * 512, 512)
                queries = jnp.concatenate(
                    [source[rows, head * HEAD : (head + 1) * HEAD] for head in range(1, 5)], axis=0
                )
                scores = lax.dot_general(
                    queries, keys, (((1,), (1,)), ((), ())), preferred_element_type=jnp.float32
                )
                scores = scores.reshape(4, QBLOCK, count) * scale + bias[None]
                scores = scores.reshape(4 * QBLOCK, count)
                top = jnp.max(scores, axis=1, keepdims=True)
                weights = jnp.exp2(scores - top).astype(jnp.bfloat16)
                mixed = jnp.dot(weights, values, preferred_element_type=jnp.float32)
                mixed = (mixed[:, :HEAD] / mixed[:, HEAD:]).astype(jnp.bfloat16)
                for head in range(4):
                    out_ref[rows, pl.ds(first + head * HEAD, HEAD)] = mixed[
                        head * QBLOCK : (head + 1) * QBLOCK
                    ]

    return pl.pallas_call(
        kernel,
        out_shape=jax.ShapeDtypeStruct((ROWS, 8 * HEAD), jnp.bfloat16),
        in_specs=[SMEM, VMEM, VMEM, VMEM],
        out_specs=VMEM,
        scratch_shapes=[
            pltpu.VMEM((ROWS, HEAD), jnp.bfloat16),
            pltpu.VMEM((ROWS, 2 * HEAD), jnp.bfloat16),
        ],
        compiler_params=pltpu.CompilerParams(vmem_limit_bytes=32 << 20),
        cost_estimate=pl.CostEstimate(
            flops=4 * 8 * ROWS * 512 * HEAD, bytes_accessed=4 << 20, transcendentals=8 * ROWS * 512
        ),
        name="attend",
    )(place, own, received, request_start)


def shards(tokens, lengths, qkv_weight, query_norm_gain, key_norm_gain):
    place = jnp.stack([lax.axis_index("z"), lax.axis_index("xh"), lax.axis_index("c")]).astype(
        jnp.int32
    )
    other_tokens = lax.ppermute(tokens, "c", SWAP)
    other_lengths = lax.ppermute(lengths, "c", SWAP)
    spread = regroup(qkv_weight).reshape(16, -1, COLS)
    block = lax.all_to_all(spread, ("c",) + TENSOR, split_axis=0, concat_axis=0, tiled=True)
    own_start, other_start = request_starts(lengths[0]), request_starts(other_lengths[0])
    own_tables, other_tables = rotary_tables(own_start), rotary_tables(other_start)
    held = hold_tokens(place, tokens)
    other_held = hold_tokens(place, other_tokens)
    early, late, *ahead = gather_blocks(
        block.reshape(GROUP, COLS), (held, other_held, *own_tables, *other_tables)
    )
    held, other_held, *tables = ahead[0]
    own_tables, other_tables = tables[:2], tables[2:]
    gains = (query_norm_gain.reshape(1, HEAD), key_norm_gain.reshape(1, HEAD))
    own_partial, other_partial = project_early(place, early, (held, other_held))
    other, ready = project_late(place, late, other_held, other_partial, *other_tables, *gains)
    received = lax.ppermute(other, "c", SWAP)
    own = project_late(place, late, held, own_partial, *own_tables, *gains, ready)
    return attend(place, own, received, own_start.reshape(ROWS, 1))


def solution(mesh):
    fine = Mesh(mesh.devices.reshape(NZ, 2, 2, 4, 2), ("z", "xh", "c") + TENSOR)
    rows = ("z", "xh", "c")
    in_specs = (P(rows, None), P(rows, None), P(rows + TENSOR, None), P(), P())
    return jax.shard_map(
        shards, mesh=fine, in_specs=in_specs, out_specs=P(rows, TENSOR), check_vma=False
    )
```

time: 450 us -> 110 us (0.24)
  waiting for transfers between devices: 284 us -> 18.8 us
  local copies, waits for them, and re-layouts: 89.3 us -> 6.44 us
  Pallas kernels: 0 us -> 37 us
  starting transfers between devices: 5.69 us -> 42.4 us
  matrix products: 32.7 us -> 0 us
  other arithmetic: 23.8 us -> 5.03 us
  between operations: 13.6 us -> 0.29 us
    all_to_all x1, waiting for transfers between devices: 143 us -> 0.6 us  [shards(): lax.all_to_all(spread, ('c',) + TENSOR, split_axis=0, concat_axis=0, tile...]
    all_gather x1 -> x0, waiting for transfers between devices: 140 us -> none  [shards(): stacked = lax.all_gather(qkv_weight, 'dp', axis=0, tiled=True)]
    ppermute x0 -> x20, starting transfers between devices: none -> 38.2 us  [the longest x6 14.9 us: down(): return lax.ppermute(array, 'z', DOWN)]
    pallas_call x0 -> x6, Pallas kernels: none -> 37 us  [the longest x1 12.4 us: project_early(): pl.pallas_call(kernel, out_shape=(shape, shape), in_specs=[SMEM] + [ANYWH...]
    dot_general x3 -> x0, matrix products: 32.7 us -> none  [the longest x1 14.9 us: shards(): jnp.dot(tokens, ordered, preferred_element_type=jnp.float32)]
    reshape x3, local copies, waits for them, and re-layouts: 29.9 us -> 0.31 us  [the longest x1 0.21 us: regroup(): query = weight[:, :8192].reshape(rows, 8, 2, 512)]
    all_to_all x1 -> x0, local copies, waits for them, and re-layouts: 21.6 us -> none  [shards(): lax.all_to_all(grouped, 'tensor', split_axis=1, concat_axis=0, tiled=True)]
    ppermute x0 -> x20, waiting for transfers between devices: none -> 18.2 us  [the longest x6 9.58 us: up(): return lax.ppermute(array, 'z', UP)]
  transfers between devices with their start and end apart: 2 -> 21, of which waited for: 2 -> 6; matrix products, arithmetic and copies ran while one was open for 0% -> 8% of each run, Pallas kernels for 0% -> 23%
where the time goes in v1:
time: 110 us
  starting transfers between devices  42.4 us (39%)
  Pallas kernels  37 us (34%)
  waiting for transfers between devices  18.8 us (17%)
  local copies, waits for them, and re-layouts  6.44 us (6%)
  other arithmetic  5.03 us (5%)
    ppermute x6, starting transfers between devices, down(): return lax.ppermute(array, 'z', DOWN)  14.9 us
    pallas_call x1, Pallas kernels, project_early(): pl.pallas_call(kernel, out_shape=(shape, shape), in_specs=[SMEM] + [ANYWH...  12.4 us
    pallas_call x2, Pallas kernels, project_late(): pl.pallas_call(kernel, out_shape=(shape, weight_shape) if first else shap...  11 us
    ppermute x6, waiting for transfers between devices, up(): return lax.ppermute(array, 'z', UP)  9.58 us
    ppermute x1, starting transfers between devices, shards(): received = lax.ppermute(other, 'c', SWAP)  8.53 us
    ppermute x5, starting transfers between devices, across(): return lax.ppermute(array, 'xh', SWAP)  8.39 us
    pallas_call x2, Pallas kernels, hold_tokens(): pl.pallas_call(kernel, out_shape=pltpu.VMEM((NZ, ROWS, DEPTH), jnp.bfloat...  8.24 us
    ppermute x5, waiting for transfers between devices, across(): return lax.ppermute(array, 'xh', SWAP)  7.87 us
  transfers between devices with their start and end apart: 21, of which 6 were waited for; matrix products, arithmetic and copies ran while one was open for 8% of the time, Pallas kernels for 23%

profile of v1, /device:TPU:1, one launch (start us, length us, event | category | flops | bytes accessed | tf_op | source)
XLA Modules:
  0.0 109.9 jit_solution(1835579918623528544)
XLA Ops:
  0.0 3.2 %collective-permute-start.2 = (bf16[768,5120]{1,0:T(8,128)(2,1)}, bf16[768,5120]{1,0:T(8,128)(2,1)}, u32[]{:S(2)}, u32[]{:S(2)}) collective-permute-start(bf16[768,5120]{1,0:T(8,128)(2,1)} %token_ref.1), channel_id=1, source_target_pairs={{0,8},{8,0},{1,9},{9,1},{2,10},{10,2},{3,11},{11,3},{4,12},{12,4},... | collective-permute-start | bytes 23592968 | tf_op jit(solution)/shard_map/ppermute | solution.py:310
  3.2 1.0 slice.17
  4.3 0.8 fusion.2
  5.8 0.9 copy.12
  6.7 4.2 %all-to-all-start = ((bf16[16,20,640]{2,1,0:T(8,128)(2,1)}), bf16[16,20,640]{2,1,0:T(8,128)(2,1)S(1)}, u32[]{:S(2)}, u32[]{:S(2)}) async-start(bf16[16,20,640]{2,1,0:T(8,128)(2,1)} %bitcast.4), calls=%async_computation | async-start | bytes 983040 | tf_op jit(solution)/shard_map/all_to_all | solution.py:313
  10.9 0.8 reduce-window_clone.1
  11.8 3.9 %hold_tokens.2.refs_10_.refs_1_ = bf16[8,768,640]{2,1,0:T(8,128)(2,1)S(1)} custom-call(s32[3]{0:T(128)S(1)} %pad_add_fusion.place_ref, bf16[768,5120]{1,0:T(8,128)(2,1)} %token_ref.1), custom_call_target="tpu_custom_call" | custom-call | bytes 16777216 | tf_op jit(solution)/shard_map/hold_tokens/pallas_call | solution.py:135
  15.7 3.1 %copy-done = bf16[8,768,640]{2,1,0:T(8,128)(2,1)} copy-done((bf16[8,768,640]{2,1,0:T(8,128)(2,1)}, bf16[8,768,640]{2,1,0:T(8,128)(2,1)S(1)}, u32[]{:S(2)}) %copy-start) | copy-done | bytes 7864344
  19.3 0.6 all-to-all-done
  19.9 1.7 %collective-permute-start = (bf16[320,640]{1,0:T(8,128)(2,1)S(1)}, bf16[320,640]{1,0:T(8,128)(2,1)S(1)}, u32[]{:S(2)}, u32[]{:S(2)}) collective-permute-start(bf16[320,640]{1,0:T(8,128)(2,1)S(1)} %reshape.58.refs_0_), channel_id=1, source_target_pairs={{0,32},{32,64},{64,96},{96,128},{128,160},{160,192},{192,224},{224... | collective-permute-start | bytes 1228808 | tf_op jit(solution)/shard_map/ppermute | solution.py:64
  21.7 4.0 %collective-permute-start.1 = (bf16[320,640]{1,0:T(8,128)(2,1)S(1)}, bf16[320,640]{1,0:T(8,128)(2,1)S(1)}, u32[]{:S(2)}, u32[]{:S(2)}) collective-permute-start(bf16[320,640]{1,0:T(8,128)(2,1)S(1)} %reshape.58.refs_0_), channel_id=1, source_target_pairs={{0,224},{32,0},{64,32},{96,64},{128,96},{160,128},{192,160},{224,1... | collective-permute-start | bytes 1228808 | tf_op jit(solution)/shard_map/ppermute | solution.py:67
  25.7 2.8 %fusion.1 = (f32[768,64]{1,0:T(8,128)S(1)}, f32[768,64]{1,0:T(8,128)S(1)}, f32[768,64]{1,0:T(8,128)S(1)}, f32[768,64]{1,0:T(8,128)S(1)}, f32[768,64]{1,0:T(8,128)S(1)}, /*index=5*/f32[768,64]{1,0:T(8,128)S(1)}) fusion(f32[64]{0:T(128)S(1)} %multiply_power_fusion, f32[768]{0:T(1024)S(1)} %subtract_convert_fusion, f32[768]{0:T(1024)S(1)} %subtract_convert_fusion.1), kind=kLoop, calls=%fused_computation.10 | loop fusion | flops 196608 | bytes 1186048 | tf_op jit(solution)/shard_map/neg | solution.py:48
  29.1 4.3 %hold_tokens.3.refs_11_.refs_8_ = bf16[8,768,640]{2,1,0:T(8,128)(2,1)S(1)} custom-call(s32[3]{0:T(128)S(1)} %pad_add_fusion.place_ref, bf16[768,5120]{1,0:T(8,128)(2,1)} %collective-permute-done.2.token_ref), custom_call_target="tpu_custom_call" | custom-call | bytes 16777216 | tf_op jit(solution)/shard_map/hold_tokens/pallas_call | solution.py:135
  33.4 0.9 collective-permute-done.refs_2_
  34.3 2.7 %collective-permute-start.9 = (bf16[320,640]{1,0:T(8,128)(2,1)S(1)}, bf16[320,640]{1,0:T(8,128)(2,1)S(1)}, u32[]{:S(2)}, u32[]{:S(2)}) collective-permute-start(bf16[320,640]{1,0:T(8,128)(2,1)S(1)} %collective-permute-done.1.refs_4_), channel_id=1, source_target_pairs={{0,224},{32,0},{64,32},{96,64},{128,96},{160,128},{192,160},{224,1... | collective-permute-start | bytes 1228808 | tf_op jit(solution)/shard_map/ppermute | solution.py:67
  37.0 2.5 %collective-permute-start.11 = (bf16[320,640]{1,0:T(8,128)(2,1)S(1)}, bf16[320,640]{1,0:T(8,128)(2,1)S(1)}, u32[]{:S(2)}, u32[]{:S(2)}) collective-permute-start(bf16[320,640]{1,0:T(8,128)(2,1)S(1)} %collective-permute-done.1.refs_4_), channel_id=1, source_target_pairs={{0,16},{16,0},{1,17},{17,1},{2,18},{18,2},{3,19},{19,3},{4,20},{20... | collective-permute-start | bytes 1228808 | tf_op jit(solution)/shard_map/ppermute | solution.py:70
  40.0 4.8 %collective-permute-done.4.refs_6_ = bf16[320,640]{1,0:T(8,128)(2,1)S(1)} collective-permute-done((bf16[320,640]{1,0:T(8,128)(2,1)S(1)}, bf16[320,640]{1,0:T(8,128)(2,1)S(1)}, u32[]{:S(2)}, u32[]{:S(2)}) %collective-permute-start.4) | collective-permute-done | bytes 409632 | tf_op jit(solution)/shard_map/ppermute | solution.py:64
  44.8 2.7 %collective-permute-start.10 = (bf16[320,640]{1,0:T(8,128)(2,1)S(1)}, bf16[320,640]{1,0:T(8,128)(2,1)S(1)}, u32[]{:S(2)}, u32[]{:S(2)}) collective-permute-start(bf16[320,640]{1,0:T(8,128)(2,1)S(1)} %collective-permute-done.9.refs_8_), channel_id=1, source_target_pairs={{0,224},{32,0},{64,32},{96,64},{128,96},{160,128},{192,160},{224,1... | collective-permute-start | bytes 1228808 | tf_op jit(solution)/shard_map/ppermute | solution.py:67
  47.5 0.6 collective-permute-start.12
  48.2 7.9 %collective-permute-done.6.refs_3_ = bf16[320,640]{1,0:T(8,128)(2,1)S(1)} collective-permute-done((bf16[320,640]{1,0:T(8,128)(2,1)S(1)}, bf16[320,640]{1,0:T(8,128)(2,1)S(1)}, u32[]{:S(2)}, u32[]{:S(2)}) %collective-permute-start.6) | collective-permute-done | bytes 409632 | tf_op jit(solution)/shard_map/ppermute | solution.py:70
  56.0 2.5 %collective-permute-start.18 = (bf16[320,640]{1,0:T(8,128)(2,1)S(1)}, bf16[320,640]{1,0:T(8,128)(2,1)S(1)}, u32[]{:S(2)}, u32[]{:S(2)}) collective-permute-start(bf16[320,640]{1,0:T(8,128)(2,1)S(1)} %reshape.58.refs_0_), channel_id=1, source_target_pairs={{0,16},{16,0},{1,17},{17,1},{2,18},{18,2},{3,19},{19,3},{4,20},{20... | collective-permute-start | bytes 1228808 | tf_op jit(solution)/shard_map/ppermute | solution.py:70
  58.5 1.3 %collective-permute-start.14 = (bf16[160,640]{1,0:T(8,128)(2,1)S(1)}, bf16[160,640]{1,0:T(8,128)(2,1)S(1)}, u32[]{:S(2)}, u32[]{:S(2)}) collective-permute-start(bf16[160,640]{1,0:T(8,128)(2,1)S(1)} %slice.20), channel_id=1, source_target_pairs={{0,32},{32,64},{64,96},{96,128},{128,160},{160,192},{192,224},{224... | collective-permute-start | bytes 614408 | tf_op jit(solution)/shard_map/ppermute | solution.py:64
  59.9 1.5 %collective-permute-start.15 = (bf16[160,640]{1,0:T(8,128)(2,1)S(1)}, bf16[160,640]{1,0:T(8,128)(2,1)S(1)}, u32[]{:S(2)}, u32[]{:S(2)}) collective-permute-start(bf16[160,640]{1,0:T(8,128)(2,1)S(1)} %slice.21), channel_id=1, source_target_pairs={{0,224},{32,0},{64,32},{96,64},{128,96},{160,128},{192,160},{224,1... | collective-permute-start | bytes 614408 | tf_op jit(solution)/shard_map/ppermute | solution.py:67
  61.4 0.8 collective-permute-done.12.refs_9_
  62.2 3.4 %collective-permute-start.13 = (bf16[320,640]{1,0:T(8,128)(2,1)S(1)}, bf16[320,640]{1,0:T(8,128)(2,1)S(1)}, u32[]{:S(2)}, u32[]{:S(2)}) collective-permute-start(bf16[320,640]{1,0:T(8,128)(2,1)S(1)} %collective-permute-done.12.refs_9_), channel_id=1, source_target_pairs={{0,224},{32,0},{64,32},{96,64},{128,96},{160,128},{192,160},{224,1... | collective-permute-start | bytes 1228808 | tf_op jit(solution)/shard_map/ppermute | solution.py:67
  65.6 3.8 %collective-permute-done.14.refs_4_ = bf16[160,640]{1,0:T(8,128)(2,1)S(1)} collective-permute-done((bf16[160,640]{1,0:T(8,128)(2,1)S(1)}, bf16[160,640]{1,0:T(8,128)(2,1)S(1)}, u32[]{:S(2)}, u32[]{:S(2)}) %collective-permute-start.14) | collective-permute-done | bytes 204832 | tf_op jit(solution)/shard_map/ppermute | solution.py:64
  69.4 2.5 %collective-permute-start.16 = (bf16[160,640]{1,0:T(8,128)(2,1)S(1)}, bf16[160,640]{1,0:T(8,128)(2,1)S(1)}, u32[]{:S(2)}, u32[]{:S(2)}) collective-permute-start(bf16[160,640]{1,0:T(8,128)(2,1)S(1)} %collective-permute-done.14.refs_4_), channel_id=1, source_target_pairs={{0,16},{16,0},{1,17},{17,1},{2,18},{18,2},{3,19},{19,3},{4,20},{20... | collective-permute-start | bytes 614408 | tf_op jit(solution)/shard_map/ppermute | solution.py:70
  72.4 12.4 %project_early.1 = (f32[768,640]{1,0:T(8,128)S(1)}, f32[768,640]{1,0:T(8,128)S(1)}) custom-call(s32[3]{0:T(128)S(1)} %pad_add_fusion.place_ref, bf16[320,640]{1,0:T(8,128)(2,1)S(1)} %reshape.58.refs_0_, bf16[320,640]{1,0:T(8,128)(2,1)S(1)} %collective-permute-done.18.refs_1_, bf16[320,640]{1,0:T(8,128)(2,1)S(1)} %collective-permute-done.refs_2_, ...), custom_call_target="tpu_custom_call" | custom-call | flops 6291456000 | bytes 18874368 | tf_op jit(solution)/shard_map/project_early/pallas_call | solution.py:173
  84.8 6.5 %project_late.2 = (bf16[768,640]{1,0:T(8,128)(2,1)S(1)}, bf16[1920,640]{1,0:T(8,128)(2,1)S(1)}) custom-call(s32[3]{0:T(128)S(1)} %pad_add_fusion.place_ref, bf16[320,640]{1,0:T(8,128)(2,1)S(1)} %collective-permute-done.5.refs_0_, bf16[320,640]{1,0:T(8,128)(2,1)S(1)} %collective-permute-done.8.refs_1_, bf16[320,640]{1,0:T(8,128)(2,1)S(1)} %collective-permute-done.10.refs_2_, ...), custom_call_target="tpu_custom_call" | custom-call | flops 1887436800 | bytes 9437184 | tf_op jit(solution)/shard_map/project_late/pallas_call | solution.py:236
  91.4 8.5 %collective-permute-start.19 = (bf16[768,640]{1,0:T(8,128)(2,1)S(1)}, bf16[768,640]{1,0:T(8,128)(2,1)S(1)}, u32[]{:S(2)}, u32[]{:S(2)}) collective-permute-start(bf16[768,640]{1,0:T(8,128)(2,1)S(1)} %get-tuple-element.28), channel_id=1, source_target_pairs={{0,8},{8,0},{1,9},{9,1},{2,10},{10,2},{3,11},{11,3},{4,12},{12,4},... | collective-permute-start | bytes 2949128 | tf_op jit(solution)/shard_map/ppermute | solution.py:326
  100.1 4.5 %project_late.3.own_ref = bf16[768,640]{1,0:T(8,128)(2,1)S(1)} custom-call(s32[3]{0:T(128)S(1)} %pad_add_fusion.place_ref, bf16[1920,640]{1,0:T(8,128)(2,1)S(1)} %get-tuple-element.24.refs_0_, bf16[8,768,640]{2,1,0:T(8,128)(2,1)S(1)} %bitcast.25, f32[768,640]{1,0:T(8,128)S(1)} %get-tuple-element.25.refs_2_, f32[768,128]{1,0:T(8,128)S(1)} %get-tuple-element.26.refs_3_, ...), custom_call_target="tpu_custom_call" | custom-call | flops 1887436800 | bytes 9437184 | tf_op jit(solution)/shard_map/project_late/pallas_call | solution.py:236
  104.5 5.4 %attend.1 = bf16[768,1024]{1,0:T(8,128)(2,1)} custom-call(s32[3]{0:T(128)S(1)} %pad_add_fusion.place_ref, bf16[768,640]{1,0:T(8,128)(2,1)S(1)} %project_late.3.own_ref, bf16[768,640]{1,0:T(8,128)(2,1)S(1)} %collective-permute-done.19.received_ref, s32[768,1]{1,0:T(8,128)S(1)} %reduce_max.23.start_ref), custom_call_target="tpu_custom_call" | custom-call | flops 1610612736 | bytes 4194304 | tf_op jit(solution)/shard_map/attend/pallas_call | solution.py:289
  (56 shorter events, 3.1 us)
Async XLA Ops:
  0.0 29.1 %collective-permute-start.2 = (bf16[768,5120]{1,0:T(8,128)(2,1)}, bf16[768,5120]{1,0:T(8,128)(2,1)}, u32[]{:S(2)}, u32[]{:S(2)}) collective-permute-start(bf16[768,5120]{1,0:T(8,128)(2,1)} %token_ref.1), channel_id=1, source_target_pairs={{0,8},{8,0},{1,9},{9,1},{2,10},{10,2},{3,11},{11,3},{4,12},{12,4},... | collective-permute-start | bytes 23592968 | tf_op jit(solution)/shard_map/ppermute | solution.py:310
  3.2 15.7 %collective-permute-start.3 = (s32[1,8]{1,0:T(1,128)}, s32[1,8]{1,0:T(1,128)S(1)}, u32[]{:S(2)}, u32[]{:S(2)}) collective-permute-start(s32[1,8]{1,0:T(1,128)} %param.6), channel_id=1, source_target_pairs={{0,8},{8,0},{1,9},{9,1},{2,10},{10,2},{3,11},{11,3},{4,12},{12,4},... | collective-permute-start | bytes 104 | tf_op jit(solution)/shard_map/ppermute | solution.py:311
  6.7 13.2 %all-to-all-start = ((bf16[16,20,640]{2,1,0:T(8,128)(2,1)}), bf16[16,20,640]{2,1,0:T(8,128)(2,1)S(1)}, u32[]{:S(2)}, u32[]{:S(2)}) async-start(bf16[16,20,640]{2,1,0:T(8,128)(2,1)} %bitcast.4), calls=%async_computation | async-start | bytes 983040 | tf_op jit(solution)/shard_map/all_to_all | solution.py:313
  11.8 7.1 %copy-start.3 = (s32[1,8]{1,0:T(1,128)S(1)}, s32[1,8]{1,0:T(1,128)}, u32[]{:S(2)}) copy-start(s32[1,8]{1,0:T(1,128)} %param.6) | copy-start | bytes 100
  15.7 3.1 %copy-start = (bf16[8,768,640]{2,1,0:T(8,128)(2,1)}, bf16[8,768,640]{2,1,0:T(8,128)(2,1)S(1)}, u32[]{:S(2)}) copy-start(bf16[8,768,640]{2,1,0:T(8,128)(2,1)S(1)} %hold_tokens.2.refs_10_.refs_1_) | copy-start | bytes 23592964
  19.9 14.4 %collective-permute-start = (bf16[320,640]{1,0:T(8,128)(2,1)S(1)}, bf16[320,640]{1,0:T(8,128)(2,1)S(1)}, u32[]{:S(2)}, u32[]{:S(2)}) collective-permute-start(bf16[320,640]{1,0:T(8,128)(2,1)S(1)} %reshape.58.refs_0_), channel_id=1, source_target_pairs={{0,32},{32,64},{64,96},{96,128},{128,160},{160,192},{192,224},{224... | collective-permute-start | bytes 1228808 | tf_op jit(solution)/shard_map/ppermute | solution.py:64
  21.7 12.7 %collective-permute-start.1 = (bf16[320,640]{1,0:T(8,128)(2,1)S(1)}, bf16[320,640]{1,0:T(8,128)(2,1)S(1)}, u32[]{:S(2)}, u32[]{:S(2)}) collective-permute-start(bf16[320,640]{1,0:T(8,128)(2,1)S(1)} %reshape.58.refs_0_), channel_id=1, source_target_pairs={{0,224},{32,0},{64,32},{96,64},{128,96},{160,128},{192,160},{224,1... | collective-permute-start | bytes 1228808 | tf_op jit(solution)/shard_map/ppermute | solution.py:67
  28.8 43.6 %slice-start = ((s8[7864320]{0:T(1024)(128)(4,1)}), s8[4194304]{0:T(1024)(128)(4,1)S(1)}, s32[]{:S(2)}) async-start(s8[7864320]{0:T(1024)(128)(4,1)} %bitcast.24), calls=%async_computation.1 | async-start | bytes 8388608
  29.1 43.3 %slice-start.1 = ((s8[7864320]{0:T(1024)(128)(4,1)}), s8[3670016]{0:T(1024)(128)(4,1)S(1)}, s32[]{:S(2)}) async-start(s8[7864320]{0:T(1024)(128)(4,1)} %bitcast.24), calls=%async_computation.2 | async-start | bytes 7340032
  34.3 10.5 %collective-permute-start.4 = (bf16[320,640]{1,0:T(8,128)(2,1)S(1)}, bf16[320,640]{1,0:T(8,128)(2,1)S(1)}, u32[]{:S(2)}, u32[]{:S(2)}) collective-permute-start(bf16[320,640]{1,0:T(8,128)(2,1)S(1)} %collective-permute-done.refs_2_), channel_id=1, source_target_pairs={{0,32},{32,64},{64,96},{96,128},{128,160},{160,192},{192,224},{224... | collective-permute-start | bytes 1228808 | tf_op jit(solution)/shard_map/ppermute | solution.py:64
  34.3 10.5 %collective-permute-start.9 = (bf16[320,640]{1,0:T(8,128)(2,1)S(1)}, bf16[320,640]{1,0:T(8,128)(2,1)S(1)}, u32[]{:S(2)}, u32[]{:S(2)}) collective-permute-start(bf16[320,640]{1,0:T(8,128)(2,1)S(1)} %collective-permute-done.1.refs_4_), channel_id=1, source_target_pairs={{0,224},{32,0},{64,32},{96,64},{128,96},{160,128},{192,160},{224,1... | collective-permute-start | bytes 1228808 | tf_op jit(solution)/shard_map/ppermute | solution.py:67
  37.0 10.5 %collective-permute-start.11 = (bf16[320,640]{1,0:T(8,128)(2,1)S(1)}, bf16[320,640]{1,0:T(8,128)(2,1)S(1)}, u32[]{:S(2)}, u32[]{:S(2)}) collective-permute-start(bf16[320,640]{1,0:T(8,128)(2,1)S(1)} %collective-permute-done.1.refs_4_), channel_id=1, source_target_pairs={{0,16},{16,0},{1,17},{17,1},{2,18},{18,2},{3,19},{19,3},{4,20},{20... | collective-permute-start | bytes 1228808 | tf_op jit(solution)/shard_map/ppermute | solution.py:70
  39.5 16.5 %collective-permute-start.6 = (bf16[320,640]{1,0:T(8,128)(2,1)S(1)}, bf16[320,640]{1,0:T(8,128)(2,1)S(1)}, u32[]{:S(2)}, u32[]{:S(2)}) collective-permute-start(bf16[320,640]{1,0:T(8,128)(2,1)S(1)} %collective-permute-done.refs_2_), channel_id=1, source_target_pairs={{0,16},{16,0},{1,17},{17,1},{2,18},{18,2},{3,19},{19,3},{4,20},{20... | collective-permute-start | bytes 1228808 | tf_op jit(solution)/shard_map/ppermute | solution.py:70
  44.8 13.6 %collective-permute-start.5 = (bf16[320,640]{1,0:T(8,128)(2,1)S(1)}, bf16[320,640]{1,0:T(8,128)(2,1)S(1)}, u32[]{:S(2)}, u32[]{:S(2)}) collective-permute-start(bf16[320,640]{1,0:T(8,128)(2,1)S(1)} %collective-permute-done.4.refs_6_), channel_id=1, source_target_pairs={{0,32},{32,64},{64,96},{96,128},{128,160},{160,192},{192,224},{224... | collective-permute-start | bytes 1228808 | tf_op jit(solution)/shard_map/ppermute | solution.py:64
  44.8 15.0 %collective-permute-start.10 = (bf16[320,640]{1,0:T(8,128)(2,1)S(1)}, bf16[320,640]{1,0:T(8,128)(2,1)S(1)}, u32[]{:S(2)}, u32[]{:S(2)}) collective-permute-start(bf16[320,640]{1,0:T(8,128)(2,1)S(1)} %collective-permute-done.9.refs_8_), channel_id=1, source_target_pairs={{0,224},{32,0},{64,32},{96,64},{128,96},{160,128},{192,160},{224,1... | collective-permute-start | bytes 1228808 | tf_op jit(solution)/shard_map/ppermute | solution.py:67
  47.5 14.6 %collective-permute-start.12 = (bf16[320,640]{1,0:T(8,128)(2,1)S(1)}, bf16[320,640]{1,0:T(8,128)(2,1)S(1)}, u32[]{:S(2)}, u32[]{:S(2)}) collective-permute-start(bf16[320,640]{1,0:T(8,128)(2,1)S(1)} %collective-permute-done.11.refs_5_), channel_id=1, source_target_pairs={{0,224},{32,0},{64,32},{96,64},{128,96},{160,128},{192,160},{224,1... | collective-permute-start | bytes 1228808 | tf_op jit(solution)/shard_map/ppermute | solution.py:67
  56.0 9.6 %collective-permute-start.7 = (bf16[320,640]{1,0:T(8,128)(2,1)S(1)}, bf16[320,640]{1,0:T(8,128)(2,1)S(1)}, u32[]{:S(2)}, u32[]{:S(2)}) collective-permute-start(bf16[320,640]{1,0:T(8,128)(2,1)S(1)} %collective-permute-done.6.refs_3_), channel_id=1, source_target_pairs={{0,32},{32,64},{64,96},{96,128},{128,160},{160,192},{192,224},{224... | collective-permute-start | bytes 1228808 | tf_op jit(solution)/shard_map/ppermute | solution.py:64
  56.0 16.4 %collective-permute-start.18 = (bf16[320,640]{1,0:T(8,128)(2,1)S(1)}, bf16[320,640]{1,0:T(8,128)(2,1)S(1)}, u32[]{:S(2)}, u32[]{:S(2)}) collective-permute-start(bf16[320,640]{1,0:T(8,128)(2,1)S(1)} %reshape.58.refs_0_), channel_id=1, source_target_pairs={{0,16},{16,0},{1,17},{17,1},{2,18},{18,2},{3,19},{19,3},{4,20},{20... | collective-permute-start | bytes 1228808 | tf_op jit(solution)/shard_map/ppermute | solution.py:70
  58.5 10.9 %collective-permute-start.14 = (bf16[160,640]{1,0:T(8,128)(2,1)S(1)}, bf16[160,640]{1,0:T(8,128)(2,1)S(1)}, u32[]{:S(2)}, u32[]{:S(2)}) collective-permute-start(bf16[160,640]{1,0:T(8,128)(2,1)S(1)} %slice.20), channel_id=1, source_target_pairs={{0,32},{32,64},{64,96},{96,128},{128,160},{160,192},{192,224},{224... | collective-permute-start | bytes 614408 | tf_op jit(solution)/shard_map/ppermute | solution.py:64
  59.9 25.0 %copy-start.1 = (f32[128]{0:T(128)S(1)}, f32[128]{0:T(128)}, u32[]{:S(2)}) copy-start(f32[128]{0:T(128)} %param.8) | copy-start | bytes 1540
  59.9 24.9 %copy-start.2 = (f32[128]{0:T(128)S(1)}, f32[128]{0:T(128)}, u32[]{:S(2)}) copy-start(f32[128]{0:T(128)} %param.9) | copy-start | bytes 1540
  59.9 12.0 %collective-permute-start.15 = (bf16[160,640]{1,0:T(8,128)(2,1)S(1)}, bf16[160,640]{1,0:T(8,128)(2,1)S(1)}, u32[]{:S(2)}, u32[]{:S(2)}) collective-permute-start(bf16[160,640]{1,0:T(8,128)(2,1)S(1)} %slice.21), channel_id=1, source_target_pairs={{0,224},{32,0},{64,32},{96,64},{128,96},{160,128},{192,160},{224,1... | collective-permute-start | bytes 614408 | tf_op jit(solution)/shard_map/ppermute | solution.py:67
  62.2 22.6 %collective-permute-start.13 = (bf16[320,640]{1,0:T(8,128)(2,1)S(1)}, bf16[320,640]{1,0:T(8,128)(2,1)S(1)}, u32[]{:S(2)}, u32[]{:S(2)}) collective-permute-start(bf16[320,640]{1,0:T(8,128)(2,1)S(1)} %collective-permute-done.12.refs_9_), channel_id=1, source_target_pairs={{0,224},{32,0},{64,32},{96,64},{128,96},{160,128},{192,160},{224,1... | collective-permute-start | bytes 1228808 | tf_op jit(solution)/shard_map/ppermute | solution.py:67
  65.6 19.2 %collective-permute-start.8 = (bf16[320,640]{1,0:T(8,128)(2,1)S(1)}, bf16[320,640]{1,0:T(8,128)(2,1)S(1)}, u32[]{:S(2)}, u32[]{:S(2)}) collective-permute-start(bf16[320,640]{1,0:T(8,128)(2,1)S(1)} %collective-permute-done.7.refs_7_), channel_id=1, source_target_pairs={{0,32},{32,64},{64,96},{96,128},{128,160},{160,192},{192,224},{224... | collective-permute-start | bytes 1228808 | tf_op jit(solution)/shard_map/ppermute | solution.py:64
  69.4 15.4 %collective-permute-start.16 = (bf16[160,640]{1,0:T(8,128)(2,1)S(1)}, bf16[160,640]{1,0:T(8,128)(2,1)S(1)}, u32[]{:S(2)}, u32[]{:S(2)}) collective-permute-start(bf16[160,640]{1,0:T(8,128)(2,1)S(1)} %collective-permute-done.14.refs_4_), channel_id=1, source_target_pairs={{0,16},{16,0},{1,17},{17,1},{2,18},{18,2},{3,19},{19,3},{4,20},{20... | collective-permute-start | bytes 614408 | tf_op jit(solution)/shard_map/ppermute | solution.py:70
  71.9 12.9 %collective-permute-start.17 = (bf16[160,640]{1,0:T(8,128)(2,1)S(1)}, bf16[160,640]{1,0:T(8,128)(2,1)S(1)}, u32[]{:S(2)}, u32[]{:S(2)}) collective-permute-start(bf16[160,640]{1,0:T(8,128)(2,1)S(1)} %collective-permute-done.15.refs_5_), channel_id=1, source_target_pairs={{0,16},{16,0},{1,17},{17,1},{2,18},{18,2},{3,19},{19,3},{4,20},{20... | collective-permute-start | bytes 614408 | tf_op jit(solution)/shard_map/ppermute | solution.py:70
  91.4 13.2 %collective-permute-start.19 = (bf16[768,640]{1,0:T(8,128)(2,1)S(1)}, bf16[768,640]{1,0:T(8,128)(2,1)S(1)}, u32[]{:S(2)}, u32[]{:S(2)}) collective-permute-start(bf16[768,640]{1,0:T(8,128)(2,1)S(1)} %get-tuple-element.28), channel_id=1, source_target_pairs={{0,8},{8,0},{1,9},{9,1},{2,10},{10,2},{3,11},{11,3},{4,12},{12,4},... | collective-permute-start | bytes 2949128 | tf_op jit(solution)/shard_map/ppermute | solution.py:326

commit v2 on v1

--- a/solution.py
+++ b/solution.py
@@ -49,15 +49,28 @@
 
 
 def regroup(weight):
-    rows = weight.shape[0]
-    query = weight[:, :8192].reshape(rows, 8, 2, 512)
-    key = weight[:, 8192:9216].reshape(rows, 8, 1, HEAD)
-    value = weight[:, 9216:].reshape(rows, 8, 1, HEAD)
-    joined = jnp.concatenate([jnp.concatenate([key, value], axis=2), query], axis=3)
-    return joined.transpose(2, 1, 0, 3)
-
-
-def gather_blocks(block, ahead):
+    rows, groups, wide = weight.shape[0], 8, COLS - HEAD
+
+    def kernel(weight_ref, out_ref):
+        for core in range(2):
+            for group in range(groups):
+                index = core * groups + group
+                first = (HEADS + core) * HEADS * HEAD + group * HEAD
+                out_ref[index, :, :HEAD] = weight_ref[:, first : first + HEAD]
+                first = (group * 2 + core) * wide
+                out_ref[index, :, HEAD:] = weight_ref[:, first : first + wide]
+
+    return pl.pallas_call(
+        kernel,
+        out_shape=jax.ShapeDtypeStruct((2 * groups, rows, COLS), weight.dtype),
+        in_specs=[VMEM],
+        out_specs=VMEM,
+        compiler_params=pltpu.CompilerParams(vmem_limit_bytes=8 << 20),
+        name="regroup",
+    )(weight)
+
+
+def gather_blocks(place, block, ahead):
     half = GROUP // 2
 
     def up(array):
@@ -69,26 +82,35 @@
     def across(array):
         return lax.ppermute(array, "xh", SWAP)
 
+    other = across(block)
     up1, down1 = up(block), down(block)
-    other = across(block)
     up1, down1, ahead = lax.optimization_barrier((up1, down1, ahead))
     up2, down2 = up(up1), down(down1)
-    other_up1, other_down1 = across(up1), across(down1)
+    up1, other = lax.optimization_barrier((up1, other))
+    other_up1 = across(up1)
+    other_down1 = down(other)
     up3, down3 = up(up2), down(down2)
-    other_up2, other_down2 = up(other_up1), down(other_down1)
+    other_down2 = across(down2)
+    other_up2 = up(other_up1)
+    first = [
+        (block, 0, 0, 0), (other, 0, 1, 0), (up1, -1, 0, 0), (other_up1, -1, 1, 0),
+    ]
+    totals = project_early(place, first, ahead[:2])
+    up3, down3, totals = lax.optimization_barrier((up3, down3, totals))
     up4, down4 = up(up3[:half]), down(down3[half:])
+    totals = project_early(place, [(down1, 1, 0, 0), (other_down1, 1, 1, 0)], ahead[:2], totals)
+    other_up2, other_down2, totals = lax.optimization_barrier((other_up2, other_down2, totals))
+    other_up3, other_down3 = up(other_up2), down(other_down2)
     other_up4, other_down4 = across(up4), across(down4)
-    other_up3, other_down3 = up(other_up2), down(other_down2)
-    early = [
-        (block, 0, 0, 0), (other, 0, 1, 0),
-        (up1, -1, 0, 0), (other_up1, -1, 1, 0), (down1, 1, 0, 0), (other_down1, 1, 1, 0),
+    second = [
         (up2, -2, 0, 0), (other_up2, -2, 1, 0), (down2, 2, 0, 0), (other_down2, 2, 1, 0),
     ]
-    late = [
+    totals = project_early(place, second, ahead[:2], totals)
+    last = [
         (up3, -3, 0, 0), (other_up3, -3, 1, 0), (down3, 3, 0, 0), (other_down3, 3, 1, 0),
         (up4, 4, 0, 0), (down4, 4, 0, half), (other_up4, 4, 1, 0), (other_down4, 4, 1, half),
     ]
-    return early, late, ahead
+    return last, totals, ahead
 
 
 def slots_of(pieces):
@@ -99,16 +121,13 @@
     return offsets
 
 
-def weight_copies(place_ref, pieces, sources, target, sems):
+def assemble(place_ref, pieces, sources, target, wanted):
     offsets = slots_of(pieces)
-    copies = [[] for _ in offsets]
-    for number, (array, offset, flip, first) in enumerate(pieces):
-        slot = offsets.index(offset)
-        side = lax.rem(place_ref[1] + flip, 2)
-        row = pl.multiple_of(side * GROUP + (slot * DEPTH + first), 16)
-        where = target.at[pl.ds(row, array.shape[0])]
-        copies[slot].append(pltpu.make_async_copy(sources[number], where, sems.at[number]))
-    return copies
+    for (array, offset, flip, first), source in zip(pieces, sources):
+        if offsets.index(offset) == wanted:
+            side = lax.rem(place_ref[1] + flip, 2)
+            row = pl.multiple_of(side * GROUP + (wanted * DEPTH + first), 16)
+            target[pl.ds(row, array.shape[0])] = source[...]
 
 
 def slot_of(offset):
@@ -144,47 +163,42 @@
     )(place, pltpu.with_memory_space_constraint(tokens, pltpu.HBM))
 
 
-def project_early(place, pieces, held_sets):
+def project_early(place, pieces, held_sets, totals=()):
     offsets = slots_of(pieces)
     count = len(offsets)
 
     def kernel(place_ref, *refs):
         sources, held_refs = refs[: len(pieces)], refs[len(pieces) : len(pieces) + 2]
-        out_refs, (weight, sem_w) = refs[len(pieces) + 2 : len(pieces) + 4], refs[len(pieces) + 4 :]
-        weights = weight_copies(place_ref, pieces, sources, weight, sem_w)
-        for group in weights:
-            for copy in group:
-                copy.start()
+        total_refs, out_refs, weight = refs[len(pieces) + 2 : -3], refs[-3:-1], refs[-1]
         for slot, offset in enumerate(offsets):
-            for copy in weights[slot]:
-                copy.wait()
-            for held_ref, out_ref in zip(held_refs, out_refs):
+            assemble(place_ref, pieces, sources, weight, slot)
+            for which, (held_ref, out_ref) in enumerate(zip(held_refs, out_refs)):
                 product = jnp.dot(
                     held_ref[slot_of(offset)],
                     weight[slot * DEPTH : (slot + 1) * DEPTH],
                     preferred_element_type=jnp.float32,
                 )
-                if slot == 0:
+                if slot:
+                    out_ref[...] += product
+                elif total_refs:
+                    out_ref[...] = total_refs[which][...] + product
+                else:
                     out_ref[...] = product
-                else:
-                    out_ref[...] += product
 
     shape = pltpu.VMEM((ROWS, COLS), jnp.float32)
     return pl.pallas_call(
         kernel,
         out_shape=(shape, shape),
-        in_specs=[SMEM] + [ANYWHERE] * len(pieces) + [VMEM] * 2,
+        in_specs=[SMEM] + [VMEM] * (len(pieces) + 2 + len(totals)),
         out_specs=(VMEM, VMEM),
-        scratch_shapes=[
-            pltpu.VMEM((count * DEPTH, COLS), jnp.bfloat16),
-            pltpu.SemaphoreType.DMA((len(pieces),)),
-        ],
+        input_output_aliases={len(pieces) + 3 + which: which for which in range(len(totals))},
+        scratch_shapes=[pltpu.VMEM((count * DEPTH, COLS), jnp.bfloat16)],
         compiler_params=pltpu.CompilerParams(vmem_limit_bytes=16 << 20),
         cost_estimate=pl.CostEstimate(
             flops=4 * ROWS * count * DEPTH * COLS, bytes_accessed=18 << 20, transcendentals=0
         ),
         name="project_early",
-    )(place, *[piece[0] for piece in pieces], *held_sets)
+    )(place, *[piece[0] for piece in pieces], *held_sets, *totals)
 
 
 def project_late(place, pieces, held, partial, cosine, sine, query_gain, key_gain, ready=None):
@@ -196,15 +210,7 @@
         sources = refs[:n_in]
         held_ref, partial_ref, cos_ref, sin_ref, qgain_ref, kgain_ref, out_ref = refs[n_in : n_in + 7]
         core = place_ref[2]
-        weights = [[] for _ in offsets]
-        if ready is None:
-            weight, sem_w = refs[n_in + 7 :]
-            weights = weight_copies(place_ref, pieces, sources, weight, sem_w)
-        else:
-            weight = sources[0]
-        for group in weights:
-            for copy in group:
-                copy.start()
+        weight = refs[n_in + 7] if ready is None else sources[0]
 
         def normed(field, gain, rows):
             factor = lax.rsqrt(jnp.mean(field * field, axis=1, keepdims=True) + NORM_EPS)
@@ -215,9 +221,8 @@
             rows = pl.ds(tile * TILE, TILE)
             result = partial_ref[rows]
             for slot, offset in enumerate(offsets):
-                if tile == 0:
-                    for copy in weights[slot]:
-                        copy.wait()
+                if tile == 0 and ready is None:
+                    assemble(place_ref, pieces, sources, weight, slot)
                 result = result + jnp.dot(
                     held_ref[slot_of(offset), rows],
                     weight[slot * DEPTH : (slot + 1) * DEPTH],
@@ -236,9 +241,8 @@
     return pl.pallas_call(
         kernel,
         out_shape=(shape, weight_shape) if first else shape,
-        in_specs=[SMEM] + ([ANYWHERE] * n_in if first else [VMEM]) + [VMEM] * 6,
+        in_specs=[SMEM] + [VMEM] * (n_in + 6),
         out_specs=(VMEM, VMEM) if first else VMEM,
-        scratch_shapes=[pltpu.SemaphoreType.DMA((len(pieces),))] if first else [],
         compiler_params=pltpu.CompilerParams(vmem_limit_bytes=16 << 20),
         cost_estimate=pl.CostEstimate(
             flops=2 * ROWS * count * DEPTH * COLS, bytes_accessed=9 << 20, transcendentals=0
@@ -309,19 +313,19 @@
     )
     other_tokens = lax.ppermute(tokens, "c", SWAP)
     other_lengths = lax.ppermute(lengths, "c", SWAP)
-    spread = regroup(qkv_weight).reshape(16, -1, COLS)
+    spread = regroup(qkv_weight)
     block = lax.all_to_all(spread, ("c",) + TENSOR, split_axis=0, concat_axis=0, tiled=True)
     own_start, other_start = request_starts(lengths[0]), request_starts(other_lengths[0])
     own_tables, other_tables = rotary_tables(own_start), rotary_tables(other_start)
     held = hold_tokens(place, tokens)
     other_held = hold_tokens(place, other_tokens)
-    early, late, *ahead = gather_blocks(
-        block.reshape(GROUP, COLS), (held, other_held, *own_tables, *other_tables)
+    late, totals, ahead = gather_blocks(
+        place, block.reshape(GROUP, COLS), (held, other_held, *own_tables, *other_tables)
     )
-    held, other_held, *tables = ahead[0]
+    held, other_held, *tables = ahead
     own_tables, other_tables = tables[:2], tables[2:]
     gains = (query_norm_gain.reshape(1, HEAD), key_norm_gain.reshape(1, HEAD))
-    own_partial, other_partial = project_early(place, early, (held, other_held))
+    own_partial, other_partial = totals
     other, ready = project_late(place, late, other_held, other_partial, *other_tables, *gains)
     received = lax.ppermute(other, "c", SWAP)
     own = project_late(place, late, held, own_partial, *own_tables, *gains, ready)

time: 110 us -> 99.5 us (0.905)
  waiting for transfers between devices: 18.8 us -> 14.3 us
  local copies, waits for them, and re-layouts: 6.44 us -> 4.44 us
  Pallas kernels: 37 us -> 35.1 us
  starting transfers between devices: 42.4 us -> 41.2 us
    ppermute x5, waiting for transfers between devices: 7.87 us -> 0.73 us  [across(): return lax.ppermute(array, 'xh', SWAP)]
    ppermute x6, waiting for transfers between devices: 0.77 us -> 4.9 us  [down(): return lax.ppermute(array, 'z', DOWN)]
    ppermute x6, waiting for transfers between devices: 9.58 us -> 7.43 us  [up(): return lax.ppermute(array, 'z', UP)]
    pallas_call x2, Pallas kernels: 11 us -> 9.13 us  [project_late(): pl.pallas_call(kernel, out_shape=(shape, weight_shape) if first else shap...]
    slice x2 -> x0, local copies, waits for them, and re-layouts: 1.86 us -> none  [the longest x1 1.02 us: regroup(): query = weight[:, :8192].reshape(rows, 8, 2, 512)]
    ppermute x5, starting transfers between devices: 8.39 us -> 7.02 us  [across(): return lax.ppermute(array, 'xh', SWAP)]
    pallas_call x1 -> x4, Pallas kernels: 12.4 us -> 12.3 us  [the longest x3 11.5 us: project_early(): pl.pallas_call(kernel, out_shape=(shape, shape), in_specs=[SMEM] + [VMEM]...]
  transfers between devices with their start and end apart: 21 -> 21, of which waited for: 6 -> 5; matrix products, arithmetic and copies ran while one was open for 8% -> 4% of each run, Pallas kernels for 23% -> 25%
where the time goes in v2:
time: 99.5 us; the launch traced here: 99.3 us
  starting transfers between devices  41.2 us (41%)
  Pallas kernels  35.1 us (35%)
  waiting for transfers between devices  14.3 us (14%)
  local copies, waits for them, and re-layouts  4.44 us (4%)
  other arithmetic  4 us (4%)
    ppermute x6, starting transfers between devices, down(): return lax.ppermute(array, 'z', DOWN)  15.5 us
    pallas_call x3, Pallas kernels, project_early(): pl.pallas_call(kernel, out_shape=(shape, shape), in_specs=[SMEM] + [VMEM]...  11.5 us
    pallas_call x2, Pallas kernels, project_late(): pl.pallas_call(kernel, out_shape=(shape, weight_shape) if first else shap...  9.13 us
    pallas_call x2, Pallas kernels, hold_tokens(): pl.pallas_call(kernel, out_shape=pltpu.VMEM((NZ, ROWS, DEPTH), jnp.bfloat...  8.24 us
    ppermute x1, starting transfers between devices, shards(): received = lax.ppermute(other, 'c', SWAP)  7.71 us
    ppermute x6, waiting for transfers between devices, up(): return lax.ppermute(array, 'z', UP)  7.43 us
    ppermute x5, starting transfers between devices, across(): return lax.ppermute(array, 'xh', SWAP)  7.02 us
    pallas_call x1, Pallas kernels, attend(): pl.pallas_call(kernel, out_shape=jax.ShapeDtypeStruct((ROWS, 8 * HEAD), j...  5.38 us
  transfers between devices with their start and end apart: 21, of which 5 were waited for; matrix products, arithmetic and copies ran while one was open for 4% of the time, Pallas kernels for 25%

profile of v2, /device:TPU:1, one launch (start us, length us, event | category | flops | bytes accessed | tf_op | source)
XLA Modules:
  0.0 99.3 jit_solution(3396630642179100253)
XLA Ops:
  0.0 3.2 %collective-permute-start.2 = (bf16[768,5120]{1,0:T(8,128)(2,1)}, bf16[768,5120]{1,0:T(8,128)(2,1)}, u32[]{:S(2)}, u32[]{:S(2)}) collective-permute-start(bf16[768,5120]{1,0:T(8,128)(2,1)} %token_ref.1), channel_id=1, source_target_pairs={{0,8},{8,0},{1,9},{9,1},{2,10},{10,2},{3,11},{11,3},{4,12},{12,4},... | collective-permute-start | bytes 23592968 | tf_op jit(solution)/shard_map/ppermute | solution.py:314
  3.2 1.0 %copy-done.1 = bf16[20,10240]{1,0:T(8,128)(2,1)S(1)} copy-done((bf16[20,10240]{1,0:T(8,128)(2,1)S(1)}, bf16[20,10240]{1,0:T(8,128)(2,1)}, u32[]{:S(2)}) %copy-start.1) | copy-done | bytes 409624
  4.3 0.8 regroup.1
  5.1 4.2 %all-to-all-start = ((bf16[16,20,640]{2,1,0:T(8,128)(2,1)}), bf16[16,20,640]{2,1,0:T(8,128)(2,1)S(1)}, u32[]{:S(2)}, u32[]{:S(2)}) async-start(bf16[16,20,640]{2,1,0:T(8,128)(2,1)} %regroup.1), calls=%async_computation | async-start | bytes 983040 | tf_op jit(solution)/shard_map/all_to_all | solution.py:317
  9.5 3.9 %hold_tokens.2.refs_4_.refs_2_.refs_1_ = bf16[8,768,640]{2,1,0:T(8,128)(2,1)S(1)} custom-call(s32[3]{0:T(128)S(1)} %pad_add_fusion.place_ref, bf16[768,5120]{1,0:T(8,128)(2,1)} %token_ref.1), custom_call_target="tpu_custom_call" | custom-call | bytes 16777216 | tf_op jit(solution)/shard_map/hold_tokens/pallas_call | solution.py:154
  13.5 3.1 %copy-done = bf16[8,768,640]{2,1,0:T(8,128)(2,1)} copy-done((bf16[8,768,640]{2,1,0:T(8,128)(2,1)}, bf16[8,768,640]{2,1,0:T(8,128)(2,1)S(1)}, u32[]{:S(2)}) %copy-start) | copy-done | bytes 7864344
  17.0 1.2 %all-to-all-done = bf16[16,20,640]{2,1,0:T(8,128)(2,1)S(1)} async-done(((bf16[16,20,640]{2,1,0:T(8,128)(2,1)}), bf16[16,20,640]{2,1,0:T(8,128)(2,1)S(1)}, u32[]{:S(2)}, u32[]{:S(2)}) %all-to-all-start) | async-done | bytes 409632 | tf_op jit(solution)/shard_map/all_to_all | solution.py:317
  18.4 1.7 %collective-permute-start = (bf16[320,640]{1,0:T(8,128)(2,1)S(1)}, bf16[320,640]{1,0:T(8,128)(2,1)S(1)}, u32[]{:S(2)}, u32[]{:S(2)}) collective-permute-start(bf16[320,640]{1,0:T(8,128)(2,1)S(1)} %reshape.42.refs_0_), channel_id=1, source_target_pairs={{0,32},{32,64},{64,96},{96,128},{128,160},{160,192},{192,224},{224... | collective-permute-start | bytes 1228808 | tf_op jit(solution)/shard_map/ppermute | solution.py:77
  20.1 4.0 %collective-permute-start.1 = (bf16[320,640]{1,0:T(8,128)(2,1)S(1)}, bf16[320,640]{1,0:T(8,128)(2,1)S(1)}, u32[]{:S(2)}, u32[]{:S(2)}) collective-permute-start(bf16[320,640]{1,0:T(8,128)(2,1)S(1)} %reshape.42.refs_0_), channel_id=1, source_target_pairs={{0,224},{32,0},{64,32},{96,64},{128,96},{160,128},{192,160},{224,1... | collective-permute-start | bytes 1228808 | tf_op jit(solution)/shard_map/ppermute | solution.py:80
  24.1 2.5 %collective-permute-start.8 = (bf16[320,640]{1,0:T(8,128)(2,1)S(1)}, bf16[320,640]{1,0:T(8,128)(2,1)S(1)}, u32[]{:S(2)}, u32[]{:S(2)}) collective-permute-start(bf16[320,640]{1,0:T(8,128)(2,1)S(1)} %reshape.42.refs_0_), channel_id=1, source_target_pairs={{0,16},{16,0},{1,17},{17,1},{2,18},{18,2},{3,19},{19,3},{4,20},{20... | collective-permute-start | bytes 1228808 | tf_op jit(solution)/shard_map/ppermute | solution.py:83
  26.5 2.8 %fusion.1 = (f32[768,64]{1,0:T(8,128)S(1)}, f32[768,64]{1,0:T(8,128)S(1)}, f32[768,64]{1,0:T(8,128)S(1)}, f32[768,64]{1,0:T(8,128)S(1)}, f32[768,64]{1,0:T(8,128)S(1)}, /*index=5*/f32[768,64]{1,0:T(8,128)S(1)}) fusion(f32[64]{0:T(128)S(1)} %multiply_power_fusion, f32[768]{0:T(1024)S(1)} %subtract_convert_fusion, f32[768]{0:T(1024)S(1)} %subtract_convert_fusion.1), kind=kLoop, calls=%fused_computation.9 | loop fusion | flops 196608 | bytes 1186048 | tf_op jit(solution)/shard_map/neg | solution.py:48
  29.9 4.3 %hold_tokens.3.refs_5_.refs_3_.refs_8_ = bf16[8,768,640]{2,1,0:T(8,128)(2,1)S(1)} custom-call(s32[3]{0:T(128)S(1)} %pad_add_fusion.place_ref, bf16[768,5120]{1,0:T(8,128)(2,1)} %collective-permute-done.2.token_ref), custom_call_target="tpu_custom_call" | custom-call | bytes 16777216 | tf_op jit(solution)/shard_map/hold_tokens/pallas_call | solution.py:154
  34.4 2.7 %collective-permute-start.6 = (bf16[320,640]{1,0:T(8,128)(2,1)S(1)}, bf16[320,640]{1,0:T(8,128)(2,1)S(1)}, u32[]{:S(2)}, u32[]{:S(2)}) collective-permute-start(bf16[320,640]{1,0:T(8,128)(2,1)S(1)} %collective-permute-done.1.refs_0_), channel_id=1, source_target_pairs={{0,224},{32,0},{64,32},{96,64},{128,96},{160,128},{192,160},{224,1... | collective-permute-start | bytes 1228808 | tf_op jit(solution)/shard_map/ppermute | solution.py:80
  37.1 0.8 collective-permute-start.9
  37.9 7.0 %collective-permute-done.4.refs_0_ = bf16[320,640]{1,0:T(8,128)(2,1)S(1)} collective-permute-done((bf16[320,640]{1,0:T(8,128)(2,1)S(1)}, bf16[320,640]{1,0:T(8,128)(2,1)S(1)}, u32[]{:S(2)}, u32[]{:S(2)}) %collective-permute-start.4) | collective-permute-done | bytes 409632 | tf_op jit(solution)/shard_map/ppermute | solution.py:77
  44.9 2.7 %collective-permute-start.7 = (bf16[320,640]{1,0:T(8,128)(2,1)S(1)}, bf16[320,640]{1,0:T(8,128)(2,1)S(1)}, u32[]{:S(2)}, u32[]{:S(2)}) collective-permute-start(bf16[320,640]{1,0:T(8,128)(2,1)S(1)} %collective-permute-done.6.refs_2_), channel_id=1, source_target_pairs={{0,224},{32,0},{64,32},{96,64},{128,96},{160,128},{192,160},{224,1... | collective-permute-start | bytes 1228808 | tf_op jit(solution)/shard_map/ppermute | solution.py:80
  47.6 1.4 %collective-permute-start.10 = (bf16[320,640]{1,0:T(8,128)(2,1)S(1)}, bf16[320,640]{1,0:T(8,128)(2,1)S(1)}, u32[]{:S(2)}, u32[]{:S(2)}) collective-permute-start(bf16[320,640]{1,0:T(8,128)(2,1)S(1)} %collective-permute-done.9.refs_3_), channel_id=1, source_target_pairs={{0,32},{32,64},{64,96},{96,128},{128,160},{160,192},{192,224},{224... | collective-permute-start | bytes 1228808 | tf_op jit(solution)/shard_map/ppermute | solution.py:77
  49.1 0.8 collective-permute-start.11
  49.8 4.3 %project_early.3 = (f32[768,640]{1,0:T(8,128)S(1)}, f32[768,640]{1,0:T(8,128)S(1)}) custom-call(s32[3]{0:T(128)S(1)} %pad_add_fusion.place_ref, bf16[320,640]{1,0:T(8,128)(2,1)S(1)} %reshape.42.refs_0_, bf16[320,640]{1,0:T(8,128)(2,1)S(1)} %collective-permute-done.8.refs_1_, bf16[320,640]{1,0:T(8,128)(2,1)S(1)} %collective-permute-done.refs_2_, ...), custom_call_target="tpu_custom_call" | custom-call | flops 2516582400 | bytes 18874368 | tf_op jit(solution)/shard_map/project_early/pallas_call | solution.py:189
  54.1 0.4 collective-permute-done.5.refs_0_
  54.7 2.7 %collective-permute-start.16 = (bf16[160,640]{1,0:T(8,128)(2,1)S(1)}, bf16[160,640]{1,0:T(8,128)(2,1)S(1)}, u32[]{:S(2)}, u32[]{:S(2)}) collective-permute-start(bf16[160,640]{1,0:T(8,128)(2,1)S(1)} %slice.7), channel_id=1, source_target_pairs={{0,224},{32,0},{64,32},{96,64},{128,96},{160,128},{192,160},{224,1... | collective-permute-start | bytes 614408 | tf_op jit(solution)/shard_map/ppermute | solution.py:80
  57.4 4.9 %collective-permute-done.12.refs_1_ = bf16[320,640]{1,0:T(8,128)(2,1)S(1)} collective-permute-done((bf16[320,640]{1,0:T(8,128)(2,1)S(1)}, bf16[320,640]{1,0:T(8,128)(2,1)S(1)}, u32[]{:S(2)}, u32[]{:S(2)}) %collective-permute-start.12) | collective-permute-done | bytes 409632 | tf_op jit(solution)/shard_map/ppermute | solution.py:80
  62.3 2.6 %project_early.4 = (f32[768,640]{1,0:T(8,128)S(1)}, f32[768,640]{1,0:T(8,128)S(1)}) custom-call(s32[3]{0:T(128)S(1)} %pad_add_fusion.place_ref, bf16[320,640]{1,0:T(8,128)(2,1)S(1)} %collective-permute-done.1.refs_0_, bf16[320,640]{1,0:T(8,128)(2,1)S(1)} %collective-permute-done.12.refs_1_, ...), custom_call_target="tpu_custom_call", output_to_operand_aliasing={{0}: (5, {}), {1}: (6, {})} | custom-call | flops 1258291200 | bytes 18874368 | tf_op jit(solution)/shard_map/project_early/pallas_call | solution.py:189
  65.2 3.3 %collective-permute-start.14 = (bf16[320,640]{1,0:T(8,128)(2,1)S(1)}, bf16[320,640]{1,0:T(8,128)(2,1)S(1)}, u32[]{:S(2)}, u32[]{:S(2)}) collective-permute-start(bf16[320,640]{1,0:T(8,128)(2,1)S(1)} %collective-permute-done.11.refs_3_), channel_id=1, source_target_pairs={{0,224},{32,0},{64,32},{96,64},{128,96},{160,128},{192,160},{224,1... | collective-permute-start | bytes 1228808 | tf_op jit(solution)/shard_map/ppermute | solution.py:80
  68.5 0.7 collective-permute-start.17
  69.3 2.2 %collective-permute-start.18 = (bf16[160,640]{1,0:T(8,128)(2,1)S(1)}, bf16[160,640]{1,0:T(8,128)(2,1)S(1)}, u32[]{:S(2)}, u32[]{:S(2)}) collective-permute-start(bf16[160,640]{1,0:T(8,128)(2,1)S(1)} %collective-permute-done.16.refs_5_), channel_id=1, source_target_pairs={{0,16},{16,0},{1,17},{17,1},{2,18},{18,2},{3,19},{19,3},{4,20},{20... | collective-permute-start | bytes 614408 | tf_op jit(solution)/shard_map/ppermute | solution.py:83
  71.5 4.6 %project_early.5 = (f32[768,640]{1,0:T(8,128)S(1)}, f32[768,640]{1,0:T(8,128)S(1)}) custom-call(s32[3]{0:T(128)S(1)} %pad_add_fusion.place_ref, bf16[320,640]{1,0:T(8,128)(2,1)S(1)} %collective-permute-done.4.refs_0_, bf16[320,640]{1,0:T(8,128)(2,1)S(1)} %collective-permute-done.10.refs_1_, ...), custom_call_target="tpu_custom_call", output_to_operand_aliasing={{0}: (7, {}), {1}: (8, {})} | custom-call | flops 2516582400 | bytes 18874368 | tf_op jit(solution)/shard_map/project_early/pallas_call | solution.py:189
  76.1 0.7 collective-permute-done.18.refs_7_
  76.9 4.7 %project_late.2 = (bf16[768,640]{1,0:T(8,128)(2,1)S(1)}, bf16[1920,640]{1,0:T(8,128)(2,1)S(1)}) custom-call(s32[3]{0:T(128)S(1)} %pad_add_fusion.place_ref, bf16[320,640]{1,0:T(8,128)(2,1)S(1)} %collective-permute-done.5.refs_0_, bf16[320,640]{1,0:T(8,128)(2,1)S(1)} %collective-permute-done.13.refs_1_, bf16[320,640]{1,0:T(8,128)(2,1)S(1)} %collective-permute-done.7.refs_2_, ...), custom_call_target="tpu_custom_call" | custom-call | flops 1887436800 | bytes 9437184 | tf_op jit(solution)/shard_map/project_late/pallas_call | solution.py:241
  81.5 7.7 %collective-permute-start.19 = (bf16[768,640]{1,0:T(8,128)(2,1)S(1)}, bf16[768,640]{1,0:T(8,128)(2,1)S(1)}, u32[]{:S(2)}, u32[]{:S(2)}) collective-permute-start(bf16[768,640]{1,0:T(8,128)(2,1)S(1)} %get-tuple-element.56), channel_id=1, source_target_pairs={{0,8},{8,0},{1,9},{9,1},{2,10},{10,2},{3,11},{11,3},{4,12},{12,4},... | collective-permute-start | bytes 2949128 | tf_op jit(solution)/shard_map/ppermute | solution.py:330
  89.4 4.5 %project_late.3.own_ref = bf16[768,640]{1,0:T(8,128)(2,1)S(1)} custom-call(s32[3]{0:T(128)S(1)} %pad_add_fusion.place_ref, bf16[1920,640]{1,0:T(8,128)(2,1)S(1)} %get-tuple-element.52.refs_0_, bf16[8,768,640]{2,1,0:T(8,128)(2,1)S(1)} %bitcast.10, f32[768,640]{1,0:T(8,128)S(1)} %get-tuple-element.53.refs_2_, f32[768,128]{1,0:T(8,128)S(1)} %get-tuple-element.54.refs_3_, ...), custom_call_target="tpu_custom_call" | custom-call | flops 1887436800 | bytes 9437184 | tf_op jit(solution)/shard_map/project_late/pallas_call | solution.py:241
  93.9 5.4 %attend.1 = bf16[768,1024]{1,0:T(8,128)(2,1)} custom-call(s32[3]{0:T(128)S(1)} %pad_add_fusion.place_ref, bf16[768,640]{1,0:T(8,128)(2,1)S(1)} %project_late.3.own_ref, bf16[768,640]{1,0:T(8,128)(2,1)S(1)} %collective-permute-done.19.received_ref, s32[768,1]{1,0:T(8,128)S(1)} %reduce_max.23.start_ref), custom_call_target="tpu_custom_call" | custom-call | flops 1610612736 | bytes 4194304 | tf_op jit(solution)/shard_map/attend/pallas_call | solution.py:293
  (51 shorter events, 2.0 us)
Async XLA Ops:
  0.0 29.9 %collective-permute-start.2 = (bf16[768,5120]{1,0:T(8,128)(2,1)}, bf16[768,5120]{1,0:T(8,128)(2,1)}, u32[]{:S(2)}, u32[]{:S(2)}) collective-permute-start(bf16[768,5120]{1,0:T(8,128)(2,1)} %token_ref.1), channel_id=1, source_target_pairs={{0,8},{8,0},{1,9},{9,1},{2,10},{10,2},{3,11},{11,3},{4,12},{12,4},... | collective-permute-start | bytes 23592968 | tf_op jit(solution)/shard_map/ppermute | solution.py:314
  3.2 13.5 %collective-permute-start.3 = (s32[1,8]{1,0:T(1,128)}, s32[1,8]{1,0:T(1,128)S(1)}, u32[]{:S(2)}, u32[]{:S(2)}) collective-permute-start(s32[1,8]{1,0:T(1,128)} %param.6), channel_id=1, source_target_pairs={{0,8},{8,0},{1,9},{9,1},{2,10},{10,2},{3,11},{11,3},{4,12},{12,4},... | collective-permute-start | bytes 104 | tf_op jit(solution)/shard_map/ppermute | solution.py:315
  3.2 1.0 %copy-start.1 = (bf16[20,10240]{1,0:T(8,128)(2,1)S(1)}, bf16[20,10240]{1,0:T(8,128)(2,1)}, u32[]{:S(2)}) copy-start(bf16[20,10240]{1,0:T(8,128)(2,1)} %weight_ref.1) | copy-start | bytes 1228804
  4.3 5.0 %copy-start.4 = (s32[1,8]{1,0:T(1,128)S(1)}, s32[1,8]{1,0:T(1,128)}, u32[]{:S(2)}) copy-start(s32[1,8]{1,0:T(1,128)} %param.6) | copy-start | bytes 100
  5.1 13.2 %all-to-all-start = ((bf16[16,20,640]{2,1,0:T(8,128)(2,1)}), bf16[16,20,640]{2,1,0:T(8,128)(2,1)S(1)}, u32[]{:S(2)}, u32[]{:S(2)}) async-start(bf16[16,20,640]{2,1,0:T(8,128)(2,1)} %regroup.1), calls=%async_computation | async-start | bytes 983040 | tf_op jit(solution)/shard_map/all_to_all | solution.py:317
  13.5 3.1 %copy-start = (bf16[8,768,640]{2,1,0:T(8,128)(2,1)}, bf16[8,768,640]{2,1,0:T(8,128)(2,1)S(1)}, u32[]{:S(2)}) copy-start(bf16[8,768,640]{2,1,0:T(8,128)(2,1)S(1)} %hold_tokens.2.refs_4_.refs_2_.refs_1_) | copy-start | bytes 23592964
  18.4 15.9 %collective-permute-start = (bf16[320,640]{1,0:T(8,128)(2,1)S(1)}, bf16[320,640]{1,0:T(8,128)(2,1)S(1)}, u32[]{:S(2)}, u32[]{:S(2)}) collective-permute-start(bf16[320,640]{1,0:T(8,128)(2,1)S(1)} %reshape.42.refs_0_), channel_id=1, source_target_pairs={{0,32},{32,64},{64,96},{96,128},{128,160},{160,192},{192,224},{224... | collective-permute-start | bytes 1228808 | tf_op jit(solution)/shard_map/ppermute | solution.py:77
  20.1 14.2 %collective-permute-start.1 = (bf16[320,640]{1,0:T(8,128)(2,1)S(1)}, bf16[320,640]{1,0:T(8,128)(2,1)S(1)}, u32[]{:S(2)}, u32[]{:S(2)}) collective-permute-start(bf16[320,640]{1,0:T(8,128)(2,1)S(1)} %reshape.42.refs_0_), channel_id=1, source_target_pairs={{0,224},{32,0},{64,32},{96,64},{128,96},{160,128},{192,160},{224,1... | collective-permute-start | bytes 1228808 | tf_op jit(solution)/shard_map/ppermute | solution.py:80
  24.1 13.0 %collective-permute-start.8 = (bf16[320,640]{1,0:T(8,128)(2,1)S(1)}, bf16[320,640]{1,0:T(8,128)(2,1)S(1)}, u32[]{:S(2)}, u32[]{:S(2)}) collective-permute-start(bf16[320,640]{1,0:T(8,128)(2,1)S(1)} %reshape.42.refs_0_), channel_id=1, source_target_pairs={{0,16},{16,0},{1,17},{17,1},{2,18},{18,2},{3,19},{19,3},{4,20},{20... | collective-permute-start | bytes 1228808 | tf_op jit(solution)/shard_map/ppermute | solution.py:83
  29.6 20.2 %slice-start = ((s8[7864320]{0:T(1024)(128)(4,1)}), s8[4194304]{0:T(1024)(128)(4,1)S(1)}, s32[]{:S(2)}) async-start(s8[7864320]{0:T(1024)(128)(4,1)} %bitcast.9), calls=%async_computation.1 | async-start | bytes 8388608
  29.9 19.9 %slice-start.1 = ((s8[7864320]{0:T(1024)(128)(4,1)}), s8[3670016]{0:T(1024)(128)(4,1)S(1)}, s32[]{:S(2)}) async-start(s8[7864320]{0:T(1024)(128)(4,1)} %bitcast.9), calls=%async_computation.2 | async-start | bytes 7340032
  34.3 10.6 %collective-permute-start.4 = (bf16[320,640]{1,0:T(8,128)(2,1)S(1)}, bf16[320,640]{1,0:T(8,128)(2,1)S(1)}, u32[]{:S(2)}, u32[]{:S(2)}) collective-permute-start(bf16[320,640]{1,0:T(8,128)(2,1)S(1)} %collective-permute-done.refs_2_), channel_id=1, source_target_pairs={{0,32},{32,64},{64,96},{96,128},{128,160},{160,192},{192,224},{224... | collective-permute-start | bytes 1228808 | tf_op jit(solution)/shard_map/ppermute | solution.py:77
  34.4 10.5 %collective-permute-start.6 = (bf16[320,640]{1,0:T(8,128)(2,1)S(1)}, bf16[320,640]{1,0:T(8,128)(2,1)S(1)}, u32[]{:S(2)}, u32[]{:S(2)}) collective-permute-start(bf16[320,640]{1,0:T(8,128)(2,1)S(1)} %collective-permute-done.1.refs_0_), channel_id=1, source_target_pairs={{0,224},{32,0},{64,32},{96,64},{128,96},{160,128},{192,160},{224,1... | collective-permute-start | bytes 1228808 | tf_op jit(solution)/shard_map/ppermute | solution.py:80
  37.1 10.6 %collective-permute-start.9 = (bf16[320,640]{1,0:T(8,128)(2,1)S(1)}, bf16[320,640]{1,0:T(8,128)(2,1)S(1)}, u32[]{:S(2)}, u32[]{:S(2)}) collective-permute-start(bf16[320,640]{1,0:T(8,128)(2,1)S(1)} %collective-permute-done.refs_2_), channel_id=1, source_target_pairs={{0,16},{16,0},{1,17},{17,1},{2,18},{18,2},{3,19},{19,3},{4,20},{20... | collective-permute-start | bytes 1228808 | tf_op jit(solution)/shard_map/ppermute | solution.py:83
  44.9 9.6 %collective-permute-start.5 = (bf16[320,640]{1,0:T(8,128)(2,1)S(1)}, bf16[320,640]{1,0:T(8,128)(2,1)S(1)}, u32[]{:S(2)}, u32[]{:S(2)}) collective-permute-start(bf16[320,640]{1,0:T(8,128)(2,1)S(1)} %collective-permute-done.4.refs_0_), channel_id=1, source_target_pairs={{0,32},{32,64},{64,96},{96,128},{128,160},{160,192},{192,224},{224... | collective-permute-start | bytes 1228808 | tf_op jit(solution)/shard_map/ppermute | solution.py:77
  44.9 9.6 %collective-permute-start.7 = (bf16[320,640]{1,0:T(8,128)(2,1)S(1)}, bf16[320,640]{1,0:T(8,128)(2,1)S(1)}, u32[]{:S(2)}, u32[]{:S(2)}) collective-permute-start(bf16[320,640]{1,0:T(8,128)(2,1)S(1)} %collective-permute-done.6.refs_2_), channel_id=1, source_target_pairs={{0,224},{32,0},{64,32},{96,64},{128,96},{160,128},{192,160},{224,1... | collective-permute-start | bytes 1228808 | tf_op jit(solution)/shard_map/ppermute | solution.py:80
  47.6 14.7 %collective-permute-start.12 = (bf16[320,640]{1,0:T(8,128)(2,1)S(1)}, bf16[320,640]{1,0:T(8,128)(2,1)S(1)}, u32[]{:S(2)}, u32[]{:S(2)}) collective-permute-start(bf16[320,640]{1,0:T(8,128)(2,1)S(1)} %collective-permute-done.8.refs_1_), channel_id=1, source_target_pairs={{0,224},{32,0},{64,32},{96,64},{128,96},{160,128},{192,160},{224,1... | collective-permute-start | bytes 1228808 | tf_op jit(solution)/shard_map/ppermute | solution.py:80
  47.6 17.3 %collective-permute-start.10 = (bf16[320,640]{1,0:T(8,128)(2,1)S(1)}, bf16[320,640]{1,0:T(8,128)(2,1)S(1)}, u32[]{:S(2)}, u32[]{:S(2)}) collective-permute-start(bf16[320,640]{1,0:T(8,128)(2,1)S(1)} %collective-permute-done.9.refs_3_), channel_id=1, source_target_pairs={{0,32},{32,64},{64,96},{96,128},{128,160},{160,192},{192,224},{224... | collective-permute-start | bytes 1228808 | tf_op jit(solution)/shard_map/ppermute | solution.py:77
  49.1 15.9 %collective-permute-start.11 = (bf16[320,640]{1,0:T(8,128)(2,1)S(1)}, bf16[320,640]{1,0:T(8,128)(2,1)S(1)}, u32[]{:S(2)}, u32[]{:S(2)}) collective-permute-start(bf16[320,640]{1,0:T(8,128)(2,1)S(1)} %collective-permute-done.6.refs_2_), channel_id=1, source_target_pairs={{0,16},{16,0},{1,17},{17,1},{2,18},{18,2},{3,19},{19,3},{4,20},{20... | collective-permute-start | bytes 1228808 | tf_op jit(solution)/shard_map/ppermute | solution.py:83
  54.5 14.0 %collective-permute-start.15 = (bf16[160,640]{1,0:T(8,128)(2,1)S(1)}, bf16[160,640]{1,0:T(8,128)(2,1)S(1)}, u32[]{:S(2)}, u32[]{:S(2)}) collective-permute-start(bf16[160,640]{1,0:T(8,128)(2,1)S(1)} %slice.6), channel_id=1, source_target_pairs={{0,32},{32,64},{64,96},{96,128},{128,160},{160,192},{192,224},{224... | collective-permute-start | bytes 614408 | tf_op jit(solution)/shard_map/ppermute | solution.py:77
  54.7 14.6 %collective-permute-start.16 = (bf16[160,640]{1,0:T(8,128)(2,1)S(1)}, bf16[160,640]{1,0:T(8,128)(2,1)S(1)}, u32[]{:S(2)}, u32[]{:S(2)}) collective-permute-start(bf16[160,640]{1,0:T(8,128)(2,1)S(1)} %slice.7), channel_id=1, source_target_pairs={{0,224},{32,0},{64,32},{96,64},{128,96},{160,128},{192,160},{224,1... | collective-permute-start | bytes 614408 | tf_op jit(solution)/shard_map/ppermute | solution.py:80
  64.9 11.9 %copy-start.2 = (f32[128]{0:T(128)S(1)}, f32[128]{0:T(128)}, u32[]{:S(2)}) copy-start(f32[128]{0:T(128)} %param.8) | copy-start | bytes 1540
  65.0 11.9 %copy-start.3 = (f32[128]{0:T(128)S(1)}, f32[128]{0:T(128)}, u32[]{:S(2)}) copy-start(f32[128]{0:T(128)} %param.9) | copy-start | bytes 1540
  65.0 11.1 %collective-permute-start.13 = (bf16[320,640]{1,0:T(8,128)(2,1)S(1)}, bf16[320,640]{1,0:T(8,128)(2,1)S(1)}, u32[]{:S(2)}, u32[]{:S(2)}) collective-permute-start(bf16[320,640]{1,0:T(8,128)(2,1)S(1)} %collective-permute-done.10.refs_1_), channel_id=1, source_target_pairs={{0,32},{32,64},{64,96},{96,128},{128,160},{160,192},{192,224},{224... | collective-permute-start | bytes 1228808 | tf_op jit(solution)/shard_map/ppermute | solution.py:77
  65.2 10.9 %collective-permute-start.14 = (bf16[320,640]{1,0:T(8,128)(2,1)S(1)}, bf16[320,640]{1,0:T(8,128)(2,1)S(1)}, u32[]{:S(2)}, u32[]{:S(2)}) collective-permute-start(bf16[320,640]{1,0:T(8,128)(2,1)S(1)} %collective-permute-done.11.refs_3_), channel_id=1, source_target_pairs={{0,224},{32,0},{64,32},{96,64},{128,96},{160,128},{192,160},{224,1... | collective-permute-start | bytes 1228808 | tf_op jit(solution)/shard_map/ppermute | solution.py:80
  68.5 7.6 %collective-permute-start.17 = (bf16[160,640]{1,0:T(8,128)(2,1)S(1)}, bf16[160,640]{1,0:T(8,128)(2,1)S(1)}, u32[]{:S(2)}, u32[]{:S(2)}) collective-permute-start(bf16[160,640]{1,0:T(8,128)(2,1)S(1)} %collective-permute-done.15.refs_4_), channel_id=1, source_target_pairs={{0,16},{16,0},{1,17},{17,1},{2,18},{18,2},{3,19},{19,3},{4,20},{20... | collective-permute-start | bytes 614408 | tf_op jit(solution)/shard_map/ppermute | solution.py:83
  69.3 7.6 %collective-permute-start.18 = (bf16[160,640]{1,0:T(8,128)(2,1)S(1)}, bf16[160,640]{1,0:T(8,128)(2,1)S(1)}, u32[]{:S(2)}, u32[]{:S(2)}) collective-permute-start(bf16[160,640]{1,0:T(8,128)(2,1)S(1)} %collective-permute-done.16.refs_5_), channel_id=1, source_target_pairs={{0,16},{16,0},{1,17},{17,1},{2,18},{18,2},{3,19},{19,3},{4,20},{20... | collective-permute-start | bytes 614408 | tf_op jit(solution)/shard_map/ppermute | solution.py:83
  81.5 12.3 %collective-permute-start.19 = (bf16[768,640]{1,0:T(8,128)(2,1)S(1)}, bf16[768,640]{1,0:T(8,128)(2,1)S(1)}, u32[]{:S(2)}, u32[]{:S(2)}) collective-permute-start(bf16[768,640]{1,0:T(8,128)(2,1)S(1)} %get-tuple-element.56), channel_id=1, source_target_pairs={{0,8},{8,0},{1,9},{9,1},{2,10},{10,2},{3,11},{11,3},{4,12},{12,4},... | collective-permute-start | bytes 2949128 | tf_op jit(solution)/shard_map/ppermute | solution.py:330

commit v3 on v2

--- a/solution.py
+++ b/solution.py
@@ -22,8 +22,8 @@
 LONGEST = 384
 QBLOCK = 128
 TENSOR = ("y", "xl")
-UP = [(z, (z + 1) % NZ) for z in range(NZ)]
-DOWN = [(z, (z - 1) % NZ) for z in range(NZ)]
+UP = [(z * 2 + c, (z + (1 - 2 * c)) % NZ * 2 + c) for z in range(NZ) for c in range(2)]
+DOWN = [(target, source) for source, target in UP]
 SWAP = [(0, 1), (1, 0)]
 
 ANYWHERE = pl.BlockSpec(memory_space=pl.ANY)
@@ -71,13 +71,11 @@
 
 
 def gather_blocks(place, block, ahead):
-    half = GROUP // 2
-
     def up(array):
-        return lax.ppermute(array, "z", UP)
+        return lax.ppermute(array, ("z", "c"), UP)
 
     def down(array):
-        return lax.ppermute(array, "z", DOWN)
+        return lax.ppermute(array, ("z", "c"), DOWN)
 
     def across(array):
         return lax.ppermute(array, "xh", SWAP)
@@ -85,31 +83,35 @@
     other = across(block)
     up1, down1 = up(block), down(block)
     up1, down1, ahead = lax.optimization_barrier((up1, down1, ahead))
+    held = ahead[:2]
     up2, down2 = up(up1), down(down1)
     up1, other = lax.optimization_barrier((up1, other))
+    other_down1 = down(other)
     other_up1 = across(up1)
-    other_down1 = down(other)
+    totals = project_early(place, [(block, 0, 0, 0), (other, 0, 1, 0)], held)
+    up2, down2, totals = lax.optimization_barrier((up2, down2, totals))
     up3, down3 = up(up2), down(down2)
     other_down2 = across(down2)
     other_up2 = up(other_up1)
-    first = [
-        (block, 0, 0, 0), (other, 0, 1, 0), (up1, -1, 0, 0), (other_up1, -1, 1, 0),
+    nearest = [
+        (up1, -1, 0, 0), (other_up1, -1, 1, 0), (down1, 1, 0, 0), (other_down1, 1, 1, 0),
     ]
-    totals = project_early(place, first, ahead[:2])
+    totals = project_early(place, nearest, held, totals)
     up3, down3, totals = lax.optimization_barrier((up3, down3, totals))
-    up4, down4 = up(up3[:half]), down(down3[half:])
-    totals = project_early(place, [(down1, 1, 0, 0), (other_down1, 1, 1, 0)], ahead[:2], totals)
-    other_up2, other_down2, totals = lax.optimization_barrier((other_up2, other_down2, totals))
-    other_up3, other_down3 = up(other_up2), down(other_down2)
-    other_up4, other_down4 = across(up4), across(down4)
+    down4 = down(down3)
+    other_down3 = across(down3)
+    other_up3 = up(other_up2)
     second = [
         (up2, -2, 0, 0), (other_up2, -2, 1, 0), (down2, 2, 0, 0), (other_down2, 2, 1, 0),
     ]
-    totals = project_early(place, second, ahead[:2], totals)
-    last = [
+    totals = project_early(place, second, held, totals)
+    down4, totals = lax.optimization_barrier((down4, totals))
+    other_down4 = across(down4)
+    third = [
         (up3, -3, 0, 0), (other_up3, -3, 1, 0), (down3, 3, 0, 0), (other_down3, 3, 1, 0),
-        (up4, 4, 0, 0), (down4, 4, 0, half), (other_up4, 4, 1, 0), (other_down4, 4, 1, half),
     ]
+    totals = project_early(place, third, held, totals)
+    last = [(down4, 4, 0, 0), (other_down4, 4, 1, 0)]
     return last, totals, ahead
 
 
@@ -136,11 +138,13 @@
 
 def hold_tokens(place, tokens):
     def kernel(place_ref, token_ref, out_ref, sems):
+        z, core = place_ref[0], place_ref[2]
+        wheres = [
+            lax.rem(z + jnp.where(core == 0, slot, (NZ - slot) % NZ), NZ) for slot in range(NZ)
+        ]
         copies = [
             pltpu.make_async_copy(
-                token_ref.at[
-                    :, pl.ds(pl.multiple_of(lax.rem(place_ref[0] + slot, NZ) * DEPTH, HEAD), DEPTH)
-                ],
+                token_ref.at[:, pl.ds(pl.multiple_of(wheres[slot] * DEPTH, HEAD), DEPTH)],
                 out_ref.at[slot],
                 sems.at[slot],
             )

time: 99.5 us -> 97.3 us (0.978)
  starting transfers between devices: 41.2 us -> 31.1 us
  waiting for transfers between devices: 14.3 us -> 20.8 us
  Pallas kernels: 35.1 us -> 36.5 us
    ppermute x12 -> x10, starting transfers between devices: 19 us -> 12.9 us  [the longest x5 11.4 us: up(): return lax.ppermute(array, ('z', 'c'), UP)]
    pallas_call x3 -> x4, Pallas kernels: 11.5 us -> 16.3 us  [project_early(): pl.pallas_call(kernel, out_shape=(shape, shape), in_specs=[SMEM] + [VMEM]...]
    ppermute x12 -> x10, waiting for transfers between devices: 12.3 us -> 16.6 us  [the longest x5 9.32 us: up(): return lax.ppermute(array, ('z', 'c'), UP)]
    ppermute x1, starting transfers between devices: 7.71 us -> 3.55 us  [shards(): received = lax.ppermute(other, 'c', SWAP)]
    pallas_call x2, Pallas kernels: 9.13 us -> 5.79 us  [project_late(): pl.pallas_call(kernel, out_shape=(shape, weight_shape) if first else shap...]
    ppermute x5, waiting for transfers between devices: 0.73 us -> 2.94 us  [across(): return lax.ppermute(array, 'xh', SWAP)]
  transfers between devices with their start and end apart: 21 -> 19, of which waited for: 5 -> 11; matrix products, arithmetic and copies ran while one was open for 4% -> 4% of each run, Pallas kernels for 25% -> 29%
where the time goes in v3:
time: 97.3 us; the launch traced here: 97.1 us
  Pallas kernels  36.5 us (38%)
  starting transfers between devices  31.1 us (32%)
  waiting for transfers between devices  20.8 us (21%)
  local copies, waits for them, and re-layouts  4.41 us (5%)
  other arithmetic  3.99 us (4%)
    pallas_call x4, Pallas kernels, project_early(): pl.pallas_call(kernel, out_shape=(shape, shape), in_specs=[SMEM] + [VMEM]...  16.3 us
    ppermute x5, starting transfers between devices, up(): return lax.ppermute(array, ('z', 'c'), UP)  11.4 us
    ppermute x5, waiting for transfers between devices, up(): return lax.ppermute(array, ('z', 'c'), UP)  9.32 us
    pallas_call x2, Pallas kernels, hold_tokens(): pl.pallas_call(kernel, out_shape=pltpu.VMEM((NZ, ROWS, DEPTH), jnp.bfloat...  8.24 us
    ppermute x5, waiting for transfers between devices, down(): return lax.ppermute(array, ('z', 'c'), DOWN)  7.32 us
    ppermute x5, starting transfers between devices, across(): return lax.ppermute(array, 'xh', SWAP)  7.28 us
    pallas_call x2, Pallas kernels, project_late(): pl.pallas_call(kernel, out_shape=(shape, weight_shape) if first else shap...  5.79 us
    pallas_call x1, Pallas kernels, attend(): pl.pallas_call(kernel, out_shape=jax.ShapeDtypeStruct((ROWS, 8 * HEAD), j...  5.38 us
  transfers between devices with their start and end apart: 19, of which 11 were waited for; matrix products, arithmetic and copies ran while one was open for 4% of the time, Pallas kernels for 29%

profile of v3, /device:TPU:1, one launch (start us, length us, event | category | flops | bytes accessed | tf_op | source)
XLA Modules:
  0.0 97.1 jit_solution(4554047780447077226)
XLA Ops:
  0.0 3.2 %collective-permute-start.2 = (bf16[768,5120]{1,0:T(8,128)(2,1)}, bf16[768,5120]{1,0:T(8,128)(2,1)}, u32[]{:S(2)}, u32[]{:S(2)}) collective-permute-start(bf16[768,5120]{1,0:T(8,128)(2,1)} %token_ref.1), channel_id=1, source_target_pairs={{0,8},{8,0},{1,9},{9,1},{2,10},{10,2},{3,11},{11,3},{4,12},{12,4},... | collective-permute-start | bytes 23592968 | tf_op jit(solution)/shard_map/ppermute | solution.py:318
  3.2 1.0 %copy-done.1 = bf16[20,10240]{1,0:T(8,128)(2,1)S(1)} copy-done((bf16[20,10240]{1,0:T(8,128)(2,1)S(1)}, bf16[20,10240]{1,0:T(8,128)(2,1)}, u32[]{:S(2)}) %copy-start.1) | copy-done | bytes 409624
  5.1 4.2 %all-to-all-start = ((bf16[16,20,640]{2,1,0:T(8,128)(2,1)}), bf16[16,20,640]{2,1,0:T(8,128)(2,1)S(1)}, u32[]{:S(2)}, u32[]{:S(2)}) async-start(bf16[16,20,640]{2,1,0:T(8,128)(2,1)} %regroup.1), calls=%async_computation | async-start | bytes 983040 | tf_op jit(solution)/shard_map/all_to_all | solution.py:321
  9.5 3.9 %hold_tokens.2.refs_2_.refs_4_.refs_1_ = bf16[8,768,640]{2,1,0:T(8,128)(2,1)S(1)} custom-call(s32[3]{0:T(128)S(1)} %pad_add_fusion.place_ref, bf16[768,5120]{1,0:T(8,128)(2,1)} %token_ref.1), custom_call_target="tpu_custom_call" | custom-call | bytes 16777216 | tf_op jit(solution)/shard_map/hold_tokens/pallas_call | solution.py:158
  13.5 3.1 %copy-done = bf16[8,768,640]{2,1,0:T(8,128)(2,1)} copy-done((bf16[8,768,640]{2,1,0:T(8,128)(2,1)}, bf16[8,768,640]{2,1,0:T(8,128)(2,1)S(1)}, u32[]{:S(2)}) %copy-start) | copy-done | bytes 7864344
  17.0 1.2 %all-to-all-done = bf16[16,20,640]{2,1,0:T(8,128)(2,1)S(1)} async-done(((bf16[16,20,640]{2,1,0:T(8,128)(2,1)}), bf16[16,20,640]{2,1,0:T(8,128)(2,1)S(1)}, u32[]{:S(2)}, u32[]{:S(2)}) %all-to-all-start) | async-done | bytes 409632 | tf_op jit(solution)/shard_map/all_to_all | solution.py:321
  18.4 5.7 %collective-permute-start = (bf16[320,640]{1,0:T(8,128)(2,1)S(1)}, bf16[320,640]{1,0:T(8,128)(2,1)S(1)}, u32[]{:S(2)}, u32[]{:S(2)}) collective-permute-start(bf16[320,640]{1,0:T(8,128)(2,1)S(1)} %reshape.42.refs_0_), channel_id=1, source_target_pairs={{0,32},{8,232},{32,64},{40,8},{64,96},{72,40},{96,128},{104,72},{1... | collective-permute-start | bytes 1228808 | tf_op jit(solution)/shard_map/ppermute | solution.py:75
  24.0 2.8 %fusion.1 = (f32[768,64]{1,0:T(8,128)S(1)}, f32[768,64]{1,0:T(8,128)S(1)}, f32[768,64]{1,0:T(8,128)S(1)}, f32[768,64]{1,0:T(8,128)S(1)}, f32[768,64]{1,0:T(8,128)S(1)}, /*index=5*/f32[768,64]{1,0:T(8,128)S(1)}) fusion(f32[64]{0:T(128)S(1)} %multiply_power_fusion, f32[768]{0:T(1024)S(1)} %subtract_convert_fusion, f32[768]{0:T(1024)S(1)} %subtract_convert_fusion.1), kind=kLoop, calls=%fused_computation.9 | loop fusion | flops 196608 | bytes 1186048 | tf_op jit(solution)/shard_map/neg | solution.py:48
  26.8 2.5 %collective-permute-start.6 = (bf16[320,640]{1,0:T(8,128)(2,1)S(1)}, bf16[320,640]{1,0:T(8,128)(2,1)S(1)}, u32[]{:S(2)}, u32[]{:S(2)}) collective-permute-start(bf16[320,640]{1,0:T(8,128)(2,1)S(1)} %reshape.42.refs_0_), channel_id=1, source_target_pairs={{0,16},{16,0},{1,17},{17,1},{2,18},{18,2},{3,19},{19,3},{4,20},{20... | collective-permute-start | bytes 1228808 | tf_op jit(solution)/shard_map/ppermute | solution.py:81
  29.9 4.3 %hold_tokens.3.refs_3_.refs_5_.refs_2_ = bf16[8,768,640]{2,1,0:T(8,128)(2,1)S(1)} custom-call(s32[3]{0:T(128)S(1)} %pad_add_fusion.place_ref, bf16[768,5120]{1,0:T(8,128)(2,1)} %collective-permute-done.2.token_ref), custom_call_target="tpu_custom_call" | custom-call | bytes 16777216 | tf_op jit(solution)/shard_map/hold_tokens/pallas_call | solution.py:158
  34.3 1.0 %collective-permute-done.1.refs_2_ = bf16[320,640]{1,0:T(8,128)(2,1)S(1)} collective-permute-done((bf16[320,640]{1,0:T(8,128)(2,1)S(1)}, bf16[320,640]{1,0:T(8,128)(2,1)S(1)}, u32[]{:S(2)}, u32[]{:S(2)}) %collective-permute-start.1) | collective-permute-done | bytes 409632 | tf_op jit(solution)/shard_map/ppermute | solution.py:78
  35.3 1.8 %collective-permute-start.4 = (bf16[320,640]{1,0:T(8,128)(2,1)S(1)}, bf16[320,640]{1,0:T(8,128)(2,1)S(1)}, u32[]{:S(2)}, u32[]{:S(2)}) collective-permute-start(bf16[320,640]{1,0:T(8,128)(2,1)S(1)} %collective-permute-done.refs_0_), channel_id=1, source_target_pairs={{0,32},{8,232},{32,64},{40,8},{64,96},{72,40},{96,128},{104,72},{1... | collective-permute-start | bytes 1228808 | tf_op jit(solution)/shard_map/ppermute | solution.py:75
  37.9 2.5 %collective-permute-start.9 = (bf16[320,640]{1,0:T(8,128)(2,1)S(1)}, bf16[320,640]{1,0:T(8,128)(2,1)S(1)}, u32[]{:S(2)}, u32[]{:S(2)}) collective-permute-start(bf16[320,640]{1,0:T(8,128)(2,1)S(1)} %collective-permute-done.refs_0_), channel_id=1, source_target_pairs={{0,16},{16,0},{1,17},{17,1},{2,18},{18,2},{3,19},{19,3},{4,20},{20... | collective-permute-start | bytes 1228808 | tf_op jit(solution)/shard_map/ppermute | solution.py:81
  40.4 2.5 %project_early.4 = (f32[768,640]{1,0:T(8,128)S(1)}, f32[768,640]{1,0:T(8,128)S(1)}) custom-call(s32[3]{0:T(128)S(1)} %pad_add_fusion.place_ref, bf16[320,640]{1,0:T(8,128)(2,1)S(1)} %reshape.42.refs_0_, bf16[320,640]{1,0:T(8,128)(2,1)S(1)} %collective-permute-done.6.refs_1_, bf16[8,768,640]{2,1,0:T(8,128)(2,1)S(1)} %bitcast.10, ...), custom_call_target="tpu_custom_call" | custom-call | flops 1258291200 | bytes 18874368 | tf_op jit(solution)/shard_map/project_early/pallas_call | solution.py:193
  42.9 2.4 %collective-permute-done.4.refs_0_ = bf16[320,640]{1,0:T(8,128)(2,1)S(1)} collective-permute-done((bf16[320,640]{1,0:T(8,128)(2,1)S(1)}, bf16[320,640]{1,0:T(8,128)(2,1)S(1)}, u32[]{:S(2)}, u32[]{:S(2)}) %collective-permute-start.4) | collective-permute-done | bytes 409632 | tf_op jit(solution)/shard_map/ppermute | solution.py:75
  45.4 3.9 %collective-permute-done.5.refs_2_ = bf16[320,640]{1,0:T(8,128)(2,1)S(1)} collective-permute-done((bf16[320,640]{1,0:T(8,128)(2,1)S(1)}, bf16[320,640]{1,0:T(8,128)(2,1)S(1)}, u32[]{:S(2)}, u32[]{:S(2)}) %collective-permute-start.5) | collective-permute-done | bytes 409632 | tf_op jit(solution)/shard_map/ppermute | solution.py:78
  49.2 1.5 %collective-permute-start.8 = (bf16[320,640]{1,0:T(8,128)(2,1)S(1)}, bf16[320,640]{1,0:T(8,128)(2,1)S(1)}, u32[]{:S(2)}, u32[]{:S(2)}) collective-permute-start(bf16[320,640]{1,0:T(8,128)(2,1)S(1)} %collective-permute-done.5.refs_2_), channel_id=1, source_target_pairs={{32,0},{232,8},{64,32},{8,40},{96,64},{40,72},{128,96},{72,104},{1... | collective-permute-start | bytes 1228808 | tf_op jit(solution)/shard_map/ppermute | solution.py:78
  51.1 1.8 %collective-permute-start.12 = (bf16[320,640]{1,0:T(8,128)(2,1)S(1)}, bf16[320,640]{1,0:T(8,128)(2,1)S(1)}, u32[]{:S(2)}, u32[]{:S(2)}) collective-permute-start(bf16[320,640]{1,0:T(8,128)(2,1)S(1)} %collective-permute-done.9.refs_1_), channel_id=1, source_target_pairs={{0,32},{8,232},{32,64},{40,8},{64,96},{72,40},{96,128},{104,72},{1... | collective-permute-start | bytes 1228808 | tf_op jit(solution)/shard_map/ppermute | solution.py:75
  53.3 4.6 %project_early.5 = (f32[768,640]{1,0:T(8,128)S(1)}, f32[768,640]{1,0:T(8,128)S(1)}) custom-call(s32[3]{0:T(128)S(1)} %pad_add_fusion.place_ref, bf16[320,640]{1,0:T(8,128)(2,1)S(1)} %collective-permute-done.refs_0_, bf16[320,640]{1,0:T(8,128)(2,1)S(1)} %collective-permute-done.9.refs_1_, ...), custom_call_target="tpu_custom_call", output_to_operand_aliasing={{0}: (7, {}), {1}: (8, {})} | custom-call | flops 2516582400 | bytes 18874368 | tf_op jit(solution)/shard_map/project_early/pallas_call | solution.py:193
  57.9 2.5 %collective-permute-done.7.refs_0_ = bf16[320,640]{1,0:T(8,128)(2,1)S(1)} collective-permute-done((bf16[320,640]{1,0:T(8,128)(2,1)S(1)}, bf16[320,640]{1,0:T(8,128)(2,1)S(1)}, u32[]{:S(2)}, u32[]{:S(2)}) %collective-permute-start.7) | collective-permute-done | bytes 409632 | tf_op jit(solution)/shard_map/ppermute | solution.py:75
  60.4 2.0 %collective-permute-done.8.refs_2_ = bf16[320,640]{1,0:T(8,128)(2,1)S(1)} collective-permute-done((bf16[320,640]{1,0:T(8,128)(2,1)S(1)}, bf16[320,640]{1,0:T(8,128)(2,1)S(1)}, u32[]{:S(2)}, u32[]{:S(2)}) %collective-permute-start.8) | collective-permute-done | bytes 409632 | tf_op jit(solution)/shard_map/ppermute | solution.py:78
  63.3 1.9 %collective-permute-done.12.refs_1_ = bf16[320,640]{1,0:T(8,128)(2,1)S(1)} collective-permute-done((bf16[320,640]{1,0:T(8,128)(2,1)S(1)}, bf16[320,640]{1,0:T(8,128)(2,1)S(1)}, u32[]{:S(2)}, u32[]{:S(2)}) %collective-permute-start.12) | collective-permute-done | bytes 409632 | tf_op jit(solution)/shard_map/ppermute | solution.py:75
  65.1 2.2 %collective-permute-start.15 = (bf16[320,640]{1,0:T(8,128)(2,1)S(1)}, bf16[320,640]{1,0:T(8,128)(2,1)S(1)}, u32[]{:S(2)}, u32[]{:S(2)}) collective-permute-start(bf16[320,640]{1,0:T(8,128)(2,1)S(1)} %collective-permute-done.12.refs_1_), channel_id=1, source_target_pairs={{0,32},{8,232},{32,64},{40,8},{64,96},{72,40},{96,128},{104,72},{1... | collective-permute-start | bytes 1228808 | tf_op jit(solution)/shard_map/ppermute | solution.py:75
  67.3 4.6 %project_early.6 = (f32[768,640]{1,0:T(8,128)S(1)}, f32[768,640]{1,0:T(8,128)S(1)}) custom-call(s32[3]{0:T(128)S(1)} %pad_add_fusion.place_ref, bf16[320,640]{1,0:T(8,128)(2,1)S(1)} %collective-permute-done.4.refs_0_, bf16[320,640]{1,0:T(8,128)(2,1)S(1)} %collective-permute-done.12.refs_1_, ...), custom_call_target="tpu_custom_call", output_to_operand_aliasing={{0}: (7, {}), {1}: (8, {})} | custom-call | flops 2516582400 | bytes 18874368 | tf_op jit(solution)/shard_map/project_early/pallas_call | solution.py:193
  72.0 1.0 %collective-permute-start.14 = (bf16[320,640]{1,0:T(8,128)(2,1)S(1)}, bf16[320,640]{1,0:T(8,128)(2,1)S(1)}, u32[]{:S(2)}, u32[]{:S(2)}) collective-permute-start(bf16[320,640]{1,0:T(8,128)(2,1)S(1)} %collective-permute-done.11.refs_0_), channel_id=1, source_target_pairs={{0,16},{16,0},{1,17},{17,1},{2,18},{18,2},{3,19},{19,3},{4,20},{20... | collective-permute-start | bytes 1228808 | tf_op jit(solution)/shard_map/ppermute | solution.py:81
  73.0 2.6 %collective-permute-done.15.refs_1_ = bf16[320,640]{1,0:T(8,128)(2,1)S(1)} collective-permute-done((bf16[320,640]{1,0:T(8,128)(2,1)S(1)}, bf16[320,640]{1,0:T(8,128)(2,1)S(1)}, u32[]{:S(2)}, u32[]{:S(2)}) %collective-permute-start.15) | collective-permute-done | bytes 409632 | tf_op jit(solution)/shard_map/ppermute | solution.py:75
  75.5 4.6 %project_early.7 = (f32[768,640]{1,0:T(8,128)S(1)}, f32[768,640]{1,0:T(8,128)S(1)}) custom-call(s32[3]{0:T(128)S(1)} %pad_add_fusion.place_ref, bf16[320,640]{1,0:T(8,128)(2,1)S(1)} %collective-permute-done.7.refs_0_, bf16[320,640]{1,0:T(8,128)(2,1)S(1)} %collective-permute-done.15.refs_1_, ...), custom_call_target="tpu_custom_call", output_to_operand_aliasing={{0}: (7, {}), {1}: (8, {})} | custom-call | flops 2516582400 | bytes 18874368 | tf_op jit(solution)/shard_map/project_early/pallas_call | solution.py:193
  80.1 2.0 %collective-permute-done.14.refs_1_ = bf16[320,640]{1,0:T(8,128)(2,1)S(1)} collective-permute-done((bf16[320,640]{1,0:T(8,128)(2,1)S(1)}, bf16[320,640]{1,0:T(8,128)(2,1)S(1)}, u32[]{:S(2)}, u32[]{:S(2)}) %collective-permute-start.14) | collective-permute-done | bytes 409632 | tf_op jit(solution)/shard_map/ppermute | solution.py:81
  82.2 2.9 %project_late.2 = (bf16[768,640]{1,0:T(8,128)(2,1)S(1)}, bf16[640,640]{1,0:T(8,128)(2,1)S(1)}) custom-call(s32[3]{0:T(128)S(1)} %pad_add_fusion.place_ref, bf16[320,640]{1,0:T(8,128)(2,1)S(1)} %collective-permute-done.11.refs_0_, bf16[320,640]{1,0:T(8,128)(2,1)S(1)} %collective-permute-done.14.refs_1_, ...), custom_call_target="tpu_custom_call" | custom-call | flops 629145600 | bytes 9437184 | tf_op jit(solution)/shard_map/project_late/pallas_call | solution.py:245
  85.1 3.6 %collective-permute-start.17 = (bf16[768,640]{1,0:T(8,128)(2,1)S(1)}, bf16[768,640]{1,0:T(8,128)(2,1)S(1)}, u32[]{:S(2)}, u32[]{:S(2)}) collective-permute-start(bf16[768,640]{1,0:T(8,128)(2,1)S(1)} %get-tuple-element.66), channel_id=1, source_target_pairs={{0,8},{8,0},{1,9},{9,1},{2,10},{10,2},{3,11},{11,3},{4,12},{12,4},... | collective-permute-start | bytes 2949128 | tf_op jit(solution)/shard_map/ppermute | solution.py:334
  88.8 2.9 %project_late.3.own_ref = bf16[768,640]{1,0:T(8,128)(2,1)S(1)} custom-call(s32[3]{0:T(128)S(1)} %pad_add_fusion.place_ref, bf16[640,640]{1,0:T(8,128)(2,1)S(1)} %get-tuple-element.62.refs_0_, bf16[8,768,640]{2,1,0:T(8,128)(2,1)S(1)} %bitcast.10, f32[768,640]{1,0:T(8,128)S(1)} %get-tuple-element.63.refs_2_, f32[768,128]{1,0:T(8,128)S(1)} %get-tuple-element.64.refs_3_, ...), custom_call_target="tpu_custom_call" | custom-call | flops 629145600 | bytes 9437184 | tf_op jit(solution)/shard_map/project_late/pallas_call | solution.py:245
  91.7 5.4 %attend.1 = bf16[768,1024]{1,0:T(8,128)(2,1)} custom-call(s32[3]{0:T(128)S(1)} %pad_add_fusion.place_ref, bf16[768,640]{1,0:T(8,128)(2,1)S(1)} %project_late.3.own_ref, bf16[768,640]{1,0:T(8,128)(2,1)S(1)} %collective-permute-done.17.received_ref, s32[768,1]{1,0:T(8,128)S(1)} %reduce_max.23.start_ref), custom_call_target="tpu_custom_call" | custom-call | flops 1610612736 | bytes 4194304 | tf_op jit(solution)/shard_map/attend/pallas_call | solution.py:297
  (46 shorter events, 4.9 us)
Async XLA Ops:
  0.0 29.9 %collective-permute-start.2 = (bf16[768,5120]{1,0:T(8,128)(2,1)}, bf16[768,5120]{1,0:T(8,128)(2,1)}, u32[]{:S(2)}, u32[]{:S(2)}) collective-permute-start(bf16[768,5120]{1,0:T(8,128)(2,1)} %token_ref.1), channel_id=1, source_target_pairs={{0,8},{8,0},{1,9},{9,1},{2,10},{10,2},{3,11},{11,3},{4,12},{12,4},... | collective-permute-start | bytes 23592968 | tf_op jit(solution)/shard_map/ppermute | solution.py:318
  3.2 13.5 %collective-permute-start.3 = (s32[1,8]{1,0:T(1,128)}, s32[1,8]{1,0:T(1,128)S(1)}, u32[]{:S(2)}, u32[]{:S(2)}) collective-permute-start(s32[1,8]{1,0:T(1,128)} %param.6), channel_id=1, source_target_pairs={{0,8},{8,0},{1,9},{9,1},{2,10},{10,2},{3,11},{11,3},{4,12},{12,4},... | collective-permute-start | bytes 104 | tf_op jit(solution)/shard_map/ppermute | solution.py:319
  3.2 1.0 %copy-start.1 = (bf16[20,10240]{1,0:T(8,128)(2,1)S(1)}, bf16[20,10240]{1,0:T(8,128)(2,1)}, u32[]{:S(2)}) copy-start(bf16[20,10240]{1,0:T(8,128)(2,1)} %weight_ref.1) | copy-start | bytes 1228804
  4.3 5.0 %copy-start.4 = (s32[1,8]{1,0:T(1,128)S(1)}, s32[1,8]{1,0:T(1,128)}, u32[]{:S(2)}) copy-start(s32[1,8]{1,0:T(1,128)} %param.6) | copy-start | bytes 100
  5.1 13.2 %all-to-all-start = ((bf16[16,20,640]{2,1,0:T(8,128)(2,1)}), bf16[16,20,640]{2,1,0:T(8,128)(2,1)S(1)}, u32[]{:S(2)}, u32[]{:S(2)}) async-start(bf16[16,20,640]{2,1,0:T(8,128)(2,1)} %regroup.1), calls=%async_computation | async-start | bytes 983040 | tf_op jit(solution)/shard_map/all_to_all | solution.py:321
  13.5 3.1 %copy-start = (bf16[8,768,640]{2,1,0:T(8,128)(2,1)}, bf16[8,768,640]{2,1,0:T(8,128)(2,1)S(1)}, u32[]{:S(2)}) copy-start(bf16[8,768,640]{2,1,0:T(8,128)(2,1)S(1)} %hold_tokens.2.refs_2_.refs_4_.refs_1_) | copy-start | bytes 23592964
  18.4 15.9 %collective-permute-start = (bf16[320,640]{1,0:T(8,128)(2,1)S(1)}, bf16[320,640]{1,0:T(8,128)(2,1)S(1)}, u32[]{:S(2)}, u32[]{:S(2)}) collective-permute-start(bf16[320,640]{1,0:T(8,128)(2,1)S(1)} %reshape.42.refs_0_), channel_id=1, source_target_pairs={{0,32},{8,232},{32,64},{40,8},{64,96},{72,40},{96,128},{104,72},{1... | collective-permute-start | bytes 1228808 | tf_op jit(solution)/shard_map/ppermute | solution.py:75
  24.0 11.3 %collective-permute-start.1 = (bf16[320,640]{1,0:T(8,128)(2,1)S(1)}, bf16[320,640]{1,0:T(8,128)(2,1)S(1)}, u32[]{:S(2)}, u32[]{:S(2)}) collective-permute-start(bf16[320,640]{1,0:T(8,128)(2,1)S(1)} %reshape.42.refs_0_), channel_id=1, source_target_pairs={{32,0},{232,8},{64,32},{8,40},{96,64},{40,72},{128,96},{72,104},{1... | collective-permute-start | bytes 1228808 | tf_op jit(solution)/shard_map/ppermute | solution.py:78
  26.8 11.1 %collective-permute-start.6 = (bf16[320,640]{1,0:T(8,128)(2,1)S(1)}, bf16[320,640]{1,0:T(8,128)(2,1)S(1)}, u32[]{:S(2)}, u32[]{:S(2)}) collective-permute-start(bf16[320,640]{1,0:T(8,128)(2,1)S(1)} %reshape.42.refs_0_), channel_id=1, source_target_pairs={{0,16},{16,0},{1,17},{17,1},{2,18},{18,2},{3,19},{19,3},{4,20},{20... | collective-permute-start | bytes 1228808 | tf_op jit(solution)/shard_map/ppermute | solution.py:81
  29.6 10.8 %slice-start = ((s8[7864320]{0:T(1024)(128)(4,1)}), s8[4194304]{0:T(1024)(128)(4,1)S(1)}, s32[]{:S(2)}) async-start(s8[7864320]{0:T(1024)(128)(4,1)} %bitcast.9), calls=%async_computation.1 | async-start | bytes 8388608
  29.9 10.5 %slice-start.1 = ((s8[7864320]{0:T(1024)(128)(4,1)}), s8[3670016]{0:T(1024)(128)(4,1)S(1)}, s32[]{:S(2)}) async-start(s8[7864320]{0:T(1024)(128)(4,1)} %bitcast.9), calls=%async_computation.2 | async-start | bytes 7340032
  35.3 10.1 %collective-permute-start.4 = (bf16[320,640]{1,0:T(8,128)(2,1)S(1)}, bf16[320,640]{1,0:T(8,128)(2,1)S(1)}, u32[]{:S(2)}, u32[]{:S(2)}) collective-permute-start(bf16[320,640]{1,0:T(8,128)(2,1)S(1)} %collective-permute-done.refs_0_), channel_id=1, source_target_pairs={{0,32},{8,232},{32,64},{40,8},{64,96},{72,40},{96,128},{104,72},{1... | collective-permute-start | bytes 1228808 | tf_op jit(solution)/shard_map/ppermute | solution.py:75
  37.0 12.2 %collective-permute-start.5 = (bf16[320,640]{1,0:T(8,128)(2,1)S(1)}, bf16[320,640]{1,0:T(8,128)(2,1)S(1)}, u32[]{:S(2)}, u32[]{:S(2)}) collective-permute-start(bf16[320,640]{1,0:T(8,128)(2,1)S(1)} %collective-permute-done.1.refs_2_), channel_id=1, source_target_pairs={{32,0},{232,8},{64,32},{8,40},{96,64},{40,72},{128,96},{72,104},{1... | collective-permute-start | bytes 1228808 | tf_op jit(solution)/shard_map/ppermute | solution.py:78
  37.9 13.2 %collective-permute-start.9 = (bf16[320,640]{1,0:T(8,128)(2,1)S(1)}, bf16[320,640]{1,0:T(8,128)(2,1)S(1)}, u32[]{:S(2)}, u32[]{:S(2)}) collective-permute-start(bf16[320,640]{1,0:T(8,128)(2,1)S(1)} %collective-permute-done.refs_0_), channel_id=1, source_target_pairs={{0,16},{16,0},{1,17},{17,1},{2,18},{18,2},{3,19},{19,3},{4,20},{20... | collective-permute-start | bytes 1228808 | tf_op jit(solution)/shard_map/ppermute | solution.py:81
  40.4 13.0 %collective-permute-start.10 = (bf16[320,640]{1,0:T(8,128)(2,1)S(1)}, bf16[320,640]{1,0:T(8,128)(2,1)S(1)}, u32[]{:S(2)}, u32[]{:S(2)}) collective-permute-start(bf16[320,640]{1,0:T(8,128)(2,1)S(1)} %collective-permute-done.6.refs_1_), channel_id=1, source_target_pairs={{32,0},{232,8},{64,32},{8,40},{96,64},{40,72},{128,96},{72,104},{1... | collective-permute-start | bytes 1228808 | tf_op jit(solution)/shard_map/ppermute | solution.py:78
  49.2 11.1 %collective-permute-start.7 = (bf16[320,640]{1,0:T(8,128)(2,1)S(1)}, bf16[320,640]{1,0:T(8,128)(2,1)S(1)}, u32[]{:S(2)}, u32[]{:S(2)}) collective-permute-start(bf16[320,640]{1,0:T(8,128)(2,1)S(1)} %collective-permute-done.4.refs_0_), channel_id=1, source_target_pairs={{0,32},{8,232},{32,64},{40,8},{64,96},{72,40},{96,128},{104,72},{1... | collective-permute-start | bytes 1228808 | tf_op jit(solution)/shard_map/ppermute | solution.py:75
  49.2 13.1 %collective-permute-start.8 = (bf16[320,640]{1,0:T(8,128)(2,1)S(1)}, bf16[320,640]{1,0:T(8,128)(2,1)S(1)}, u32[]{:S(2)}, u32[]{:S(2)}) collective-permute-start(bf16[320,640]{1,0:T(8,128)(2,1)S(1)} %collective-permute-done.5.refs_2_), channel_id=1, source_target_pairs={{32,0},{232,8},{64,32},{8,40},{96,64},{40,72},{128,96},{72,104},{1... | collective-permute-start | bytes 1228808 | tf_op jit(solution)/shard_map/ppermute | solution.py:78
  50.7 16.6 %collective-permute-start.13 = (bf16[320,640]{1,0:T(8,128)(2,1)S(1)}, bf16[320,640]{1,0:T(8,128)(2,1)S(1)}, u32[]{:S(2)}, u32[]{:S(2)}) collective-permute-start(bf16[320,640]{1,0:T(8,128)(2,1)S(1)} %collective-permute-done.5.refs_2_), channel_id=1, source_target_pairs={{0,16},{16,0},{1,17},{17,1},{2,18},{18,2},{3,19},{19,3},{4,20},{20... | collective-permute-start | bytes 1228808 | tf_op jit(solution)/shard_map/ppermute | solution.py:81
  51.1 14.0 %collective-permute-start.12 = (bf16[320,640]{1,0:T(8,128)(2,1)S(1)}, bf16[320,640]{1,0:T(8,128)(2,1)S(1)}, u32[]{:S(2)}, u32[]{:S(2)}) collective-permute-start(bf16[320,640]{1,0:T(8,128)(2,1)S(1)} %collective-permute-done.9.refs_1_), channel_id=1, source_target_pairs={{0,32},{8,232},{32,64},{40,8},{64,96},{72,40},{96,128},{104,72},{1... | collective-permute-start | bytes 1228808 | tf_op jit(solution)/shard_map/ppermute | solution.py:75
  62.4 9.6 %collective-permute-start.11 = (bf16[320,640]{1,0:T(8,128)(2,1)S(1)}, bf16[320,640]{1,0:T(8,128)(2,1)S(1)}, u32[]{:S(2)}, u32[]{:S(2)}) collective-permute-start(bf16[320,640]{1,0:T(8,128)(2,1)S(1)} %collective-permute-done.8.refs_2_), channel_id=1, source_target_pairs={{32,0},{232,8},{64,32},{8,40},{96,64},{40,72},{128,96},{72,104},{1... | collective-permute-start | bytes 1228808 | tf_op jit(solution)/shard_map/ppermute | solution.py:78
  62.4 10.6 %collective-permute-start.16 = (bf16[320,640]{1,0:T(8,128)(2,1)S(1)}, bf16[320,640]{1,0:T(8,128)(2,1)S(1)}, u32[]{:S(2)}, u32[]{:S(2)}) collective-permute-start(bf16[320,640]{1,0:T(8,128)(2,1)S(1)} %collective-permute-done.8.refs_2_), channel_id=1, source_target_pairs={{0,16},{16,0},{1,17},{17,1},{2,18},{18,2},{3,19},{19,3},{4,20},{20... | collective-permute-start | bytes 1228808 | tf_op jit(solution)/shard_map/ppermute | solution.py:81
  65.1 10.4 %collective-permute-start.15 = (bf16[320,640]{1,0:T(8,128)(2,1)S(1)}, bf16[320,640]{1,0:T(8,128)(2,1)S(1)}, u32[]{:S(2)}, u32[]{:S(2)}) collective-permute-start(bf16[320,640]{1,0:T(8,128)(2,1)S(1)} %collective-permute-done.12.refs_1_), channel_id=1, source_target_pairs={{0,32},{8,232},{32,64},{40,8},{64,96},{72,40},{96,128},{104,72},{1... | collective-permute-start | bytes 1228808 | tf_op jit(solution)/shard_map/ppermute | solution.py:75
  71.9 10.2 %copy-start.2 = (f32[128]{0:T(128)S(1)}, f32[128]{0:T(128)}, u32[]{:S(2)}) copy-start(f32[128]{0:T(128)} %param.8) | copy-start | bytes 1540
  72.0 10.2 %copy-start.3 = (f32[128]{0:T(128)S(1)}, f32[128]{0:T(128)}, u32[]{:S(2)}) copy-start(f32[128]{0:T(128)} %param.9) | copy-start | bytes 1540
  72.0 10.2 %collective-permute-start.14 = (bf16[320,640]{1,0:T(8,128)(2,1)S(1)}, bf16[320,640]{1,0:T(8,128)(2,1)S(1)}, u32[]{:S(2)}, u32[]{:S(2)}) collective-permute-start(bf16[320,640]{1,0:T(8,128)(2,1)S(1)} %collective-permute-done.11.refs_0_), channel_id=1, source_target_pairs={{0,16},{16,0},{1,17},{17,1},{2,18},{18,2},{3,19},{19,3},{4,20},{20... | collective-permute-start | bytes 1228808 | tf_op jit(solution)/shard_map/ppermute | solution.py:81
  85.1 6.6 %collective-permute-start.17 = (bf16[768,640]{1,0:T(8,128)(2,1)S(1)}, bf16[768,640]{1,0:T(8,128)(2,1)S(1)}, u32[]{:S(2)}, u32[]{:S(2)}) collective-permute-start(bf16[768,640]{1,0:T(8,128)(2,1)S(1)} %get-tuple-element.66), channel_id=1, source_target_pairs={{0,8},{8,0},{1,9},{9,1},{2,10},{10,2},{3,11},{11,3},{4,12},{12,4},... | collective-permute-start | bytes 2949128 | tf_op jit(solution)/shard_map/ppermute | solution.py:334

commit v4 on v3

--- a/solution.py
+++ b/solution.py
@@ -105,8 +105,8 @@
         (up2, -2, 0, 0), (other_up2, -2, 1, 0), (down2, 2, 0, 0), (other_down2, 2, 1, 0),
     ]
     totals = project_early(place, second, held, totals)
-    down4, totals = lax.optimization_barrier((down4, totals))
-    other_down4 = across(down4)
+    other_down3, totals = lax.optimization_barrier((other_down3, totals))
+    other_down4 = down(other_down3)
     third = [
         (up3, -3, 0, 0), (other_up3, -3, 1, 0), (down3, 3, 0, 0), (other_down3, 3, 1, 0),
     ]
@@ -174,20 +174,16 @@
     def kernel(place_ref, *refs):
         sources, held_refs = refs[: len(pieces)], refs[len(pieces) : len(pieces) + 2]
         total_refs, out_refs, weight = refs[len(pieces) + 2 : -3], refs[-3:-1], refs[-1]
-        for slot, offset in enumerate(offsets):
+        for slot in range(count):
             assemble(place_ref, pieces, sources, weight, slot)
-            for which, (held_ref, out_ref) in enumerate(zip(held_refs, out_refs)):
-                product = jnp.dot(
-                    held_ref[slot_of(offset)],
-                    weight[slot * DEPTH : (slot + 1) * DEPTH],
-                    preferred_element_type=jnp.float32,
+        for which, (held_ref, out_ref) in enumerate(zip(held_refs, out_refs)):
+            for tile in range(TILES):
+                rows = pl.ds(tile * TILE, TILE)
+                part = jnp.concatenate(
+                    [held_ref[slot_of(offset), rows] for offset in offsets], axis=1
                 )
-                if slot:
-                    out_ref[...] += product
-                elif total_refs:
-                    out_ref[...] = total_refs[which][...] + product
-                else:
-                    out_ref[...] = product
+                product = jnp.dot(part, weight[...], preferred_element_type=jnp.float32)
+                out_ref[rows] = total_refs[which][rows] + product if total_refs else product
 
     shape = pltpu.VMEM((ROWS, COLS), jnp.float32)
     return pl.pallas_call(
@@ -261,8 +257,13 @@
 def attend(place, own, received, request_start):
     scale = math.log2(math.e) / math.sqrt(HEAD)
 
-    def kernel(place_ref, own_ref, received_ref, start_ref, out_ref, key_ref, value_ref):
+    def kernel(place_ref, own_ref, received_ref, start_ref, out_hbm, key_ref, value_ref, out_ref, sems):
         core = place_ref[2]
+
+        def written(block):
+            rows = pl.ds(block * QBLOCK, QBLOCK)
+            return pltpu.make_async_copy(out_ref.at[rows], out_hbm.at[rows], sems.at[block])
+
         key_ref[...] = jnp.where(core == 0, own_ref[:, :HEAD], received_ref[:, :HEAD])
         value_ref[:, :HEAD] = jnp.where(core == 0, received_ref[:, :HEAD], own_ref[:, :HEAD])
         value_ref[:, HEAD:] = jnp.ones((ROWS, HEAD), jnp.bfloat16)
@@ -293,15 +294,20 @@
                     out_ref[rows, pl.ds(first + head * HEAD, HEAD)] = mixed[
                         head * QBLOCK : (head + 1) * QBLOCK
                     ]
+            written(block).start()
+        for block in range(ROWS // QBLOCK):
+            written(block).wait()
 
     return pl.pallas_call(
         kernel,
         out_shape=jax.ShapeDtypeStruct((ROWS, 8 * HEAD), jnp.bfloat16),
         in_specs=[SMEM, VMEM, VMEM, VMEM],
-        out_specs=VMEM,
+        out_specs=ANYWHERE,
         scratch_shapes=[
             pltpu.VMEM((ROWS, HEAD), jnp.bfloat16),
             pltpu.VMEM((ROWS, 2 * HEAD), jnp.bfloat16),
+            pltpu.VMEM((ROWS, HEADS * HEAD), jnp.bfloat16),
+            pltpu.SemaphoreType.DMA((ROWS // QBLOCK,)),
         ],
         compiler_params=pltpu.CompilerParams(vmem_limit_bytes=32 << 20),
         cost_estimate=pl.CostEstimate(
@@ -321,6 +327,7 @@
     block = lax.all_to_all(spread, ("c",) + TENSOR, split_axis=0, concat_axis=0, tiled=True)
     own_start, other_start = request_starts(lengths[0]), request_starts(other_lengths[0])
     own_tables, other_tables = rotary_tables(own_start), rotary_tables(other_start)
+    block, own_tables, other_tables = lax.optimization_barrier((block, own_tables, other_tables))
     held = hold_tokens(place, tokens)
     other_held = hold_tokens(place, other_tokens)
     late, totals, ahead = gather_blocks(

time: 97.3 us -> 95.3 us (0.979)
  waiting for transfers between devices: 20.8 us -> 28.2 us
  starting transfers between devices: 31.1 us -> 26.6 us
  local copies, waits for them, and re-layouts: 4.41 us -> 1.28 us
  Pallas kernels: 36.5 us -> 34.7 us
    all_to_all x1, waiting for transfers between devices: 1.24 us -> 5 us  [shards(): lax.all_to_all(spread, ('c',) + TENSOR, split_axis=0, concat_axis=0, tile...]
    unnamed x14 -> x8, local copies, waits for them, and re-layouts: 4.17 us -> 1.04 us
    ppermute x5 -> x6, waiting for transfers between devices: 7.32 us -> 10.2 us  [down(): return lax.ppermute(array, ('z', 'c'), DOWN)]
    ppermute x1, starting transfers between devices: 3.55 us -> 1.29 us  [shards(): received = lax.ppermute(other, 'c', SWAP)]
    ppermute x5 -> x4, starting transfers between devices: 7.28 us -> 5.45 us  [across(): return lax.ppermute(array, 'xh', SWAP)]
    pallas_call x4, Pallas kernels: 16.3 us -> 15.3 us  [project_early(): pl.pallas_call(kernel, out_shape=(shape, shape), in_specs=[SMEM] + [VMEM]...]
    ppermute x5 -> x4, waiting for transfers between devices: 2.94 us -> 3.23 us  [across(): return lax.ppermute(array, 'xh', SWAP)]
  transfers between devices with their start and end apart: 19 -> 19, of which waited for: 11 -> 11; matrix products, arithmetic and copies ran while one was open for 4% -> 4% of each run, Pallas kernels for 29% -> 28%
where the time goes in v4:
time: 95.3 us; the launch traced here: 95 us
  Pallas kernels  34.7 us (36%)
  waiting for transfers between devices  28.2 us (30%)
  starting transfers between devices  26.6 us (28%)
  other arithmetic  4 us (4%)
  local copies, waits for them, and re-layouts  1.28 us (1%)
    pallas_call x4, Pallas kernels, project_early(): pl.pallas_call(kernel, out_shape=(shape, shape), in_specs=[SMEM] + [VMEM]...  15.3 us
    ppermute x5, starting transfers between devices, up(): return lax.ppermute(array, ('z', 'c'), UP)  10.6 us
    ppermute x6, waiting for transfers between devices, down(): return lax.ppermute(array, ('z', 'c'), DOWN)  10.2 us
    ppermute x5, waiting for transfers between devices, up(): return lax.ppermute(array, ('z', 'c'), UP)  9.72 us
    pallas_call x2, Pallas kernels, hold_tokens(): pl.pallas_call(kernel, out_shape=pltpu.VMEM((NZ, ROWS, DEPTH), jnp.bfloat...  7.83 us
    pallas_call x2, Pallas kernels, project_late(): pl.pallas_call(kernel, out_shape=(shape, weight_shape) if first else shap...  5.79 us
    ppermute x4, starting transfers between devices, across(): return lax.ppermute(array, 'xh', SWAP)  5.45 us
    all_to_all x1, waiting for transfers between devices, shards(): lax.all_to_all(spread, ('c',) + TENSOR, split_axis=0, concat_axis=0, tile...  5 us
  transfers between devices with their start and end apart: 19, of which 11 were waited for; matrix products, arithmetic and copies ran while one was open for 4% of the time, Pallas kernels for 28%

profile of v4, /device:TPU:1, one launch (start us, length us, event | category | flops | bytes accessed | tf_op | source)
XLA Modules:
  0.0 95.0 jit_solution(17891212087607992684)
XLA Ops:
  0.0 3.2 %collective-permute-start.3 = (bf16[768,5120]{1,0:T(8,128)(2,1)}, bf16[768,5120]{1,0:T(8,128)(2,1)}, u32[]{:S(2)}, u32[]{:S(2)}) collective-permute-start(bf16[768,5120]{1,0:T(8,128)(2,1)} %token_ref.1), channel_id=1, source_target_pairs={{0,8},{8,0},{1,9},{9,1},{2,10},{10,2},{3,11},{11,3},{4,12},{12,4},... | collective-permute-start | bytes 23592968 | tf_op jit(solution)/shard_map/ppermute | solution.py:324
  3.2 1.0 %copy-done = bf16[20,10240]{1,0:T(8,128)(2,1)S(1)} copy-done((bf16[20,10240]{1,0:T(8,128)(2,1)S(1)}, bf16[20,10240]{1,0:T(8,128)(2,1)}, u32[]{:S(2)}) %copy-start) | copy-done | bytes 409624
  5.1 4.2 %all-to-all-start = ((bf16[16,20,640]{2,1,0:T(8,128)(2,1)}), bf16[16,20,640]{2,1,0:T(8,128)(2,1)S(1)}, u32[]{:S(2)}, u32[]{:S(2)}) async-start(bf16[16,20,640]{2,1,0:T(8,128)(2,1)} %regroup.1), calls=%async_computation | async-start | bytes 983040 | tf_op jit(solution)/shard_map/all_to_all | solution.py:327
  9.9 2.8 %fusion.1 = (f32[768,64]{1,0:T(8,128)S(1)}, f32[768,64]{1,0:T(8,128)S(1)}, f32[768,64]{1,0:T(8,128)S(1)}, f32[768,64]{1,0:T(8,128)S(1)}, f32[768,64]{1,0:T(8,128)S(1)}, /*index=5*/f32[768,64]{1,0:T(8,128)S(1)}) fusion(f32[64]{0:T(128)S(1)} %multiply_power_fusion, f32[768]{0:T(1024)S(1)} %subtract_convert_fusion, f32[768]{0:T(1024)S(1)} %subtract_convert_fusion.1), kind=kLoop, calls=%fused_computation.9 | loop fusion | flops 196608 | bytes 1186048 | tf_op jit(solution)/shard_map/neg | solution.py:48
  13.3 5.0 %all-to-all-done = bf16[16,20,640]{2,1,0:T(8,128)(2,1)S(1)} async-done(((bf16[16,20,640]{2,1,0:T(8,128)(2,1)}), bf16[16,20,640]{2,1,0:T(8,128)(2,1)S(1)}, u32[]{:S(2)}, u32[]{:S(2)}) %all-to-all-start) | async-done | bytes 409632 | tf_op jit(solution)/shard_map/all_to_all | solution.py:327
  18.4 5.7 %collective-permute-start.1 = (bf16[320,640]{1,0:T(8,128)(2,1)S(1)}, bf16[320,640]{1,0:T(8,128)(2,1)S(1)}, u32[]{:S(2)}, u32[]{:S(2)}) collective-permute-start(bf16[320,640]{1,0:T(8,128)(2,1)S(1)} %reshape.42.refs_0_), channel_id=1, source_target_pairs={{0,32},{8,232},{32,64},{40,8},{64,96},{72,40},{96,128},{104,72},{1... | collective-permute-start | bytes 1228808 | tf_op jit(solution)/shard_map/ppermute | solution.py:75
  24.0 2.5 %collective-permute-start.6 = (bf16[320,640]{1,0:T(8,128)(2,1)S(1)}, bf16[320,640]{1,0:T(8,128)(2,1)S(1)}, u32[]{:S(2)}, u32[]{:S(2)}) collective-permute-start(bf16[320,640]{1,0:T(8,128)(2,1)S(1)} %reshape.42.refs_0_), channel_id=1, source_target_pairs={{0,16},{16,0},{1,17},{17,1},{2,18},{18,2},{3,19},{19,3},{4,20},{20... | collective-permute-start | bytes 1228808 | tf_op jit(solution)/shard_map/ppermute | solution.py:81
  26.5 3.9 %hold_tokens.2.refs_2_.refs_4_.refs_1_ = bf16[8,768,640]{2,1,0:T(8,128)(2,1)S(1)} custom-call(s32[3]{0:T(128)S(1)} %pad_add_fusion.place_ref, bf16[768,5120]{1,0:T(8,128)(2,1)} %token_ref.1), custom_call_target="tpu_custom_call" | custom-call | bytes 16777216 | tf_op jit(solution)/shard_map/hold_tokens/pallas_call | solution.py:158
  30.5 3.9 %hold_tokens.3.refs_3_.refs_5_.refs_2_ = bf16[8,768,640]{2,1,0:T(8,128)(2,1)S(1)} custom-call(s32[3]{0:T(128)S(1)} %pad_add_fusion.place_ref, bf16[768,5120]{1,0:T(8,128)(2,1)} %collective-permute-done.3.token_ref), custom_call_target="tpu_custom_call" | custom-call | bytes 16777216 | tf_op jit(solution)/shard_map/hold_tokens/pallas_call | solution.py:158
  34.4 0.9 collective-permute-done.2.refs_2_
  35.3 1.9 %collective-permute-start.4 = (bf16[320,640]{1,0:T(8,128)(2,1)S(1)}, bf16[320,640]{1,0:T(8,128)(2,1)S(1)}, u32[]{:S(2)}, u32[]{:S(2)}) collective-permute-start(bf16[320,640]{1,0:T(8,128)(2,1)S(1)} %collective-permute-done.1.refs_0_), channel_id=1, source_target_pairs={{0,32},{8,232},{32,64},{40,8},{64,96},{72,40},{96,128},{104,72},{1... | collective-permute-start | bytes 1228808 | tf_op jit(solution)/shard_map/ppermute | solution.py:75
  37.2 1.9 %collective-permute-start.9 = (bf16[320,640]{1,0:T(8,128)(2,1)S(1)}, bf16[320,640]{1,0:T(8,128)(2,1)S(1)}, u32[]{:S(2)}, u32[]{:S(2)}) collective-permute-start(bf16[320,640]{1,0:T(8,128)(2,1)S(1)} %collective-permute-done.1.refs_0_), channel_id=1, source_target_pairs={{0,16},{16,0},{1,17},{17,1},{2,18},{18,2},{3,19},{19,3},{4,20},{20... | collective-permute-start | bytes 1228808 | tf_op jit(solution)/shard_map/ppermute | solution.py:81
  39.1 2.5 %project_early.4 = (f32[768,640]{1,0:T(8,128)S(1)}, f32[768,640]{1,0:T(8,128)S(1)}) custom-call(s32[3]{0:T(128)S(1)} %pad_add_fusion.place_ref, bf16[320,640]{1,0:T(8,128)(2,1)S(1)} %reshape.42.refs_0_, bf16[320,640]{1,0:T(8,128)(2,1)S(1)} %collective-permute-done.6.refs_1_, bf16[8,768,640]{2,1,0:T(8,128)(2,1)S(1)} %hold_tokens.2.refs_2_.refs_4_.refs_1_, ...), custom_call_target="tpu_custom_call" | custom-call | flops 1258291200 | bytes 18874368 | tf_op jit(solution)/shard_map/project_early/pallas_call | solution.py:189
  41.6 3.6 %collective-permute-done.4.refs_0_ = bf16[320,640]{1,0:T(8,128)(2,1)S(1)} collective-permute-done((bf16[320,640]{1,0:T(8,128)(2,1)S(1)}, bf16[320,640]{1,0:T(8,128)(2,1)S(1)}, u32[]{:S(2)}, u32[]{:S(2)}) %collective-permute-start.4) | collective-permute-done | bytes 409632 | tf_op jit(solution)/shard_map/ppermute | solution.py:75
  45.2 4.1 %collective-permute-done.5.refs_2_ = bf16[320,640]{1,0:T(8,128)(2,1)S(1)} collective-permute-done((bf16[320,640]{1,0:T(8,128)(2,1)S(1)}, bf16[320,640]{1,0:T(8,128)(2,1)S(1)}, u32[]{:S(2)}, u32[]{:S(2)}) %collective-permute-start.5) | collective-permute-done | bytes 409632 | tf_op jit(solution)/shard_map/ppermute | solution.py:78
  49.4 1.5 %collective-permute-start.8 = (bf16[320,640]{1,0:T(8,128)(2,1)S(1)}, bf16[320,640]{1,0:T(8,128)(2,1)S(1)}, u32[]{:S(2)}, u32[]{:S(2)}) collective-permute-start(bf16[320,640]{1,0:T(8,128)(2,1)S(1)} %collective-permute-done.5.refs_2_), channel_id=1, source_target_pairs={{32,0},{232,8},{64,32},{8,40},{96,64},{40,72},{128,96},{72,104},{1... | collective-permute-start | bytes 1228808 | tf_op jit(solution)/shard_map/ppermute | solution.py:78
  51.2 1.2 %collective-permute-start.13 = (bf16[320,640]{1,0:T(8,128)(2,1)S(1)}, bf16[320,640]{1,0:T(8,128)(2,1)S(1)}, u32[]{:S(2)}, u32[]{:S(2)}) collective-permute-start(bf16[320,640]{1,0:T(8,128)(2,1)S(1)} %collective-permute-done.9.refs_1_), channel_id=1, source_target_pairs={{0,32},{8,232},{32,64},{40,8},{64,96},{72,40},{96,128},{104,72},{1... | collective-permute-start | bytes 1228808 | tf_op jit(solution)/shard_map/ppermute | solution.py:75
  52.4 1.0 %collective-permute-done.10.refs_3_ = bf16[320,640]{1,0:T(8,128)(2,1)S(1)} collective-permute-done((bf16[320,640]{1,0:T(8,128)(2,1)S(1)}, bf16[320,640]{1,0:T(8,128)(2,1)S(1)}, u32[]{:S(2)}, u32[]{:S(2)}) %collective-permute-start.10) | collective-permute-done | bytes 409632 | tf_op jit(solution)/shard_map/ppermute | solution.py:78
  53.5 4.3 %project_early.5 = (f32[768,640]{1,0:T(8,128)S(1)}, f32[768,640]{1,0:T(8,128)S(1)}) custom-call(s32[3]{0:T(128)S(1)} %pad_add_fusion.place_ref, bf16[320,640]{1,0:T(8,128)(2,1)S(1)} %collective-permute-done.1.refs_0_, bf16[320,640]{1,0:T(8,128)(2,1)S(1)} %collective-permute-done.9.refs_1_, ...), custom_call_target="tpu_custom_call", output_to_operand_aliasing={{0}: (7, {}), {1}: (8, {})} | custom-call | flops 2516582400 | bytes 18874368 | tf_op jit(solution)/shard_map/project_early/pallas_call | solution.py:189
  57.7 2.8 %collective-permute-done.7.refs_0_ = bf16[320,640]{1,0:T(8,128)(2,1)S(1)} collective-permute-done((bf16[320,640]{1,0:T(8,128)(2,1)S(1)}, bf16[320,640]{1,0:T(8,128)(2,1)S(1)}, u32[]{:S(2)}, u32[]{:S(2)}) %collective-permute-start.7) | collective-permute-done | bytes 409632 | tf_op jit(solution)/shard_map/ppermute | solution.py:75
  60.5 2.0 %collective-permute-done.8.refs_2_ = bf16[320,640]{1,0:T(8,128)(2,1)S(1)} collective-permute-done((bf16[320,640]{1,0:T(8,128)(2,1)S(1)}, bf16[320,640]{1,0:T(8,128)(2,1)S(1)}, u32[]{:S(2)}, u32[]{:S(2)}) %collective-permute-start.8) | collective-permute-done | bytes 409632 | tf_op jit(solution)/shard_map/ppermute | solution.py:78
  63.3 2.0 %collective-permute-done.13.refs_1_ = bf16[320,640]{1,0:T(8,128)(2,1)S(1)} collective-permute-done((bf16[320,640]{1,0:T(8,128)(2,1)S(1)}, bf16[320,640]{1,0:T(8,128)(2,1)S(1)}, u32[]{:S(2)}, u32[]{:S(2)}) %collective-permute-start.13) | collective-permute-done | bytes 409632 | tf_op jit(solution)/shard_map/ppermute | solution.py:75
  65.2 1.9 %collective-permute-start.16 = (bf16[320,640]{1,0:T(8,128)(2,1)S(1)}, bf16[320,640]{1,0:T(8,128)(2,1)S(1)}, u32[]{:S(2)}, u32[]{:S(2)}) collective-permute-start(bf16[320,640]{1,0:T(8,128)(2,1)S(1)} %collective-permute-done.13.refs_1_), channel_id=1, source_target_pairs={{0,32},{8,232},{32,64},{40,8},{64,96},{72,40},{96,128},{104,72},{1... | collective-permute-start | bytes 1228808 | tf_op jit(solution)/shard_map/ppermute | solution.py:75
  67.1 4.2 %project_early.6 = (f32[768,640]{1,0:T(8,128)S(1)}, f32[768,640]{1,0:T(8,128)S(1)}) custom-call(s32[3]{0:T(128)S(1)} %pad_add_fusion.place_ref, bf16[320,640]{1,0:T(8,128)(2,1)S(1)} %collective-permute-done.4.refs_0_, bf16[320,640]{1,0:T(8,128)(2,1)S(1)} %collective-permute-done.13.refs_1_, ...), custom_call_target="tpu_custom_call", output_to_operand_aliasing={{0}: (7, {}), {1}: (8, {})} | custom-call | flops 2516582400 | bytes 18874368 | tf_op jit(solution)/shard_map/project_early/pallas_call | solution.py:189
  71.4 3.2 %collective-permute-done.12.refs_3_ = bf16[320,640]{1,0:T(8,128)(2,1)S(1)} collective-permute-done((bf16[320,640]{1,0:T(8,128)(2,1)S(1)}, bf16[320,640]{1,0:T(8,128)(2,1)S(1)}, u32[]{:S(2)}, u32[]{:S(2)}) %collective-permute-start.12) | collective-permute-done | bytes 409632 | tf_op jit(solution)/shard_map/ppermute | solution.py:81
  74.9 1.3 %collective-permute-done.16.refs_1_ = bf16[320,640]{1,0:T(8,128)(2,1)S(1)} collective-permute-done((bf16[320,640]{1,0:T(8,128)(2,1)S(1)}, bf16[320,640]{1,0:T(8,128)(2,1)S(1)}, u32[]{:S(2)}, u32[]{:S(2)}) %collective-permute-start.16) | collective-permute-done | bytes 409632 | tf_op jit(solution)/shard_map/ppermute | solution.py:75
  76.2 4.3 %project_early.7 = (f32[768,640]{1,0:T(8,128)S(1)}, f32[768,640]{1,0:T(8,128)S(1)}) custom-call(s32[3]{0:T(128)S(1)} %pad_add_fusion.place_ref, bf16[320,640]{1,0:T(8,128)(2,1)S(1)} %collective-permute-done.7.refs_0_, bf16[320,640]{1,0:T(8,128)(2,1)S(1)} %collective-permute-done.16.refs_1_, ...), custom_call_target="tpu_custom_call", output_to_operand_aliasing={{0}: (7, {}), {1}: (8, {})} | custom-call | flops 2516582400 | bytes 18874368 | tf_op jit(solution)/shard_map/project_early/pallas_call | solution.py:189
  80.5 2.1 %collective-permute-done.15.refs_1_ = bf16[320,640]{1,0:T(8,128)(2,1)S(1)} collective-permute-done((bf16[320,640]{1,0:T(8,128)(2,1)S(1)}, bf16[320,640]{1,0:T(8,128)(2,1)S(1)}, u32[]{:S(2)}, u32[]{:S(2)}) %collective-permute-start.15) | collective-permute-done | bytes 409632 | tf_op jit(solution)/shard_map/ppermute | solution.py:78
  82.6 2.9 %project_late.2 = (bf16[768,640]{1,0:T(8,128)(2,1)S(1)}, bf16[640,640]{1,0:T(8,128)(2,1)S(1)}) custom-call(s32[3]{0:T(128)S(1)} %pad_add_fusion.place_ref, bf16[320,640]{1,0:T(8,128)(2,1)S(1)} %collective-permute-done.11.refs_0_, bf16[320,640]{1,0:T(8,128)(2,1)S(1)} %collective-permute-done.15.refs_1_, ...), custom_call_target="tpu_custom_call" | custom-call | flops 629145600 | bytes 9437184 | tf_op jit(solution)/shard_map/project_late/pallas_call | solution.py:241
  85.6 1.3 %collective-permute-start.17 = (bf16[768,640]{1,0:T(8,128)(2,1)S(1)}, bf16[768,640]{1,0:T(8,128)(2,1)S(1)}, u32[]{:S(2)}, u32[]{:S(2)}) collective-permute-start(bf16[768,640]{1,0:T(8,128)(2,1)S(1)} %get-tuple-element.76), channel_id=1, source_target_pairs={{0,8},{8,0},{1,9},{9,1},{2,10},{10,2},{3,11},{11,3},{4,12},{12,4},... | collective-permute-start | bytes 2949128 | tf_op jit(solution)/shard_map/ppermute | solution.py:341
  87.0 2.9 %project_late.3.own_ref = bf16[768,640]{1,0:T(8,128)(2,1)S(1)} custom-call(s32[3]{0:T(128)S(1)} %pad_add_fusion.place_ref, bf16[640,640]{1,0:T(8,128)(2,1)S(1)} %get-tuple-element.72.refs_0_, bf16[8,768,640]{2,1,0:T(8,128)(2,1)S(1)} %hold_tokens.2.refs_2_.refs_4_.refs_1_, f32[768,640]{1,0:T(8,128)S(1)} %get-tuple-element.73.refs_2_, ...), custom_call_target="tpu_custom_call" | custom-call | flops 629145600 | bytes 9437184 | tf_op jit(solution)/shard_map/project_late/pallas_call | solution.py:241
  89.9 5.0 %attend.1 = bf16[768,1024]{1,0:T(8,128)(2,1)} custom-call(s32[3]{0:T(128)S(1)} %pad_add_fusion.place_ref, bf16[768,640]{1,0:T(8,128)(2,1)S(1)} %project_late.3.own_ref, bf16[768,640]{1,0:T(8,128)(2,1)S(1)} %collective-permute-done.17.received_ref, s32[768,1]{1,0:T(8,128)S(1)} %reduce_max.23.start_ref), custom_call_target="tpu_custom_call" | custom-call | flops 1610612736 | bytes 4194304 | tf_op jit(solution)/shard_map/attend/pallas_call | solution.py:301
  (39 shorter events, 3.7 us)
Async XLA Ops:
  0.0 30.5 %collective-permute-start.3 = (bf16[768,5120]{1,0:T(8,128)(2,1)}, bf16[768,5120]{1,0:T(8,128)(2,1)}, u32[]{:S(2)}, u32[]{:S(2)}) collective-permute-start(bf16[768,5120]{1,0:T(8,128)(2,1)} %token_ref.1), channel_id=1, source_target_pairs={{0,8},{8,0},{1,9},{9,1},{2,10},{10,2},{3,11},{11,3},{4,12},{12,4},... | collective-permute-start | bytes 23592968 | tf_op jit(solution)/shard_map/ppermute | solution.py:324
  3.2 6.4 %collective-permute-start = (s32[1,8]{1,0:T(1,128)}, s32[1,8]{1,0:T(1,128)S(1)}, u32[]{:S(2)}, u32[]{:S(2)}) collective-permute-start(s32[1,8]{1,0:T(1,128)} %param.6), channel_id=1, source_target_pairs={{0,8},{8,0},{1,9},{9,1},{2,10},{10,2},{3,11},{11,3},{4,12},{12,4},... | collective-permute-start | bytes 104 | tf_op jit(solution)/shard_map/ppermute | solution.py:325
  3.2 1.0 %copy-start = (bf16[20,10240]{1,0:T(8,128)(2,1)S(1)}, bf16[20,10240]{1,0:T(8,128)(2,1)}, u32[]{:S(2)}) copy-start(bf16[20,10240]{1,0:T(8,128)(2,1)} %weight_ref.1) | copy-start | bytes 1228804
  4.3 5.0 %copy-start.3 = (s32[1,8]{1,0:T(1,128)S(1)}, s32[1,8]{1,0:T(1,128)}, u32[]{:S(2)}) copy-start(s32[1,8]{1,0:T(1,128)} %param.6) | copy-start | bytes 100
  5.1 13.2 %all-to-all-start = ((bf16[16,20,640]{2,1,0:T(8,128)(2,1)}), bf16[16,20,640]{2,1,0:T(8,128)(2,1)S(1)}, u32[]{:S(2)}, u32[]{:S(2)}) async-start(bf16[16,20,640]{2,1,0:T(8,128)(2,1)} %regroup.1), calls=%async_computation | async-start | bytes 983040 | tf_op jit(solution)/shard_map/all_to_all | solution.py:327
  18.4 16.0 %collective-permute-start.1 = (bf16[320,640]{1,0:T(8,128)(2,1)S(1)}, bf16[320,640]{1,0:T(8,128)(2,1)S(1)}, u32[]{:S(2)}, u32[]{:S(2)}) collective-permute-start(bf16[320,640]{1,0:T(8,128)(2,1)S(1)} %reshape.42.refs_0_), channel_id=1, source_target_pairs={{0,32},{8,232},{32,64},{40,8},{64,96},{72,40},{96,128},{104,72},{1... | collective-permute-start | bytes 1228808 | tf_op jit(solution)/shard_map/ppermute | solution.py:75
  24.0 11.3 %collective-permute-start.2 = (bf16[320,640]{1,0:T(8,128)(2,1)S(1)}, bf16[320,640]{1,0:T(8,128)(2,1)S(1)}, u32[]{:S(2)}, u32[]{:S(2)}) collective-permute-start(bf16[320,640]{1,0:T(8,128)(2,1)S(1)} %reshape.42.refs_0_), channel_id=1, source_target_pairs={{32,0},{232,8},{64,32},{8,40},{96,64},{40,72},{128,96},{72,104},{1... | collective-permute-start | bytes 1228808 | tf_op jit(solution)/shard_map/ppermute | solution.py:78
  24.0 13.2 %collective-permute-start.6 = (bf16[320,640]{1,0:T(8,128)(2,1)S(1)}, bf16[320,640]{1,0:T(8,128)(2,1)S(1)}, u32[]{:S(2)}, u32[]{:S(2)}) collective-permute-start(bf16[320,640]{1,0:T(8,128)(2,1)S(1)} %reshape.42.refs_0_), channel_id=1, source_target_pairs={{0,16},{16,0},{1,17},{17,1},{2,18},{18,2},{3,19},{19,3},{4,20},{20... | collective-permute-start | bytes 1228808 | tf_op jit(solution)/shard_map/ppermute | solution.py:81
  35.3 9.9 %collective-permute-start.4 = (bf16[320,640]{1,0:T(8,128)(2,1)S(1)}, bf16[320,640]{1,0:T(8,128)(2,1)S(1)}, u32[]{:S(2)}, u32[]{:S(2)}) collective-permute-start(bf16[320,640]{1,0:T(8,128)(2,1)S(1)} %collective-permute-done.1.refs_0_), channel_id=1, source_target_pairs={{0,32},{8,232},{32,64},{40,8},{64,96},{72,40},{96,128},{104,72},{1... | collective-permute-start | bytes 1228808 | tf_op jit(solution)/shard_map/ppermute | solution.py:75
  37.2 12.2 %collective-permute-start.5 = (bf16[320,640]{1,0:T(8,128)(2,1)S(1)}, bf16[320,640]{1,0:T(8,128)(2,1)S(1)}, u32[]{:S(2)}, u32[]{:S(2)}) collective-permute-start(bf16[320,640]{1,0:T(8,128)(2,1)S(1)} %collective-permute-done.2.refs_2_), channel_id=1, source_target_pairs={{32,0},{232,8},{64,32},{8,40},{96,64},{40,72},{128,96},{72,104},{1... | collective-permute-start | bytes 1228808 | tf_op jit(solution)/shard_map/ppermute | solution.py:78
  37.2 14.0 %collective-permute-start.9 = (bf16[320,640]{1,0:T(8,128)(2,1)S(1)}, bf16[320,640]{1,0:T(8,128)(2,1)S(1)}, u32[]{:S(2)}, u32[]{:S(2)}) collective-permute-start(bf16[320,640]{1,0:T(8,128)(2,1)S(1)} %collective-permute-done.1.refs_0_), channel_id=1, source_target_pairs={{0,16},{16,0},{1,17},{17,1},{2,18},{18,2},{3,19},{19,3},{4,20},{20... | collective-permute-start | bytes 1228808 | tf_op jit(solution)/shard_map/ppermute | solution.py:81
  39.0 14.4 %collective-permute-start.10 = (bf16[320,640]{1,0:T(8,128)(2,1)S(1)}, bf16[320,640]{1,0:T(8,128)(2,1)S(1)}, u32[]{:S(2)}, u32[]{:S(2)}) collective-permute-start(bf16[320,640]{1,0:T(8,128)(2,1)S(1)} %collective-permute-done.6.refs_1_), channel_id=1, source_target_pairs={{32,0},{232,8},{64,32},{8,40},{96,64},{40,72},{128,96},{72,104},{1... | collective-permute-start | bytes 1228808 | tf_op jit(solution)/shard_map/ppermute | solution.py:78
  49.4 11.1 %collective-permute-start.7 = (bf16[320,640]{1,0:T(8,128)(2,1)S(1)}, bf16[320,640]{1,0:T(8,128)(2,1)S(1)}, u32[]{:S(2)}, u32[]{:S(2)}) collective-permute-start(bf16[320,640]{1,0:T(8,128)(2,1)S(1)} %collective-permute-done.4.refs_0_), channel_id=1, source_target_pairs={{0,32},{8,232},{32,64},{40,8},{64,96},{72,40},{96,128},{104,72},{1... | collective-permute-start | bytes 1228808 | tf_op jit(solution)/shard_map/ppermute | solution.py:75
  49.4 13.1 %collective-permute-start.8 = (bf16[320,640]{1,0:T(8,128)(2,1)S(1)}, bf16[320,640]{1,0:T(8,128)(2,1)S(1)}, u32[]{:S(2)}, u32[]{:S(2)}) collective-permute-start(bf16[320,640]{1,0:T(8,128)(2,1)S(1)} %collective-permute-done.5.refs_2_), channel_id=1, source_target_pairs={{32,0},{232,8},{64,32},{8,40},{96,64},{40,72},{128,96},{72,104},{1... | collective-permute-start | bytes 1228808 | tf_op jit(solution)/shard_map/ppermute | solution.py:78
  50.8 16.3 %collective-permute-start.14 = (bf16[320,640]{1,0:T(8,128)(2,1)S(1)}, bf16[320,640]{1,0:T(8,128)(2,1)S(1)}, u32[]{:S(2)}, u32[]{:S(2)}) collective-permute-start(bf16[320,640]{1,0:T(8,128)(2,1)S(1)} %collective-permute-done.5.refs_2_), channel_id=1, source_target_pairs={{0,16},{16,0},{1,17},{17,1},{2,18},{18,2},{3,19},{19,3},{4,20},{20... | collective-permute-start | bytes 1228808 | tf_op jit(solution)/shard_map/ppermute | solution.py:81
  51.2 14.0 %collective-permute-start.13 = (bf16[320,640]{1,0:T(8,128)(2,1)S(1)}, bf16[320,640]{1,0:T(8,128)(2,1)S(1)}, u32[]{:S(2)}, u32[]{:S(2)}) collective-permute-start(bf16[320,640]{1,0:T(8,128)(2,1)S(1)} %collective-permute-done.9.refs_1_), channel_id=1, source_target_pairs={{0,32},{8,232},{32,64},{40,8},{64,96},{72,40},{96,128},{104,72},{1... | collective-permute-start | bytes 1228808 | tf_op jit(solution)/shard_map/ppermute | solution.py:75
  62.5 12.1 %collective-permute-start.12 = (bf16[320,640]{1,0:T(8,128)(2,1)S(1)}, bf16[320,640]{1,0:T(8,128)(2,1)S(1)}, u32[]{:S(2)}, u32[]{:S(2)}) collective-permute-start(bf16[320,640]{1,0:T(8,128)(2,1)S(1)} %collective-permute-done.8.refs_2_), channel_id=1, source_target_pairs={{0,16},{16,0},{1,17},{17,1},{2,18},{18,2},{3,19},{19,3},{4,20},{20... | collective-permute-start | bytes 1228808 | tf_op jit(solution)/shard_map/ppermute | solution.py:81
  63.3 17.2 %collective-permute-start.11 = (bf16[320,640]{1,0:T(8,128)(2,1)S(1)}, bf16[320,640]{1,0:T(8,128)(2,1)S(1)}, u32[]{:S(2)}, u32[]{:S(2)}) collective-permute-start(bf16[320,640]{1,0:T(8,128)(2,1)S(1)} %collective-permute-done.8.refs_2_), channel_id=1, source_target_pairs={{32,0},{232,8},{64,32},{8,40},{96,64},{40,72},{128,96},{72,104},{1... | collective-permute-start | bytes 1228808 | tf_op jit(solution)/shard_map/ppermute | solution.py:78
  65.2 11.0 %collective-permute-start.16 = (bf16[320,640]{1,0:T(8,128)(2,1)S(1)}, bf16[320,640]{1,0:T(8,128)(2,1)S(1)}, u32[]{:S(2)}, u32[]{:S(2)}) collective-permute-start(bf16[320,640]{1,0:T(8,128)(2,1)S(1)} %collective-permute-done.13.refs_1_), channel_id=1, source_target_pairs={{0,32},{8,232},{32,64},{40,8},{64,96},{72,40},{96,128},{104,72},{1... | collective-permute-start | bytes 1228808 | tf_op jit(solution)/shard_map/ppermute | solution.py:75
  74.6 8.0 %copy-start.1 = (f32[128]{0:T(128)S(1)}, f32[128]{0:T(128)}, u32[]{:S(2)}) copy-start(f32[128]{0:T(128)} %param.8) | copy-start | bytes 1540
  74.6 8.0 %copy-start.2 = (f32[128]{0:T(128)S(1)}, f32[128]{0:T(128)}, u32[]{:S(2)}) copy-start(f32[128]{0:T(128)} %param.9) | copy-start | bytes 1540
  74.6 8.0 %collective-permute-start.15 = (bf16[320,640]{1,0:T(8,128)(2,1)S(1)}, bf16[320,640]{1,0:T(8,128)(2,1)S(1)}, u32[]{:S(2)}, u32[]{:S(2)}) collective-permute-start(bf16[320,640]{1,0:T(8,128)(2,1)S(1)} %collective-permute-done.12.refs_3_), channel_id=1, source_target_pairs={{32,0},{232,8},{64,32},{8,40},{96,64},{40,72},{128,96},{72,104},{1... | collective-permute-start | bytes 1228808 | tf_op jit(solution)/shard_map/ppermute | solution.py:78
  85.6 4.3 %collective-permute-start.17 = (bf16[768,640]{1,0:T(8,128)(2,1)S(1)}, bf16[768,640]{1,0:T(8,128)(2,1)S(1)}, u32[]{:S(2)}, u32[]{:S(2)}) collective-permute-start(bf16[768,640]{1,0:T(8,128)(2,1)S(1)} %get-tuple-element.76), channel_id=1, source_target_pairs={{0,8},{8,0},{1,9},{9,1},{2,10},{10,2},{3,11},{11,3},{4,12},{12,4},... | collective-permute-start | bytes 2949128 | tf_op jit(solution)/shard_map/ppermute | solution.py:341

commit v5 on v4

--- a/solution.py
+++ b/solution.py
@@ -213,7 +213,14 @@
         weight = refs[n_in + 7] if ready is None else sources[0]
 
         def normed(field, gain, rows):
-            factor = lax.rsqrt(jnp.mean(field * field, axis=1, keepdims=True) + NORM_EPS)
+            square = field * field
+            upper = square.astype(jnp.bfloat16)
+            lower = (square - upper.astype(jnp.float32)).astype(jnp.bfloat16)
+            ones = jnp.ones((2 * HEAD, HEAD), jnp.bfloat16)
+            total = jnp.dot(
+                jnp.concatenate([upper, lower], axis=1), ones, preferred_element_type=jnp.float32
+            )
+            factor = lax.rsqrt(total * (1.0 / HEAD) + NORM_EPS)
             field = field * factor * gain
             return field * cos_ref[rows] + pltpu.roll(field, HEAD // 2, 1) * sin_ref[rows]
 
@@ -284,10 +291,9 @@
                 scores = lax.dot_general(
                     queries, keys, (((1,), (1,)), ((), ())), preferred_element_type=jnp.float32
                 )
-                scores = scores.reshape(4, QBLOCK, count) * scale + bias[None]
-                scores = scores.reshape(4 * QBLOCK, count)
+                scores = (scores.reshape(4, QBLOCK, count) + bias[None]).reshape(4 * QBLOCK, count)
                 top = jnp.max(scores, axis=1, keepdims=True)
-                weights = jnp.exp2(scores - top).astype(jnp.bfloat16)
+                weights = jnp.exp2((scores - top) * scale).astype(jnp.bfloat16)
                 mixed = jnp.dot(weights, values, preferred_element_type=jnp.float32)
                 mixed = (mixed[:, :HEAD] / mixed[:, HEAD:]).astype(jnp.bfloat16)
                 for head in range(4):

time: 95.3 us -> 94.3 us (0.990)
  Pallas kernels: 34.7 us -> 33.7 us
  transfers between devices with their start and end apart: 19 -> 19, of which waited for: 11 -> 11; matrix products, arithmetic and copies ran while one was open for 4% -> 5% of each run, Pallas kernels for 28% -> 28%
where the time goes in v5:
time: 94.3 us; the launch traced here: 94.1 us
  Pallas kernels  33.7 us (36%)
  waiting for transfers between devices  28.2 us (30%)
  starting transfers between devices  26.6 us (28%)
  other arithmetic  4 us (4%)
  local copies, waits for them, and re-layouts  1.28 us (1%)
    pallas_call x4, Pallas kernels, project_early(): pl.pallas_call(kernel, out_shape=(shape, shape), in_specs=[SMEM] + [VMEM]...  15.3 us
    ppermute x5, starting transfers between devices, up(): return lax.ppermute(array, ('z', 'c'), UP)  10.6 us
    ppermute x6, waiting for transfers between devices, down(): return lax.ppermute(array, ('z', 'c'), DOWN)  10.2 us
    ppermute x5, waiting for transfers between devices, up(): return lax.ppermute(array, ('z', 'c'), UP)  9.72 us
    pallas_call x2, Pallas kernels, hold_tokens(): pl.pallas_call(kernel, out_shape=pltpu.VMEM((NZ, ROWS, DEPTH), jnp.bfloat...  7.83 us
    ppermute x4, starting transfers between devices, across(): return lax.ppermute(array, 'xh', SWAP)  5.45 us
    all_to_all x1, waiting for transfers between devices, shards(): lax.all_to_all(spread, ('c',) + TENSOR, split_axis=0, concat_axis=0, tile...  5 us
    pallas_call x2, Pallas kernels, project_late(): pl.pallas_call(kernel, out_shape=(shape, weight_shape) if first else shap...  4.92 us
  transfers between devices with their start and end apart: 19, of which 11 were waited for; matrix products, arithmetic and copies ran while one was open for 5% of the time, Pallas kernels for 28%

profile of v5, /device:TPU:1, one launch (start us, length us, event | category | flops | bytes accessed | tf_op | source)
XLA Modules:
  0.0 94.1 jit_solution(8288655236470002341)
XLA Ops:
  0.0 3.2 %collective-permute-start.3 = (bf16[768,5120]{1,0:T(8,128)(2,1)}, bf16[768,5120]{1,0:T(8,128)(2,1)}, u32[]{:S(2)}, u32[]{:S(2)}) collective-permute-start(bf16[768,5120]{1,0:T(8,128)(2,1)} %token_ref.1), channel_id=1, source_target_pairs={{0,8},{8,0},{1,9},{9,1},{2,10},{10,2},{3,11},{11,3},{4,12},{12,4},... | collective-permute-start | bytes 23592968 | tf_op jit(solution)/shard_map/ppermute | solution.py:330
  3.2 1.0 %copy-done = bf16[20,10240]{1,0:T(8,128)(2,1)S(1)} copy-done((bf16[20,10240]{1,0:T(8,128)(2,1)S(1)}, bf16[20,10240]{1,0:T(8,128)(2,1)}, u32[]{:S(2)}) %copy-start) | copy-done | bytes 409624
  5.1 4.2 %all-to-all-start = ((bf16[16,20,640]{2,1,0:T(8,128)(2,1)}), bf16[16,20,640]{2,1,0:T(8,128)(2,1)S(1)}, u32[]{:S(2)}, u32[]{:S(2)}) async-start(bf16[16,20,640]{2,1,0:T(8,128)(2,1)} %regroup.1), calls=%async_computation | async-start | bytes 983040 | tf_op jit(solution)/shard_map/all_to_all | solution.py:333
  9.9 2.8 %fusion.1 = (f32[768,64]{1,0:T(8,128)S(1)}, f32[768,64]{1,0:T(8,128)S(1)}, f32[768,64]{1,0:T(8,128)S(1)}, f32[768,64]{1,0:T(8,128)S(1)}, f32[768,64]{1,0:T(8,128)S(1)}, /*index=5*/f32[768,64]{1,0:T(8,128)S(1)}) fusion(f32[64]{0:T(128)S(1)} %multiply_power_fusion, f32[768]{0:T(1024)S(1)} %subtract_convert_fusion, f32[768]{0:T(1024)S(1)} %subtract_convert_fusion.1), kind=kLoop, calls=%fused_computation.9 | loop fusion | flops 196608 | bytes 1186048 | tf_op jit(solution)/shard_map/neg | solution.py:48
  13.3 5.0 %all-to-all-done = bf16[16,20,640]{2,1,0:T(8,128)(2,1)S(1)} async-done(((bf16[16,20,640]{2,1,0:T(8,128)(2,1)}), bf16[16,20,640]{2,1,0:T(8,128)(2,1)S(1)}, u32[]{:S(2)}, u32[]{:S(2)}) %all-to-all-start) | async-done | bytes 409632 | tf_op jit(solution)/shard_map/all_to_all | solution.py:333
  18.4 5.7 %collective-permute-start.1 = (bf16[320,640]{1,0:T(8,128)(2,1)S(1)}, bf16[320,640]{1,0:T(8,128)(2,1)S(1)}, u32[]{:S(2)}, u32[]{:S(2)}) collective-permute-start(bf16[320,640]{1,0:T(8,128)(2,1)S(1)} %reshape.42.refs_0_), channel_id=1, source_target_pairs={{0,32},{8,232},{32,64},{40,8},{64,96},{72,40},{96,128},{104,72},{1... | collective-permute-start | bytes 1228808 | tf_op jit(solution)/shard_map/ppermute | solution.py:75
  24.0 2.5 %collective-permute-start.6 = (bf16[320,640]{1,0:T(8,128)(2,1)S(1)}, bf16[320,640]{1,0:T(8,128)(2,1)S(1)}, u32[]{:S(2)}, u32[]{:S(2)}) collective-permute-start(bf16[320,640]{1,0:T(8,128)(2,1)S(1)} %reshape.42.refs_0_), channel_id=1, source_target_pairs={{0,16},{16,0},{1,17},{17,1},{2,18},{18,2},{3,19},{19,3},{4,20},{20... | collective-permute-start | bytes 1228808 | tf_op jit(solution)/shard_map/ppermute | solution.py:81
  26.5 3.9 %hold_tokens.2.refs_2_.refs_4_.refs_1_ = bf16[8,768,640]{2,1,0:T(8,128)(2,1)S(1)} custom-call(s32[3]{0:T(128)S(1)} %pad_add_fusion.place_ref, bf16[768,5120]{1,0:T(8,128)(2,1)} %token_ref.1), custom_call_target="tpu_custom_call" | custom-call | bytes 16777216 | tf_op jit(solution)/shard_map/hold_tokens/pallas_call | solution.py:158
  30.5 3.9 %hold_tokens.3.refs_3_.refs_5_.refs_2_ = bf16[8,768,640]{2,1,0:T(8,128)(2,1)S(1)} custom-call(s32[3]{0:T(128)S(1)} %pad_add_fusion.place_ref, bf16[768,5120]{1,0:T(8,128)(2,1)} %collective-permute-done.3.token_ref), custom_call_target="tpu_custom_call" | custom-call | bytes 16777216 | tf_op jit(solution)/shard_map/hold_tokens/pallas_call | solution.py:158
  34.4 0.9 collective-permute-done.2.refs_2_
  35.3 1.9 %collective-permute-start.4 = (bf16[320,640]{1,0:T(8,128)(2,1)S(1)}, bf16[320,640]{1,0:T(8,128)(2,1)S(1)}, u32[]{:S(2)}, u32[]{:S(2)}) collective-permute-start(bf16[320,640]{1,0:T(8,128)(2,1)S(1)} %collective-permute-done.1.refs_0_), channel_id=1, source_target_pairs={{0,32},{8,232},{32,64},{40,8},{64,96},{72,40},{96,128},{104,72},{1... | collective-permute-start | bytes 1228808 | tf_op jit(solution)/shard_map/ppermute | solution.py:75
  37.2 1.9 %collective-permute-start.9 = (bf16[320,640]{1,0:T(8,128)(2,1)S(1)}, bf16[320,640]{1,0:T(8,128)(2,1)S(1)}, u32[]{:S(2)}, u32[]{:S(2)}) collective-permute-start(bf16[320,640]{1,0:T(8,128)(2,1)S(1)} %collective-permute-done.1.refs_0_), channel_id=1, source_target_pairs={{0,16},{16,0},{1,17},{17,1},{2,18},{18,2},{3,19},{19,3},{4,20},{20... | collective-permute-start | bytes 1228808 | tf_op jit(solution)/shard_map/ppermute | solution.py:81
  39.1 2.5 %project_early.4 = (f32[768,640]{1,0:T(8,128)S(1)}, f32[768,640]{1,0:T(8,128)S(1)}) custom-call(s32[3]{0:T(128)S(1)} %pad_add_fusion.place_ref, bf16[320,640]{1,0:T(8,128)(2,1)S(1)} %reshape.42.refs_0_, bf16[320,640]{1,0:T(8,128)(2,1)S(1)} %collective-permute-done.6.refs_1_, bf16[8,768,640]{2,1,0:T(8,128)(2,1)S(1)} %hold_tokens.2.refs_2_.refs_4_.refs_1_, ...), custom_call_target="tpu_custom_call" | custom-call | flops 1258291200 | bytes 18874368 | tf_op jit(solution)/shard_map/project_early/pallas_call | solution.py:189
  41.6 3.6 %collective-permute-done.4.refs_0_ = bf16[320,640]{1,0:T(8,128)(2,1)S(1)} collective-permute-done((bf16[320,640]{1,0:T(8,128)(2,1)S(1)}, bf16[320,640]{1,0:T(8,128)(2,1)S(1)}, u32[]{:S(2)}, u32[]{:S(2)}) %collective-permute-start.4) | collective-permute-done | bytes 409632 | tf_op jit(solution)/shard_map/ppermute | solution.py:75
  45.2 4.1 %collective-permute-done.5.refs_2_ = bf16[320,640]{1,0:T(8,128)(2,1)S(1)} collective-permute-done((bf16[320,640]{1,0:T(8,128)(2,1)S(1)}, bf16[320,640]{1,0:T(8,128)(2,1)S(1)}, u32[]{:S(2)}, u32[]{:S(2)}) %collective-permute-start.5) | collective-permute-done | bytes 409632 | tf_op jit(solution)/shard_map/ppermute | solution.py:78
  49.4 1.5 %collective-permute-start.8 = (bf16[320,640]{1,0:T(8,128)(2,1)S(1)}, bf16[320,640]{1,0:T(8,128)(2,1)S(1)}, u32[]{:S(2)}, u32[]{:S(2)}) collective-permute-start(bf16[320,640]{1,0:T(8,128)(2,1)S(1)} %collective-permute-done.5.refs_2_), channel_id=1, source_target_pairs={{32,0},{232,8},{64,32},{8,40},{96,64},{40,72},{128,96},{72,104},{1... | collective-permute-start | bytes 1228808 | tf_op jit(solution)/shard_map/ppermute | solution.py:78
  51.2 1.2 %collective-permute-start.13 = (bf16[320,640]{1,0:T(8,128)(2,1)S(1)}, bf16[320,640]{1,0:T(8,128)(2,1)S(1)}, u32[]{:S(2)}, u32[]{:S(2)}) collective-permute-start(bf16[320,640]{1,0:T(8,128)(2,1)S(1)} %collective-permute-done.9.refs_1_), channel_id=1, source_target_pairs={{0,32},{8,232},{32,64},{40,8},{64,96},{72,40},{96,128},{104,72},{1... | collective-permute-start | bytes 1228808 | tf_op jit(solution)/shard_map/ppermute | solution.py:75
  52.4 1.0 %collective-permute-done.10.refs_3_ = bf16[320,640]{1,0:T(8,128)(2,1)S(1)} collective-permute-done((bf16[320,640]{1,0:T(8,128)(2,1)S(1)}, bf16[320,640]{1,0:T(8,128)(2,1)S(1)}, u32[]{:S(2)}, u32[]{:S(2)}) %collective-permute-start.10) | collective-permute-done | bytes 409632 | tf_op jit(solution)/shard_map/ppermute | solution.py:78
  53.5 4.3 %project_early.5 = (f32[768,640]{1,0:T(8,128)S(1)}, f32[768,640]{1,0:T(8,128)S(1)}) custom-call(s32[3]{0:T(128)S(1)} %pad_add_fusion.place_ref, bf16[320,640]{1,0:T(8,128)(2,1)S(1)} %collective-permute-done.1.refs_0_, bf16[320,640]{1,0:T(8,128)(2,1)S(1)} %collective-permute-done.9.refs_1_, ...), custom_call_target="tpu_custom_call", output_to_operand_aliasing={{0}: (7, {}), {1}: (8, {})} | custom-call | flops 2516582400 | bytes 18874368 | tf_op jit(solution)/shard_map/project_early/pallas_call | solution.py:189
  57.7 2.8 %collective-permute-done.7.refs_0_ = bf16[320,640]{1,0:T(8,128)(2,1)S(1)} collective-permute-done((bf16[320,640]{1,0:T(8,128)(2,1)S(1)}, bf16[320,640]{1,0:T(8,128)(2,1)S(1)}, u32[]{:S(2)}, u32[]{:S(2)}) %collective-permute-start.7) | collective-permute-done | bytes 409632 | tf_op jit(solution)/shard_map/ppermute | solution.py:75
  60.5 2.0 %collective-permute-done.8.refs_2_ = bf16[320,640]{1,0:T(8,128)(2,1)S(1)} collective-permute-done((bf16[320,640]{1,0:T(8,128)(2,1)S(1)}, bf16[320,640]{1,0:T(8,128)(2,1)S(1)}, u32[]{:S(2)}, u32[]{:S(2)}) %collective-permute-start.8) | collective-permute-done | bytes 409632 | tf_op jit(solution)/shard_map/ppermute | solution.py:78
  63.3 2.0 %collective-permute-done.13.refs_1_ = bf16[320,640]{1,0:T(8,128)(2,1)S(1)} collective-permute-done((bf16[320,640]{1,0:T(8,128)(2,1)S(1)}, bf16[320,640]{1,0:T(8,128)(2,1)S(1)}, u32[]{:S(2)}, u32[]{:S(2)}) %collective-permute-start.13) | collective-permute-done | bytes 409632 | tf_op jit(solution)/shard_map/ppermute | solution.py:75
  65.2 1.9 %collective-permute-start.16 = (bf16[320,640]{1,0:T(8,128)(2,1)S(1)}, bf16[320,640]{1,0:T(8,128)(2,1)S(1)}, u32[]{:S(2)}, u32[]{:S(2)}) collective-permute-start(bf16[320,640]{1,0:T(8,128)(2,1)S(1)} %collective-permute-done.13.refs_1_), channel_id=1, source_target_pairs={{0,32},{8,232},{32,64},{40,8},{64,96},{72,40},{96,128},{104,72},{1... | collective-permute-start | bytes 1228808 | tf_op jit(solution)/shard_map/ppermute | solution.py:75
  67.1 4.2 %project_early.6 = (f32[768,640]{1,0:T(8,128)S(1)}, f32[768,640]{1,0:T(8,128)S(1)}) custom-call(s32[3]{0:T(128)S(1)} %pad_add_fusion.place_ref, bf16[320,640]{1,0:T(8,128)(2,1)S(1)} %collective-permute-done.4.refs_0_, bf16[320,640]{1,0:T(8,128)(2,1)S(1)} %collective-permute-done.13.refs_1_, ...), custom_call_target="tpu_custom_call", output_to_operand_aliasing={{0}: (7, {}), {1}: (8, {})} | custom-call | flops 2516582400 | bytes 18874368 | tf_op jit(solution)/shard_map/project_early/pallas_call | solution.py:189
  71.4 3.2 %collective-permute-done.12.refs_3_ = bf16[320,640]{1,0:T(8,128)(2,1)S(1)} collective-permute-done((bf16[320,640]{1,0:T(8,128)(2,1)S(1)}, bf16[320,640]{1,0:T(8,128)(2,1)S(1)}, u32[]{:S(2)}, u32[]{:S(2)}) %collective-permute-start.12) | collective-permute-done | bytes 409632 | tf_op jit(solution)/shard_map/ppermute | solution.py:81
  74.9 1.3 %collective-permute-done.16.refs_1_ = bf16[320,640]{1,0:T(8,128)(2,1)S(1)} collective-permute-done((bf16[320,640]{1,0:T(8,128)(2,1)S(1)}, bf16[320,640]{1,0:T(8,128)(2,1)S(1)}, u32[]{:S(2)}, u32[]{:S(2)}) %collective-permute-start.16) | collective-permute-done | bytes 409632 | tf_op jit(solution)/shard_map/ppermute | solution.py:75
  76.2 4.3 %project_early.7 = (f32[768,640]{1,0:T(8,128)S(1)}, f32[768,640]{1,0:T(8,128)S(1)}) custom-call(s32[3]{0:T(128)S(1)} %pad_add_fusion.place_ref, bf16[320,640]{1,0:T(8,128)(2,1)S(1)} %collective-permute-done.7.refs_0_, bf16[320,640]{1,0:T(8,128)(2,1)S(1)} %collective-permute-done.16.refs_1_, ...), custom_call_target="tpu_custom_call", output_to_operand_aliasing={{0}: (7, {}), {1}: (8, {})} | custom-call | flops 2516582400 | bytes 18874368 | tf_op jit(solution)/shard_map/project_early/pallas_call | solution.py:189
  80.5 2.1 %collective-permute-done.15.refs_1_ = bf16[320,640]{1,0:T(8,128)(2,1)S(1)} collective-permute-done((bf16[320,640]{1,0:T(8,128)(2,1)S(1)}, bf16[320,640]{1,0:T(8,128)(2,1)S(1)}, u32[]{:S(2)}, u32[]{:S(2)}) %collective-permute-start.15) | collective-permute-done | bytes 409632 | tf_op jit(solution)/shard_map/ppermute | solution.py:78
  82.6 2.5 %project_late.2 = (bf16[768,640]{1,0:T(8,128)(2,1)S(1)}, bf16[640,640]{1,0:T(8,128)(2,1)S(1)}) custom-call(s32[3]{0:T(128)S(1)} %pad_add_fusion.place_ref, bf16[320,640]{1,0:T(8,128)(2,1)S(1)} %collective-permute-done.11.refs_0_, bf16[320,640]{1,0:T(8,128)(2,1)S(1)} %collective-permute-done.15.refs_1_, ...), custom_call_target="tpu_custom_call" | custom-call | flops 629145600 | bytes 9437184 | tf_op jit(solution)/shard_map/project_late/pallas_call | solution.py:248
  85.1 1.3 %collective-permute-start.17 = (bf16[768,640]{1,0:T(8,128)(2,1)S(1)}, bf16[768,640]{1,0:T(8,128)(2,1)S(1)}, u32[]{:S(2)}, u32[]{:S(2)}) collective-permute-start(bf16[768,640]{1,0:T(8,128)(2,1)S(1)} %get-tuple-element.76), channel_id=1, source_target_pairs={{0,8},{8,0},{1,9},{9,1},{2,10},{10,2},{3,11},{11,3},{4,12},{12,4},... | collective-permute-start | bytes 2949128 | tf_op jit(solution)/shard_map/ppermute | solution.py:347
  86.6 2.4 %project_late.3.own_ref = bf16[768,640]{1,0:T(8,128)(2,1)S(1)} custom-call(s32[3]{0:T(128)S(1)} %pad_add_fusion.place_ref, bf16[640,640]{1,0:T(8,128)(2,1)S(1)} %get-tuple-element.72.refs_0_, bf16[8,768,640]{2,1,0:T(8,128)(2,1)S(1)} %hold_tokens.2.refs_2_.refs_4_.refs_1_, f32[768,640]{1,0:T(8,128)S(1)} %get-tuple-element.73.refs_2_, ...), custom_call_target="tpu_custom_call" | custom-call | flops 629145600 | bytes 9437184 | tf_op jit(solution)/shard_map/project_late/pallas_call | solution.py:248
  89.0 4.9 %attend.1 = bf16[768,1024]{1,0:T(8,128)(2,1)} custom-call(s32[3]{0:T(128)S(1)} %pad_add_fusion.place_ref, bf16[768,640]{1,0:T(8,128)(2,1)S(1)} %project_late.3.own_ref, bf16[768,640]{1,0:T(8,128)(2,1)S(1)} %collective-permute-done.17.received_ref, s32[768,1]{1,0:T(8,128)S(1)} %reduce_max.23.start_ref), custom_call_target="tpu_custom_call" | custom-call | flops 1610612736 | bytes 4194304 | tf_op jit(solution)/shard_map/attend/pallas_call | solution.py:307
  (39 shorter events, 3.7 us)
Async XLA Ops:
  0.0 30.5 %collective-permute-start.3 = (bf16[768,5120]{1,0:T(8,128)(2,1)}, bf16[768,5120]{1,0:T(8,128)(2,1)}, u32[]{:S(2)}, u32[]{:S(2)}) collective-permute-start(bf16[768,5120]{1,0:T(8,128)(2,1)} %token_ref.1), channel_id=1, source_target_pairs={{0,8},{8,0},{1,9},{9,1},{2,10},{10,2},{3,11},{11,3},{4,12},{12,4},... | collective-permute-start | bytes 23592968 | tf_op jit(solution)/shard_map/ppermute | solution.py:330
  3.2 6.4 %collective-permute-start = (s32[1,8]{1,0:T(1,128)}, s32[1,8]{1,0:T(1,128)S(1)}, u32[]{:S(2)}, u32[]{:S(2)}) collective-permute-start(s32[1,8]{1,0:T(1,128)} %param.6), channel_id=1, source_target_pairs={{0,8},{8,0},{1,9},{9,1},{2,10},{10,2},{3,11},{11,3},{4,12},{12,4},... | collective-permute-start | bytes 104 | tf_op jit(solution)/shard_map/ppermute | solution.py:331
  3.2 1.0 %copy-start = (bf16[20,10240]{1,0:T(8,128)(2,1)S(1)}, bf16[20,10240]{1,0:T(8,128)(2,1)}, u32[]{:S(2)}) copy-start(bf16[20,10240]{1,0:T(8,128)(2,1)} %weight_ref.1) | copy-start | bytes 1228804
  4.3 5.0 %copy-start.3 = (s32[1,8]{1,0:T(1,128)S(1)}, s32[1,8]{1,0:T(1,128)}, u32[]{:S(2)}) copy-start(s32[1,8]{1,0:T(1,128)} %param.6) | copy-start | bytes 100
  5.1 13.2 %all-to-all-start = ((bf16[16,20,640]{2,1,0:T(8,128)(2,1)}), bf16[16,20,640]{2,1,0:T(8,128)(2,1)S(1)}, u32[]{:S(2)}, u32[]{:S(2)}) async-start(bf16[16,20,640]{2,1,0:T(8,128)(2,1)} %regroup.1), calls=%async_computation | async-start | bytes 983040 | tf_op jit(solution)/shard_map/all_to_all | solution.py:333
  18.4 16.0 %collective-permute-start.1 = (bf16[320,640]{1,0:T(8,128)(2,1)S(1)}, bf16[320,640]{1,0:T(8,128)(2,1)S(1)}, u32[]{:S(2)}, u32[]{:S(2)}) collective-permute-start(bf16[320,640]{1,0:T(8,128)(2,1)S(1)} %reshape.42.refs_0_), channel_id=1, source_target_pairs={{0,32},{8,232},{32,64},{40,8},{64,96},{72,40},{96,128},{104,72},{1... | collective-permute-start | bytes 1228808 | tf_op jit(solution)/shard_map/ppermute | solution.py:75
  24.0 11.3 %collective-permute-start.2 = (bf16[320,640]{1,0:T(8,128)(2,1)S(1)}, bf16[320,640]{1,0:T(8,128)(2,1)S(1)}, u32[]{:S(2)}, u32[]{:S(2)}) collective-permute-start(bf16[320,640]{1,0:T(8,128)(2,1)S(1)} %reshape.42.refs_0_), channel_id=1, source_target_pairs={{32,0},{232,8},{64,32},{8,40},{96,64},{40,72},{128,96},{72,104},{1... | collective-permute-start | bytes 1228808 | tf_op jit(solution)/shard_map/ppermute | solution.py:78
  24.0 13.2 %collective-permute-start.6 = (bf16[320,640]{1,0:T(8,128)(2,1)S(1)}, bf16[320,640]{1,0:T(8,128)(2,1)S(1)}, u32[]{:S(2)}, u32[]{:S(2)}) collective-permute-start(bf16[320,640]{1,0:T(8,128)(2,1)S(1)} %reshape.42.refs_0_), channel_id=1, source_target_pairs={{0,16},{16,0},{1,17},{17,1},{2,18},{18,2},{3,19},{19,3},{4,20},{20... | collective-permute-start | bytes 1228808 | tf_op jit(solution)/shard_map/ppermute | solution.py:81
  35.3 9.9 %collective-permute-start.4 = (bf16[320,640]{1,0:T(8,128)(2,1)S(1)}, bf16[320,640]{1,0:T(8,128)(2,1)S(1)}, u32[]{:S(2)}, u32[]{:S(2)}) collective-permute-start(bf16[320,640]{1,0:T(8,128)(2,1)S(1)} %collective-permute-done.1.refs_0_), channel_id=1, source_target_pairs={{0,32},{8,232},{32,64},{40,8},{64,96},{72,40},{96,128},{104,72},{1... | collective-permute-start | bytes 1228808 | tf_op jit(solution)/shard_map/ppermute | solution.py:75
  37.2 12.2 %collective-permute-start.5 = (bf16[320,640]{1,0:T(8,128)(2,1)S(1)}, bf16[320,640]{1,0:T(8,128)(2,1)S(1)}, u32[]{:S(2)}, u32[]{:S(2)}) collective-permute-start(bf16[320,640]{1,0:T(8,128)(2,1)S(1)} %collective-permute-done.2.refs_2_), channel_id=1, source_target_pairs={{32,0},{232,8},{64,32},{8,40},{96,64},{40,72},{128,96},{72,104},{1... | collective-permute-start | bytes 1228808 | tf_op jit(solution)/shard_map/ppermute | solution.py:78
  37.2 14.0 %collective-permute-start.9 = (bf16[320,640]{1,0:T(8,128)(2,1)S(1)}, bf16[320,640]{1,0:T(8,128)(2,1)S(1)}, u32[]{:S(2)}, u32[]{:S(2)}) collective-permute-start(bf16[320,640]{1,0:T(8,128)(2,1)S(1)} %collective-permute-done.1.refs_0_), channel_id=1, source_target_pairs={{0,16},{16,0},{1,17},{17,1},{2,18},{18,2},{3,19},{19,3},{4,20},{20... | collective-permute-start | bytes 1228808 | tf_op jit(solution)/shard_map/ppermute | solution.py:81
  39.0 14.4 %collective-permute-start.10 = (bf16[320,640]{1,0:T(8,128)(2,1)S(1)}, bf16[320,640]{1,0:T(8,128)(2,1)S(1)}, u32[]{:S(2)}, u32[]{:S(2)}) collective-permute-start(bf16[320,640]{1,0:T(8,128)(2,1)S(1)} %collective-permute-done.6.refs_1_), channel_id=1, source_target_pairs={{32,0},{232,8},{64,32},{8,40},{96,64},{40,72},{128,96},{72,104},{1... | collective-permute-start | bytes 1228808 | tf_op jit(solution)/shard_map/ppermute | solution.py:78
  49.4 11.1 %collective-permute-start.7 = (bf16[320,640]{1,0:T(8,128)(2,1)S(1)}, bf16[320,640]{1,0:T(8,128)(2,1)S(1)}, u32[]{:S(2)}, u32[]{:S(2)}) collective-permute-start(bf16[320,640]{1,0:T(8,128)(2,1)S(1)} %collective-permute-done.4.refs_0_), channel_id=1, source_target_pairs={{0,32},{8,232},{32,64},{40,8},{64,96},{72,40},{96,128},{104,72},{1... | collective-permute-start | bytes 1228808 | tf_op jit(solution)/shard_map/ppermute | solution.py:75
  49.4 13.1 %collective-permute-start.8 = (bf16[320,640]{1,0:T(8,128)(2,1)S(1)}, bf16[320,640]{1,0:T(8,128)(2,1)S(1)}, u32[]{:S(2)}, u32[]{:S(2)}) collective-permute-start(bf16[320,640]{1,0:T(8,128)(2,1)S(1)} %collective-permute-done.5.refs_2_), channel_id=1, source_target_pairs={{32,0},{232,8},{64,32},{8,40},{96,64},{40,72},{128,96},{72,104},{1... | collective-permute-start | bytes 1228808 | tf_op jit(solution)/shard_map/ppermute | solution.py:78
  50.8 16.3 %collective-permute-start.14 = (bf16[320,640]{1,0:T(8,128)(2,1)S(1)}, bf16[320,640]{1,0:T(8,128)(2,1)S(1)}, u32[]{:S(2)}, u32[]{:S(2)}) collective-permute-start(bf16[320,640]{1,0:T(8,128)(2,1)S(1)} %collective-permute-done.5.refs_2_), channel_id=1, source_target_pairs={{0,16},{16,0},{1,17},{17,1},{2,18},{18,2},{3,19},{19,3},{4,20},{20... | collective-permute-start | bytes 1228808 | tf_op jit(solution)/shard_map/ppermute | solution.py:81
  51.2 14.0 %collective-permute-start.13 = (bf16[320,640]{1,0:T(8,128)(2,1)S(1)}, bf16[320,640]{1,0:T(8,128)(2,1)S(1)}, u32[]{:S(2)}, u32[]{:S(2)}) collective-permute-start(bf16[320,640]{1,0:T(8,128)(2,1)S(1)} %collective-permute-done.9.refs_1_), channel_id=1, source_target_pairs={{0,32},{8,232},{32,64},{40,8},{64,96},{72,40},{96,128},{104,72},{1... | collective-permute-start | bytes 1228808 | tf_op jit(solution)/shard_map/ppermute | solution.py:75
  62.5 12.1 %collective-permute-start.12 = (bf16[320,640]{1,0:T(8,128)(2,1)S(1)}, bf16[320,640]{1,0:T(8,128)(2,1)S(1)}, u32[]{:S(2)}, u32[]{:S(2)}) collective-permute-start(bf16[320,640]{1,0:T(8,128)(2,1)S(1)} %collective-permute-done.8.refs_2_), channel_id=1, source_target_pairs={{0,16},{16,0},{1,17},{17,1},{2,18},{18,2},{3,19},{19,3},{4,20},{20... | collective-permute-start | bytes 1228808 | tf_op jit(solution)/shard_map/ppermute | solution.py:81
  63.3 17.2 %collective-permute-start.11 = (bf16[320,640]{1,0:T(8,128)(2,1)S(1)}, bf16[320,640]{1,0:T(8,128)(2,1)S(1)}, u32[]{:S(2)}, u32[]{:S(2)}) collective-permute-start(bf16[320,640]{1,0:T(8,128)(2,1)S(1)} %collective-permute-done.8.refs_2_), channel_id=1, source_target_pairs={{32,0},{232,8},{64,32},{8,40},{96,64},{40,72},{128,96},{72,104},{1... | collective-permute-start | bytes 1228808 | tf_op jit(solution)/shard_map/ppermute | solution.py:78
  65.2 11.0 %collective-permute-start.16 = (bf16[320,640]{1,0:T(8,128)(2,1)S(1)}, bf16[320,640]{1,0:T(8,128)(2,1)S(1)}, u32[]{:S(2)}, u32[]{:S(2)}) collective-permute-start(bf16[320,640]{1,0:T(8,128)(2,1)S(1)} %collective-permute-done.13.refs_1_), channel_id=1, source_target_pairs={{0,32},{8,232},{32,64},{40,8},{64,96},{72,40},{96,128},{104,72},{1... | collective-permute-start | bytes 1228808 | tf_op jit(solution)/shard_map/ppermute | solution.py:75
  74.6 8.0 %copy-start.1 = (f32[128]{0:T(128)S(1)}, f32[128]{0:T(128)}, u32[]{:S(2)}) copy-start(f32[128]{0:T(128)} %param.8) | copy-start | bytes 1540
  74.6 8.0 %copy-start.2 = (f32[128]{0:T(128)S(1)}, f32[128]{0:T(128)}, u32[]{:S(2)}) copy-start(f32[128]{0:T(128)} %param.9) | copy-start | bytes 1540
  74.6 8.0 %collective-permute-start.15 = (bf16[320,640]{1,0:T(8,128)(2,1)S(1)}, bf16[320,640]{1,0:T(8,128)(2,1)S(1)}, u32[]{:S(2)}, u32[]{:S(2)}) collective-permute-start(bf16[320,640]{1,0:T(8,128)(2,1)S(1)} %collective-permute-done.12.refs_3_), channel_id=1, source_target_pairs={{32,0},{232,8},{64,32},{8,40},{96,64},{40,72},{128,96},{72,104},{1... | collective-permute-start | bytes 1228808 | tf_op jit(solution)/shard_map/ppermute | solution.py:78
  85.1 3.9 %collective-permute-start.17 = (bf16[768,640]{1,0:T(8,128)(2,1)S(1)}, bf16[768,640]{1,0:T(8,128)(2,1)S(1)}, u32[]{:S(2)}, u32[]{:S(2)}) collective-permute-start(bf16[768,640]{1,0:T(8,128)(2,1)S(1)} %get-tuple-element.76), channel_id=1, source_target_pairs={{0,8},{8,0},{1,9},{9,1},{2,10},{10,2},{3,11},{11,3},{4,12},{12,4},... | collective-permute-start | bytes 2949128 | tf_op jit(solution)/shard_map/ppermute | solution.py:347

commit v6 on v5

--- a/solution.py
+++ b/solution.py
@@ -82,7 +82,9 @@
 
     other = across(block)
     up1, down1 = up(block), down(block)
-    up1, down1, ahead = lax.optimization_barrier((up1, down1, ahead))
+    held, other_held, *tables = ahead
+    up1, down1, held, tables = lax.optimization_barrier((up1, down1, held, tables))
+    ahead = (held, other_held, *tables)
     held = ahead[:2]
     up2, down2 = up(up1), down(down1)
     up1, other = lax.optimization_barrier((up1, other))

time: 94.3 us -> 94.3 us (level)
  waiting for transfers between devices: 28.2 us -> 22.9 us
  starting transfers between devices: 26.6 us -> 31.8 us
    ppermute x5, waiting for transfers between devices: 9.72 us -> 5.12 us  [up(): return lax.ppermute(array, ('z', 'c'), UP)]
    ppermute x4, starting transfers between devices: 5.45 us -> 9.21 us  [across(): return lax.ppermute(array, 'xh', SWAP)]
    ppermute x4, waiting for transfers between devices: 3.23 us -> 0.43 us  [across(): return lax.ppermute(array, 'xh', SWAP)]
    ppermute x6, waiting for transfers between devices: 10.2 us -> 12.3 us  [down(): return lax.ppermute(array, ('z', 'c'), DOWN)]
where the time goes in v6:
time: 94.3 us; the launch traced here: 94 us
  Pallas kernels  33.7 us (36%)
  starting transfers between devices  31.8 us (34%)
  waiting for transfers between devices  22.9 us (24%)
  other arithmetic  4 us (4%)
  local copies, waits for them, and re-layouts  1.28 us (1%)
    pallas_call x4, Pallas kernels, project_early(): pl.pallas_call(kernel, out_shape=(shape, shape), in_specs=[SMEM] + [VMEM]...  15.3 us
    ppermute x6, waiting for transfers between devices, down(): return lax.ppermute(array, ('z', 'c'), DOWN)  12.3 us
    ppermute x5, starting transfers between devices, up(): return lax.ppermute(array, ('z', 'c'), UP)  10.9 us
    ppermute x4, starting transfers between devices, across(): return lax.ppermute(array, 'xh', SWAP)  9.21 us
    pallas_call x2, Pallas kernels, hold_tokens(): pl.pallas_call(kernel, out_shape=pltpu.VMEM((NZ, ROWS, DEPTH), jnp.bfloat...  7.83 us
    ppermute x5, waiting for transfers between devices, up(): return lax.ppermute(array, ('z', 'c'), UP)  5.12 us
    all_to_all x1, waiting for transfers between devices, shards(): lax.all_to_all(spread, ('c',) + TENSOR, split_axis=0, concat_axis=0, tile...  5 us
    pallas_call x2, Pallas kernels, project_late(): pl.pallas_call(kernel, out_shape=(shape, weight_shape) if first else shap...  4.92 us
  transfers between devices with their start and end apart: 19, of which 11 were waited for; matrix products, arithmetic and copies ran while one was open for 5% of the time, Pallas kernels for 28%

profile of v6, /device:TPU:1, one launch (start us, length us, event | category | flops | bytes accessed | tf_op | source)
XLA Modules:
  0.0 94.0 jit_solution(18392391883294117026)
XLA Ops:
  0.0 3.2 %collective-permute-start.6 = (bf16[768,5120]{1,0:T(8,128)(2,1)}, bf16[768,5120]{1,0:T(8,128)(2,1)}, u32[]{:S(2)}, u32[]{:S(2)}) collective-permute-start(bf16[768,5120]{1,0:T(8,128)(2,1)} %token_ref.1), channel_id=1, source_target_pairs={{0,8},{8,0},{1,9},{9,1},{2,10},{10,2},{3,11},{11,3},{4,12},{12,4},... | collective-permute-start | bytes 23592968 | tf_op jit(solution)/shard_map/ppermute | solution.py:332
  3.2 1.0 %copy-done = bf16[20,10240]{1,0:T(8,128)(2,1)S(1)} copy-done((bf16[20,10240]{1,0:T(8,128)(2,1)S(1)}, bf16[20,10240]{1,0:T(8,128)(2,1)}, u32[]{:S(2)}) %copy-start) | copy-done | bytes 409624
  5.1 4.2 %all-to-all-start = ((bf16[16,20,640]{2,1,0:T(8,128)(2,1)}), bf16[16,20,640]{2,1,0:T(8,128)(2,1)S(1)}, u32[]{:S(2)}, u32[]{:S(2)}) async-start(bf16[16,20,640]{2,1,0:T(8,128)(2,1)} %regroup.1), calls=%async_computation | async-start | bytes 983040 | tf_op jit(solution)/shard_map/all_to_all | solution.py:335
  9.9 2.8 %fusion.1 = (f32[768,64]{1,0:T(8,128)S(1)}, f32[768,64]{1,0:T(8,128)S(1)}, f32[768,64]{1,0:T(8,128)S(1)}, f32[768,64]{1,0:T(8,128)S(1)}, f32[768,64]{1,0:T(8,128)S(1)}, /*index=5*/f32[768,64]{1,0:T(8,128)S(1)}) fusion(f32[64]{0:T(128)S(1)} %multiply_power_fusion, f32[768]{0:T(1024)S(1)} %subtract_convert_fusion, f32[768]{0:T(1024)S(1)} %subtract_convert_fusion.1), kind=kLoop, calls=%fused_computation.9 | loop fusion | flops 196608 | bytes 1186048 | tf_op jit(solution)/shard_map/neg | solution.py:48
  13.3 5.0 %all-to-all-done = bf16[16,20,640]{2,1,0:T(8,128)(2,1)S(1)} async-done(((bf16[16,20,640]{2,1,0:T(8,128)(2,1)}), bf16[16,20,640]{2,1,0:T(8,128)(2,1)S(1)}, u32[]{:S(2)}, u32[]{:S(2)}) %all-to-all-start) | async-done | bytes 409632 | tf_op jit(solution)/shard_map/all_to_all | solution.py:335
  18.4 5.7 %collective-permute-start.1 = (bf16[320,640]{1,0:T(8,128)(2,1)S(1)}, bf16[320,640]{1,0:T(8,128)(2,1)S(1)}, u32[]{:S(2)}, u32[]{:S(2)}) collective-permute-start(bf16[320,640]{1,0:T(8,128)(2,1)S(1)} %reshape.42.refs_0_), channel_id=1, source_target_pairs={{0,32},{8,232},{32,64},{40,8},{64,96},{72,40},{96,128},{104,72},{1... | collective-permute-start | bytes 1228808 | tf_op jit(solution)/shard_map/ppermute | solution.py:75
  24.0 2.5 %collective-permute-start.5 = (bf16[320,640]{1,0:T(8,128)(2,1)S(1)}, bf16[320,640]{1,0:T(8,128)(2,1)S(1)}, u32[]{:S(2)}, u32[]{:S(2)}) collective-permute-start(bf16[320,640]{1,0:T(8,128)(2,1)S(1)} %reshape.42.refs_0_), channel_id=1, source_target_pairs={{0,16},{16,0},{1,17},{17,1},{2,18},{18,2},{3,19},{19,3},{4,20},{20... | collective-permute-start | bytes 1228808 | tf_op jit(solution)/shard_map/ppermute | solution.py:81
  26.5 3.9 %hold_tokens.2.refs_2_.refs_4_.refs_1_ = bf16[8,768,640]{2,1,0:T(8,128)(2,1)S(1)} custom-call(s32[3]{0:T(128)S(1)} %pad_add_fusion.place_ref, bf16[768,5120]{1,0:T(8,128)(2,1)} %token_ref.1), custom_call_target="tpu_custom_call" | custom-call | bytes 16777216 | tf_op jit(solution)/shard_map/hold_tokens/pallas_call | solution.py:160
  30.5 1.1 %collective-permute-done.1.refs_0_ = bf16[320,640]{1,0:T(8,128)(2,1)S(1)} collective-permute-done((bf16[320,640]{1,0:T(8,128)(2,1)S(1)}, bf16[320,640]{1,0:T(8,128)(2,1)S(1)}, u32[]{:S(2)}, u32[]{:S(2)}) %collective-permute-start.1) | collective-permute-done | bytes 409632 | tf_op jit(solution)/shard_map/ppermute | solution.py:75
  31.6 3.7 %collective-permute-done.2.refs_2_ = bf16[320,640]{1,0:T(8,128)(2,1)S(1)} collective-permute-done((bf16[320,640]{1,0:T(8,128)(2,1)S(1)}, bf16[320,640]{1,0:T(8,128)(2,1)S(1)}, u32[]{:S(2)}, u32[]{:S(2)}) %collective-permute-start.2) | collective-permute-done | bytes 409632 | tf_op jit(solution)/shard_map/ppermute | solution.py:78
  35.4 1.3 %collective-permute-start.4 = (bf16[320,640]{1,0:T(8,128)(2,1)S(1)}, bf16[320,640]{1,0:T(8,128)(2,1)S(1)}, u32[]{:S(2)}, u32[]{:S(2)}) collective-permute-start(bf16[320,640]{1,0:T(8,128)(2,1)S(1)} %collective-permute-done.2.refs_2_), channel_id=1, source_target_pairs={{32,0},{232,8},{64,32},{8,40},{96,64},{40,72},{128,96},{72,104},{1... | collective-permute-start | bytes 1228808 | tf_op jit(solution)/shard_map/ppermute | solution.py:78
  36.8 2.3 %collective-permute-start.9 = (bf16[320,640]{1,0:T(8,128)(2,1)S(1)}, bf16[320,640]{1,0:T(8,128)(2,1)S(1)}, u32[]{:S(2)}, u32[]{:S(2)}) collective-permute-start(bf16[320,640]{1,0:T(8,128)(2,1)S(1)} %collective-permute-done.1.refs_0_), channel_id=1, source_target_pairs={{0,16},{16,0},{1,17},{17,1},{2,18},{18,2},{3,19},{19,3},{4,20},{20... | collective-permute-start | bytes 1228808 | tf_op jit(solution)/shard_map/ppermute | solution.py:81
  39.1 3.9 %hold_tokens.3.refs_3_.refs_5_.refs_2_ = bf16[8,768,640]{2,1,0:T(8,128)(2,1)S(1)} custom-call(s32[3]{0:T(128)S(1)} %pad_add_fusion.place_ref, bf16[768,5120]{1,0:T(8,128)(2,1)} %collective-permute-done.6.token_ref), custom_call_target="tpu_custom_call" | custom-call | bytes 16777216 | tf_op jit(solution)/shard_map/hold_tokens/pallas_call | solution.py:160
  43.0 2.5 %project_early.4 = (f32[768,640]{1,0:T(8,128)S(1)}, f32[768,640]{1,0:T(8,128)S(1)}) custom-call(s32[3]{0:T(128)S(1)} %pad_add_fusion.place_ref, bf16[320,640]{1,0:T(8,128)(2,1)S(1)} %reshape.42.refs_0_, bf16[320,640]{1,0:T(8,128)(2,1)S(1)} %collective-permute-done.5.refs_1_, bf16[8,768,640]{2,1,0:T(8,128)(2,1)S(1)} %hold_tokens.2.refs_2_.refs_4_.refs_1_, ...), custom_call_target="tpu_custom_call" | custom-call | flops 1258291200 | bytes 18874368 | tf_op jit(solution)/shard_map/project_early/pallas_call | solution.py:191
  45.5 1.2 %collective-permute-done.3.refs_0_ = bf16[320,640]{1,0:T(8,128)(2,1)S(1)} collective-permute-done((bf16[320,640]{1,0:T(8,128)(2,1)S(1)}, bf16[320,640]{1,0:T(8,128)(2,1)S(1)}, u32[]{:S(2)}, u32[]{:S(2)}) %collective-permute-start.3) | collective-permute-done | bytes 409632 | tf_op jit(solution)/shard_map/ppermute | solution.py:75
  47.4 1.1 %collective-permute-start.7 = (bf16[320,640]{1,0:T(8,128)(2,1)S(1)}, bf16[320,640]{1,0:T(8,128)(2,1)S(1)}, u32[]{:S(2)}, u32[]{:S(2)}) collective-permute-start(bf16[320,640]{1,0:T(8,128)(2,1)S(1)} %collective-permute-done.3.refs_0_), channel_id=1, source_target_pairs={{0,32},{8,232},{32,64},{40,8},{64,96},{72,40},{96,128},{104,72},{1... | collective-permute-start | bytes 1228808 | tf_op jit(solution)/shard_map/ppermute | solution.py:75
  48.8 2.3 %collective-permute-start.13 = (bf16[320,640]{1,0:T(8,128)(2,1)S(1)}, bf16[320,640]{1,0:T(8,128)(2,1)S(1)}, u32[]{:S(2)}, u32[]{:S(2)}) collective-permute-start(bf16[320,640]{1,0:T(8,128)(2,1)S(1)} %collective-permute-done.9.refs_1_), channel_id=1, source_target_pairs={{0,32},{8,232},{32,64},{40,8},{64,96},{72,40},{96,128},{104,72},{1... | collective-permute-start | bytes 1228808 | tf_op jit(solution)/shard_map/ppermute | solution.py:75
  51.1 1.3 %collective-permute-start.14 = (bf16[320,640]{1,0:T(8,128)(2,1)S(1)}, bf16[320,640]{1,0:T(8,128)(2,1)S(1)}, u32[]{:S(2)}, u32[]{:S(2)}) collective-permute-start(bf16[320,640]{1,0:T(8,128)(2,1)S(1)} %collective-permute-done.4.refs_2_), channel_id=1, source_target_pairs={{0,16},{16,0},{1,17},{17,1},{2,18},{18,2},{3,19},{19,3},{4,20},{20... | collective-permute-start | bytes 1228808 | tf_op jit(solution)/shard_map/ppermute | solution.py:81
  52.5 4.3 %project_early.5 = (f32[768,640]{1,0:T(8,128)S(1)}, f32[768,640]{1,0:T(8,128)S(1)}) custom-call(s32[3]{0:T(128)S(1)} %pad_add_fusion.place_ref, bf16[320,640]{1,0:T(8,128)(2,1)S(1)} %collective-permute-done.1.refs_0_, bf16[320,640]{1,0:T(8,128)(2,1)S(1)} %collective-permute-done.9.refs_1_, ...), custom_call_target="tpu_custom_call", output_to_operand_aliasing={{0}: (7, {}), {1}: (8, {})} | custom-call | flops 2516582400 | bytes 18874368 | tf_op jit(solution)/shard_map/project_early/pallas_call | solution.py:191
  56.7 2.5 %collective-permute-done.8.refs_2_ = bf16[320,640]{1,0:T(8,128)(2,1)S(1)} collective-permute-done((bf16[320,640]{1,0:T(8,128)(2,1)S(1)}, bf16[320,640]{1,0:T(8,128)(2,1)S(1)}, u32[]{:S(2)}, u32[]{:S(2)}) %collective-permute-start.8) | collective-permute-done | bytes 409632 | tf_op jit(solution)/shard_map/ppermute | solution.py:78
  59.3 3.1 %collective-permute-start.12 = (bf16[320,640]{1,0:T(8,128)(2,1)S(1)}, bf16[320,640]{1,0:T(8,128)(2,1)S(1)}, u32[]{:S(2)}, u32[]{:S(2)}) collective-permute-start(bf16[320,640]{1,0:T(8,128)(2,1)S(1)} %collective-permute-done.8.refs_2_), channel_id=1, source_target_pairs={{0,16},{16,0},{1,17},{17,1},{2,18},{18,2},{3,19},{19,3},{4,20},{20... | collective-permute-start | bytes 1228808 | tf_op jit(solution)/shard_map/ppermute | solution.py:81
  62.4 1.3 %collective-permute-done.13.refs_1_ = bf16[320,640]{1,0:T(8,128)(2,1)S(1)} collective-permute-done((bf16[320,640]{1,0:T(8,128)(2,1)S(1)}, bf16[320,640]{1,0:T(8,128)(2,1)S(1)}, u32[]{:S(2)}, u32[]{:S(2)}) %collective-permute-start.13) | collective-permute-done | bytes 409632 | tf_op jit(solution)/shard_map/ppermute | solution.py:75
  63.7 1.7 %collective-permute-start.16 = (bf16[320,640]{1,0:T(8,128)(2,1)S(1)}, bf16[320,640]{1,0:T(8,128)(2,1)S(1)}, u32[]{:S(2)}, u32[]{:S(2)}) collective-permute-start(bf16[320,640]{1,0:T(8,128)(2,1)S(1)} %collective-permute-done.13.refs_1_), channel_id=1, source_target_pairs={{0,32},{8,232},{32,64},{40,8},{64,96},{72,40},{96,128},{104,72},{1... | collective-permute-start | bytes 1228808 | tf_op jit(solution)/shard_map/ppermute | solution.py:75
  65.4 4.3 %project_early.6 = (f32[768,640]{1,0:T(8,128)S(1)}, f32[768,640]{1,0:T(8,128)S(1)}) custom-call(s32[3]{0:T(128)S(1)} %pad_add_fusion.place_ref, bf16[320,640]{1,0:T(8,128)(2,1)S(1)} %collective-permute-done.3.refs_0_, bf16[320,640]{1,0:T(8,128)(2,1)S(1)} %collective-permute-done.13.refs_1_, ...), custom_call_target="tpu_custom_call", output_to_operand_aliasing={{0}: (7, {}), {1}: (8, {})} | custom-call | flops 2516582400 | bytes 18874368 | tf_op jit(solution)/shard_map/project_early/pallas_call | solution.py:191
  70.1 0.9 collective-permute-start.15
  71.0 1.5 %collective-permute-done.16.refs_1_ = bf16[320,640]{1,0:T(8,128)(2,1)S(1)} collective-permute-done((bf16[320,640]{1,0:T(8,128)(2,1)S(1)}, bf16[320,640]{1,0:T(8,128)(2,1)S(1)}, u32[]{:S(2)}, u32[]{:S(2)}) %collective-permute-start.16) | collective-permute-done | bytes 409632 | tf_op jit(solution)/shard_map/ppermute | solution.py:75
  72.4 4.3 %project_early.7 = (f32[768,640]{1,0:T(8,128)S(1)}, f32[768,640]{1,0:T(8,128)S(1)}) custom-call(s32[3]{0:T(128)S(1)} %pad_add_fusion.place_ref, bf16[320,640]{1,0:T(8,128)(2,1)S(1)} %collective-permute-done.7.refs_0_, bf16[320,640]{1,0:T(8,128)(2,1)S(1)} %collective-permute-done.16.refs_1_, ...), custom_call_target="tpu_custom_call", output_to_operand_aliasing={{0}: (7, {}), {1}: (8, {})} | custom-call | flops 2516582400 | bytes 18874368 | tf_op jit(solution)/shard_map/project_early/pallas_call | solution.py:191
  77.0 5.1 %collective-permute-done.15.refs_1_ = bf16[320,640]{1,0:T(8,128)(2,1)S(1)} collective-permute-done((bf16[320,640]{1,0:T(8,128)(2,1)S(1)}, bf16[320,640]{1,0:T(8,128)(2,1)S(1)}, u32[]{:S(2)}, u32[]{:S(2)}) %collective-permute-start.15) | collective-permute-done | bytes 409632 | tf_op jit(solution)/shard_map/ppermute | solution.py:78
  82.2 2.5 %project_late.2 = (bf16[768,640]{1,0:T(8,128)(2,1)S(1)}, bf16[640,640]{1,0:T(8,128)(2,1)S(1)}) custom-call(s32[3]{0:T(128)S(1)} %pad_add_fusion.place_ref, bf16[320,640]{1,0:T(8,128)(2,1)S(1)} %collective-permute-done.11.refs_0_, bf16[320,640]{1,0:T(8,128)(2,1)S(1)} %collective-permute-done.15.refs_1_, ...), custom_call_target="tpu_custom_call" | custom-call | flops 629145600 | bytes 9437184 | tf_op jit(solution)/shard_map/project_late/pallas_call | solution.py:250
  84.7 1.7 %collective-permute-start.17 = (bf16[768,640]{1,0:T(8,128)(2,1)S(1)}, bf16[768,640]{1,0:T(8,128)(2,1)S(1)}, u32[]{:S(2)}, u32[]{:S(2)}) collective-permute-start(bf16[768,640]{1,0:T(8,128)(2,1)S(1)} %get-tuple-element.74), channel_id=1, source_target_pairs={{0,8},{8,0},{1,9},{9,1},{2,10},{10,2},{3,11},{11,3},{4,12},{12,4},... | collective-permute-start | bytes 2949128 | tf_op jit(solution)/shard_map/ppermute | solution.py:349
  86.6 2.4 %project_late.3.own_ref = bf16[768,640]{1,0:T(8,128)(2,1)S(1)} custom-call(s32[3]{0:T(128)S(1)} %pad_add_fusion.place_ref, bf16[640,640]{1,0:T(8,128)(2,1)S(1)} %get-tuple-element.70.refs_0_, bf16[8,768,640]{2,1,0:T(8,128)(2,1)S(1)} %hold_tokens.2.refs_2_.refs_4_.refs_1_, f32[768,640]{1,0:T(8,128)S(1)} %get-tuple-element.71.refs_2_, ...), custom_call_target="tpu_custom_call" | custom-call | flops 629145600 | bytes 9437184 | tf_op jit(solution)/shard_map/project_late/pallas_call | solution.py:250
  89.0 4.9 %attend.1 = bf16[768,1024]{1,0:T(8,128)(2,1)} custom-call(s32[3]{0:T(128)S(1)} %pad_add_fusion.place_ref, bf16[768,640]{1,0:T(8,128)(2,1)S(1)} %project_late.3.own_ref, bf16[768,640]{1,0:T(8,128)(2,1)S(1)} %collective-permute-done.17.received_ref, s32[768,1]{1,0:T(8,128)S(1)} %reduce_max.23.start_ref), custom_call_target="tpu_custom_call" | custom-call | flops 1610612736 | bytes 4194304 | tf_op jit(solution)/shard_map/attend/pallas_call | solution.py:309
  (39 shorter events, 4.2 us)
Async XLA Ops:
  0.0 39.1 %collective-permute-start.6 = (bf16[768,5120]{1,0:T(8,128)(2,1)}, bf16[768,5120]{1,0:T(8,128)(2,1)}, u32[]{:S(2)}, u32[]{:S(2)}) collective-permute-start(bf16[768,5120]{1,0:T(8,128)(2,1)} %token_ref.1), channel_id=1, source_target_pairs={{0,8},{8,0},{1,9},{9,1},{2,10},{10,2},{3,11},{11,3},{4,12},{12,4},... | collective-permute-start | bytes 23592968 | tf_op jit(solution)/shard_map/ppermute | solution.py:332
  3.2 6.4 %collective-permute-start = (s32[1,8]{1,0:T(1,128)}, s32[1,8]{1,0:T(1,128)S(1)}, u32[]{:S(2)}, u32[]{:S(2)}) collective-permute-start(s32[1,8]{1,0:T(1,128)} %param.6), channel_id=1, source_target_pairs={{0,8},{8,0},{1,9},{9,1},{2,10},{10,2},{3,11},{11,3},{4,12},{12,4},... | collective-permute-start | bytes 104 | tf_op jit(solution)/shard_map/ppermute | solution.py:333
  3.2 1.0 %copy-start = (bf16[20,10240]{1,0:T(8,128)(2,1)S(1)}, bf16[20,10240]{1,0:T(8,128)(2,1)}, u32[]{:S(2)}) copy-start(bf16[20,10240]{1,0:T(8,128)(2,1)} %weight_ref.1) | copy-start | bytes 1228804
  4.3 5.0 %copy-start.3 = (s32[1,8]{1,0:T(1,128)S(1)}, s32[1,8]{1,0:T(1,128)}, u32[]{:S(2)}) copy-start(s32[1,8]{1,0:T(1,128)} %param.6) | copy-start | bytes 100
  5.1 13.2 %all-to-all-start = ((bf16[16,20,640]{2,1,0:T(8,128)(2,1)}), bf16[16,20,640]{2,1,0:T(8,128)(2,1)S(1)}, u32[]{:S(2)}, u32[]{:S(2)}) async-start(bf16[16,20,640]{2,1,0:T(8,128)(2,1)} %regroup.1), calls=%async_computation | async-start | bytes 983040 | tf_op jit(solution)/shard_map/all_to_all | solution.py:335
  18.4 13.2 %collective-permute-start.1 = (bf16[320,640]{1,0:T(8,128)(2,1)S(1)}, bf16[320,640]{1,0:T(8,128)(2,1)S(1)}, u32[]{:S(2)}, u32[]{:S(2)}) collective-permute-start(bf16[320,640]{1,0:T(8,128)(2,1)S(1)} %reshape.42.refs_0_), channel_id=1, source_target_pairs={{0,32},{8,232},{32,64},{40,8},{64,96},{72,40},{96,128},{104,72},{1... | collective-permute-start | bytes 1228808 | tf_op jit(solution)/shard_map/ppermute | solution.py:75
  24.0 11.3 %collective-permute-start.2 = (bf16[320,640]{1,0:T(8,128)(2,1)S(1)}, bf16[320,640]{1,0:T(8,128)(2,1)S(1)}, u32[]{:S(2)}, u32[]{:S(2)}) collective-permute-start(bf16[320,640]{1,0:T(8,128)(2,1)S(1)} %reshape.42.refs_0_), channel_id=1, source_target_pairs={{32,0},{232,8},{64,32},{8,40},{96,64},{40,72},{128,96},{72,104},{1... | collective-permute-start | bytes 1228808 | tf_op jit(solution)/shard_map/ppermute | solution.py:78
  24.0 12.7 %collective-permute-start.5 = (bf16[320,640]{1,0:T(8,128)(2,1)S(1)}, bf16[320,640]{1,0:T(8,128)(2,1)S(1)}, u32[]{:S(2)}, u32[]{:S(2)}) collective-permute-start(bf16[320,640]{1,0:T(8,128)(2,1)S(1)} %reshape.42.refs_0_), channel_id=1, source_target_pairs={{0,16},{16,0},{1,17},{17,1},{2,18},{18,2},{3,19},{19,3},{4,20},{20... | collective-permute-start | bytes 1228808 | tf_op jit(solution)/shard_map/ppermute | solution.py:81
  35.3 11.4 %collective-permute-start.3 = (bf16[320,640]{1,0:T(8,128)(2,1)S(1)}, bf16[320,640]{1,0:T(8,128)(2,1)S(1)}, u32[]{:S(2)}, u32[]{:S(2)}) collective-permute-start(bf16[320,640]{1,0:T(8,128)(2,1)S(1)} %collective-permute-done.1.refs_0_), channel_id=1, source_target_pairs={{0,32},{8,232},{32,64},{40,8},{64,96},{72,40},{96,128},{104,72},{1... | collective-permute-start | bytes 1228808 | tf_op jit(solution)/shard_map/ppermute | solution.py:75
  35.4 11.9 %collective-permute-start.4 = (bf16[320,640]{1,0:T(8,128)(2,1)S(1)}, bf16[320,640]{1,0:T(8,128)(2,1)S(1)}, u32[]{:S(2)}, u32[]{:S(2)}) collective-permute-start(bf16[320,640]{1,0:T(8,128)(2,1)S(1)} %collective-permute-done.2.refs_2_), channel_id=1, source_target_pairs={{32,0},{232,8},{64,32},{8,40},{96,64},{40,72},{128,96},{72,104},{1... | collective-permute-start | bytes 1228808 | tf_op jit(solution)/shard_map/ppermute | solution.py:78
  36.8 12.1 %collective-permute-start.9 = (bf16[320,640]{1,0:T(8,128)(2,1)S(1)}, bf16[320,640]{1,0:T(8,128)(2,1)S(1)}, u32[]{:S(2)}, u32[]{:S(2)}) collective-permute-start(bf16[320,640]{1,0:T(8,128)(2,1)S(1)} %collective-permute-done.1.refs_0_), channel_id=1, source_target_pairs={{0,16},{16,0},{1,17},{17,1},{2,18},{18,2},{3,19},{19,3},{4,20},{20... | collective-permute-start | bytes 1228808 | tf_op jit(solution)/shard_map/ppermute | solution.py:81
  39.0 13.4 %collective-permute-start.10 = (bf16[320,640]{1,0:T(8,128)(2,1)S(1)}, bf16[320,640]{1,0:T(8,128)(2,1)S(1)}, u32[]{:S(2)}, u32[]{:S(2)}) collective-permute-start(bf16[320,640]{1,0:T(8,128)(2,1)S(1)} %collective-permute-done.5.refs_1_), channel_id=1, source_target_pairs={{32,0},{232,8},{64,32},{8,40},{96,64},{40,72},{128,96},{72,104},{1... | collective-permute-start | bytes 1228808 | tf_op jit(solution)/shard_map/ppermute | solution.py:78
  47.4 9.4 %collective-permute-start.7 = (bf16[320,640]{1,0:T(8,128)(2,1)S(1)}, bf16[320,640]{1,0:T(8,128)(2,1)S(1)}, u32[]{:S(2)}, u32[]{:S(2)}) collective-permute-start(bf16[320,640]{1,0:T(8,128)(2,1)S(1)} %collective-permute-done.3.refs_0_), channel_id=1, source_target_pairs={{0,32},{8,232},{32,64},{40,8},{64,96},{72,40},{96,128},{104,72},{1... | collective-permute-start | bytes 1228808 | tf_op jit(solution)/shard_map/ppermute | solution.py:75
  48.5 10.8 %collective-permute-start.8 = (bf16[320,640]{1,0:T(8,128)(2,1)S(1)}, bf16[320,640]{1,0:T(8,128)(2,1)S(1)}, u32[]{:S(2)}, u32[]{:S(2)}) collective-permute-start(bf16[320,640]{1,0:T(8,128)(2,1)S(1)} %collective-permute-done.4.refs_2_), channel_id=1, source_target_pairs={{32,0},{232,8},{64,32},{8,40},{96,64},{40,72},{128,96},{72,104},{1... | collective-permute-start | bytes 1228808 | tf_op jit(solution)/shard_map/ppermute | solution.py:78
  48.8 14.9 %collective-permute-start.13 = (bf16[320,640]{1,0:T(8,128)(2,1)S(1)}, bf16[320,640]{1,0:T(8,128)(2,1)S(1)}, u32[]{:S(2)}, u32[]{:S(2)}) collective-permute-start(bf16[320,640]{1,0:T(8,128)(2,1)S(1)} %collective-permute-done.9.refs_1_), channel_id=1, source_target_pairs={{0,32},{8,232},{32,64},{40,8},{64,96},{72,40},{96,128},{104,72},{1... | collective-permute-start | bytes 1228808 | tf_op jit(solution)/shard_map/ppermute | solution.py:75
  51.1 14.2 %collective-permute-start.14 = (bf16[320,640]{1,0:T(8,128)(2,1)S(1)}, bf16[320,640]{1,0:T(8,128)(2,1)S(1)}, u32[]{:S(2)}, u32[]{:S(2)}) collective-permute-start(bf16[320,640]{1,0:T(8,128)(2,1)S(1)} %collective-permute-done.4.refs_2_), channel_id=1, source_target_pairs={{0,16},{16,0},{1,17},{17,1},{2,18},{18,2},{3,19},{19,3},{4,20},{20... | collective-permute-start | bytes 1228808 | tf_op jit(solution)/shard_map/ppermute | solution.py:81
  59.3 10.8 %collective-permute-start.12 = (bf16[320,640]{1,0:T(8,128)(2,1)S(1)}, bf16[320,640]{1,0:T(8,128)(2,1)S(1)}, u32[]{:S(2)}, u32[]{:S(2)}) collective-permute-start(bf16[320,640]{1,0:T(8,128)(2,1)S(1)} %collective-permute-done.8.refs_2_), channel_id=1, source_target_pairs={{0,16},{16,0},{1,17},{17,1},{2,18},{18,2},{3,19},{19,3},{4,20},{20... | collective-permute-start | bytes 1228808 | tf_op jit(solution)/shard_map/ppermute | solution.py:81
  63.7 8.7 %collective-permute-start.16 = (bf16[320,640]{1,0:T(8,128)(2,1)S(1)}, bf16[320,640]{1,0:T(8,128)(2,1)S(1)}, u32[]{:S(2)}, u32[]{:S(2)}) collective-permute-start(bf16[320,640]{1,0:T(8,128)(2,1)S(1)} %collective-permute-done.13.refs_1_), channel_id=1, source_target_pairs={{0,32},{8,232},{32,64},{40,8},{64,96},{72,40},{96,128},{104,72},{1... | collective-permute-start | bytes 1228808 | tf_op jit(solution)/shard_map/ppermute | solution.py:75
  65.4 11.7 %collective-permute-start.11 = (bf16[320,640]{1,0:T(8,128)(2,1)S(1)}, bf16[320,640]{1,0:T(8,128)(2,1)S(1)}, u32[]{:S(2)}, u32[]{:S(2)}) collective-permute-start(bf16[320,640]{1,0:T(8,128)(2,1)S(1)} %collective-permute-done.8.refs_2_), channel_id=1, source_target_pairs={{32,0},{232,8},{64,32},{8,40},{96,64},{40,72},{128,96},{72,104},{1... | collective-permute-start | bytes 1228808 | tf_op jit(solution)/shard_map/ppermute | solution.py:78
  70.1 12.1 %copy-start.1 = (f32[128]{0:T(128)S(1)}, f32[128]{0:T(128)}, u32[]{:S(2)}) copy-start(f32[128]{0:T(128)} %param.8) | copy-start | bytes 1540
  70.1 12.1 %copy-start.2 = (f32[128]{0:T(128)S(1)}, f32[128]{0:T(128)}, u32[]{:S(2)}) copy-start(f32[128]{0:T(128)} %param.9) | copy-start | bytes 1540
  70.1 12.1 %collective-permute-start.15 = (bf16[320,640]{1,0:T(8,128)(2,1)S(1)}, bf16[320,640]{1,0:T(8,128)(2,1)S(1)}, u32[]{:S(2)}, u32[]{:S(2)}) collective-permute-start(bf16[320,640]{1,0:T(8,128)(2,1)S(1)} %collective-permute-done.12.refs_3_), channel_id=1, source_target_pairs={{32,0},{232,8},{64,32},{8,40},{96,64},{40,72},{128,96},{72,104},{1... | collective-permute-start | bytes 1228808 | tf_op jit(solution)/shard_map/ppermute | solution.py:78
  84.7 4.3 %collective-permute-start.17 = (bf16[768,640]{1,0:T(8,128)(2,1)S(1)}, bf16[768,640]{1,0:T(8,128)(2,1)S(1)}, u32[]{:S(2)}, u32[]{:S(2)}) collective-permute-start(bf16[768,640]{1,0:T(8,128)(2,1)S(1)} %get-tuple-element.74), channel_id=1, source_target_pairs={{0,8},{8,0},{1,9},{9,1},{2,10},{10,2},{3,11},{11,3},{4,12},{12,4},... | collective-permute-start | bytes 2949128 | tf_op jit(solution)/shard_map/ppermute | solution.py:349

commit v7 on v6

--- a/solution.py
+++ b/solution.py
@@ -100,7 +100,7 @@
     ]
     totals = project_early(place, nearest, held, totals)
     up3, down3, totals = lax.optimization_barrier((up3, down3, totals))
-    down4 = down(down3)
+    up4 = up(up3)
     other_down3 = across(down3)
     other_up3 = up(other_up2)
     second = [
@@ -113,7 +113,7 @@
         (up3, -3, 0, 0), (other_up3, -3, 1, 0), (down3, 3, 0, 0), (other_down3, 3, 1, 0),
     ]
     totals = project_early(place, third, held, totals)
-    last = [(down4, 4, 0, 0), (other_down4, 4, 1, 0)]
+    last = [(up4, 4, 0, 0), (other_down4, 4, 1, 0)]
     return last, totals, ahead
 
 

time: 94.3 us -> 94.4 us (level)
    ppermute x6 -> x5, waiting for transfers between devices: 12.3 us -> 14 us  [down(): return lax.ppermute(array, ('z', 'c'), DOWN)]
    ppermute x5 -> x6, waiting for transfers between devices: 5.12 us -> 3.66 us  [up(): return lax.ppermute(array, ('z', 'c'), UP)]
    ppermute x6 -> x5, starting transfers between devices: 2.6 us -> 3.06 us  [down(): return lax.ppermute(array, ('z', 'c'), DOWN)]
    ppermute x5 -> x6, starting transfers between devices: 10.9 us -> 10.9 us  [up(): return lax.ppermute(array, ('z', 'c'), UP)]
  transfers between devices with their start and end apart: 19 -> 19, of which waited for: 11 -> 9; matrix products, arithmetic and copies ran while one was open for 5% -> 5% of each run, Pallas kernels for 28% -> 28%
where the time goes in v7:
time: 94.4 us; the launch traced here: 94.1 us
  Pallas kernels  33.7 us (36%)
  starting transfers between devices  31.7 us (34%)
  waiting for transfers between devices  23 us (24%)
  other arithmetic  4 us (4%)
  local copies, waits for them, and re-layouts  1.28 us (1%)
    pallas_call x4, Pallas kernels, project_early(): pl.pallas_call(kernel, out_shape=(shape, shape), in_specs=[SMEM] + [VMEM]...  15.3 us
    ppermute x5, waiting for transfers between devices, down(): return lax.ppermute(array, ('z', 'c'), DOWN)  14 us
    ppermute x6, starting transfers between devices, up(): return lax.ppermute(array, ('z', 'c'), UP)  10.9 us
    ppermute x4, starting transfers between devices, across(): return lax.ppermute(array, 'xh', SWAP)  9.21 us
    pallas_call x2, Pallas kernels, hold_tokens(): pl.pallas_call(kernel, out_shape=pltpu.VMEM((NZ, ROWS, DEPTH), jnp.bfloat...  7.83 us
    all_to_all x1, waiting for transfers between devices, shards(): lax.all_to_all(spread, ('c',) + TENSOR, split_axis=0, concat_axis=0, tile...  5 us
    pallas_call x2, Pallas kernels, project_late(): pl.pallas_call(kernel, out_shape=(shape, weight_shape) if first else shap...  4.92 us
    pallas_call x1, Pallas kernels, attend(): pl.pallas_call(kernel, out_shape=jax.ShapeDtypeStruct((ROWS, 8 * HEAD), j...  4.86 us
  transfers between devices with their start and end apart: 19, of which 9 were waited for; matrix products, arithmetic and copies ran while one was open for 5% of the time, Pallas kernels for 28%

profile of v7, /device:TPU:1, one launch (start us, length us, event | category | flops | bytes accessed | tf_op | source)
XLA Modules:
  0.0 94.1 jit_solution(3807944453218105114)
XLA Ops:
  0.0 3.2 %collective-permute-start.6 = (bf16[768,5120]{1,0:T(8,128)(2,1)}, bf16[768,5120]{1,0:T(8,128)(2,1)}, u32[]{:S(2)}, u32[]{:S(2)}) collective-permute-start(bf16[768,5120]{1,0:T(8,128)(2,1)} %token_ref.1), channel_id=1, source_target_pairs={{0,8},{8,0},{1,9},{9,1},{2,10},{10,2},{3,11},{11,3},{4,12},{12,4},... | collective-permute-start | bytes 23592968 | tf_op jit(solution)/shard_map/ppermute | solution.py:332
  3.2 1.0 %copy-done = bf16[20,10240]{1,0:T(8,128)(2,1)S(1)} copy-done((bf16[20,10240]{1,0:T(8,128)(2,1)S(1)}, bf16[20,10240]{1,0:T(8,128)(2,1)}, u32[]{:S(2)}) %copy-start) | copy-done | bytes 409624
  4.3 0.8 regroup.1
  5.1 4.2 %all-to-all-start = ((bf16[16,20,640]{2,1,0:T(8,128)(2,1)}), bf16[16,20,640]{2,1,0:T(8,128)(2,1)S(1)}, u32[]{:S(2)}, u32[]{:S(2)}) async-start(bf16[16,20,640]{2,1,0:T(8,128)(2,1)} %regroup.1), calls=%async_computation | async-start | bytes 983040 | tf_op jit(solution)/shard_map/all_to_all | solution.py:335
  9.9 2.8 %fusion.1 = (f32[768,64]{1,0:T(8,128)S(1)}, f32[768,64]{1,0:T(8,128)S(1)}, f32[768,64]{1,0:T(8,128)S(1)}, f32[768,64]{1,0:T(8,128)S(1)}, f32[768,64]{1,0:T(8,128)S(1)}, /*index=5*/f32[768,64]{1,0:T(8,128)S(1)}) fusion(f32[64]{0:T(128)S(1)} %multiply_power_fusion, f32[768]{0:T(1024)S(1)} %subtract_convert_fusion, f32[768]{0:T(1024)S(1)} %subtract_convert_fusion.1), kind=kLoop, calls=%fused_computation.9 | loop fusion | flops 196608 | bytes 1186048 | tf_op jit(solution)/shard_map/neg | solution.py:48
  13.3 5.0 %all-to-all-done = bf16[16,20,640]{2,1,0:T(8,128)(2,1)S(1)} async-done(((bf16[16,20,640]{2,1,0:T(8,128)(2,1)}), bf16[16,20,640]{2,1,0:T(8,128)(2,1)S(1)}, u32[]{:S(2)}, u32[]{:S(2)}) %all-to-all-start) | async-done | bytes 409632 | tf_op jit(solution)/shard_map/all_to_all | solution.py:335
  18.4 5.7 %collective-permute-start.1 = (bf16[320,640]{1,0:T(8,128)(2,1)S(1)}, bf16[320,640]{1,0:T(8,128)(2,1)S(1)}, u32[]{:S(2)}, u32[]{:S(2)}) collective-permute-start(bf16[320,640]{1,0:T(8,128)(2,1)S(1)} %reshape.42.refs_0_), channel_id=1, source_target_pairs={{0,32},{8,232},{32,64},{40,8},{64,96},{72,40},{96,128},{104,72},{1... | collective-permute-start | bytes 1228808 | tf_op jit(solution)/shard_map/ppermute | solution.py:75
  24.0 2.5 %collective-permute-start.5 = (bf16[320,640]{1,0:T(8,128)(2,1)S(1)}, bf16[320,640]{1,0:T(8,128)(2,1)S(1)}, u32[]{:S(2)}, u32[]{:S(2)}) collective-permute-start(bf16[320,640]{1,0:T(8,128)(2,1)S(1)} %reshape.42.refs_0_), channel_id=1, source_target_pairs={{0,16},{16,0},{1,17},{17,1},{2,18},{18,2},{3,19},{19,3},{4,20},{20... | collective-permute-start | bytes 1228808 | tf_op jit(solution)/shard_map/ppermute | solution.py:81
  26.5 3.9 %hold_tokens.2.refs_2_.refs_4_.refs_1_ = bf16[8,768,640]{2,1,0:T(8,128)(2,1)S(1)} custom-call(s32[3]{0:T(128)S(1)} %pad_add_fusion.place_ref, bf16[768,5120]{1,0:T(8,128)(2,1)} %token_ref.1), custom_call_target="tpu_custom_call" | custom-call | bytes 16777216 | tf_op jit(solution)/shard_map/hold_tokens/pallas_call | solution.py:160
  30.5 1.1 %collective-permute-done.1.refs_0_ = bf16[320,640]{1,0:T(8,128)(2,1)S(1)} collective-permute-done((bf16[320,640]{1,0:T(8,128)(2,1)S(1)}, bf16[320,640]{1,0:T(8,128)(2,1)S(1)}, u32[]{:S(2)}, u32[]{:S(2)}) %collective-permute-start.1) | collective-permute-done | bytes 409632 | tf_op jit(solution)/shard_map/ppermute | solution.py:75
  31.6 3.7 %collective-permute-done.2.refs_2_ = bf16[320,640]{1,0:T(8,128)(2,1)S(1)} collective-permute-done((bf16[320,640]{1,0:T(8,128)(2,1)S(1)}, bf16[320,640]{1,0:T(8,128)(2,1)S(1)}, u32[]{:S(2)}, u32[]{:S(2)}) %collective-permute-start.2) | collective-permute-done | bytes 409632 | tf_op jit(solution)/shard_map/ppermute | solution.py:78
  35.4 1.3 %collective-permute-start.4 = (bf16[320,640]{1,0:T(8,128)(2,1)S(1)}, bf16[320,640]{1,0:T(8,128)(2,1)S(1)}, u32[]{:S(2)}, u32[]{:S(2)}) collective-permute-start(bf16[320,640]{1,0:T(8,128)(2,1)S(1)} %collective-permute-done.2.refs_2_), channel_id=1, source_target_pairs={{32,0},{232,8},{64,32},{8,40},{96,64},{40,72},{128,96},{72,104},{1... | collective-permute-start | bytes 1228808 | tf_op jit(solution)/shard_map/ppermute | solution.py:78
  36.8 2.3 %collective-permute-start.9 = (bf16[320,640]{1,0:T(8,128)(2,1)S(1)}, bf16[320,640]{1,0:T(8,128)(2,1)S(1)}, u32[]{:S(2)}, u32[]{:S(2)}) collective-permute-start(bf16[320,640]{1,0:T(8,128)(2,1)S(1)} %collective-permute-done.1.refs_0_), channel_id=1, source_target_pairs={{0,16},{16,0},{1,17},{17,1},{2,18},{18,2},{3,19},{19,3},{4,20},{20... | collective-permute-start | bytes 1228808 | tf_op jit(solution)/shard_map/ppermute | solution.py:81
  39.1 3.9 %hold_tokens.3.refs_3_.refs_5_.refs_2_ = bf16[8,768,640]{2,1,0:T(8,128)(2,1)S(1)} custom-call(s32[3]{0:T(128)S(1)} %pad_add_fusion.place_ref, bf16[768,5120]{1,0:T(8,128)(2,1)} %collective-permute-done.6.token_ref), custom_call_target="tpu_custom_call" | custom-call | bytes 16777216 | tf_op jit(solution)/shard_map/hold_tokens/pallas_call | solution.py:160
  43.0 2.5 %project_early.4 = (f32[768,640]{1,0:T(8,128)S(1)}, f32[768,640]{1,0:T(8,128)S(1)}) custom-call(s32[3]{0:T(128)S(1)} %pad_add_fusion.place_ref, bf16[320,640]{1,0:T(8,128)(2,1)S(1)} %reshape.42.refs_0_, bf16[320,640]{1,0:T(8,128)(2,1)S(1)} %collective-permute-done.5.refs_1_, bf16[8,768,640]{2,1,0:T(8,128)(2,1)S(1)} %hold_tokens.2.refs_2_.refs_4_.refs_1_, ...), custom_call_target="tpu_custom_call" | custom-call | flops 1258291200 | bytes 18874368 | tf_op jit(solution)/shard_map/project_early/pallas_call | solution.py:191
  45.5 1.2 %collective-permute-done.3.refs_0_ = bf16[320,640]{1,0:T(8,128)(2,1)S(1)} collective-permute-done((bf16[320,640]{1,0:T(8,128)(2,1)S(1)}, bf16[320,640]{1,0:T(8,128)(2,1)S(1)}, u32[]{:S(2)}, u32[]{:S(2)}) %collective-permute-start.3) | collective-permute-done | bytes 409632 | tf_op jit(solution)/shard_map/ppermute | solution.py:75
  47.4 1.1 %collective-permute-start.7 = (bf16[320,640]{1,0:T(8,128)(2,1)S(1)}, bf16[320,640]{1,0:T(8,128)(2,1)S(1)}, u32[]{:S(2)}, u32[]{:S(2)}) collective-permute-start(bf16[320,640]{1,0:T(8,128)(2,1)S(1)} %collective-permute-done.3.refs_0_), channel_id=1, source_target_pairs={{0,32},{8,232},{32,64},{40,8},{64,96},{72,40},{96,128},{104,72},{1... | collective-permute-start | bytes 1228808 | tf_op jit(solution)/shard_map/ppermute | solution.py:75
  48.8 2.3 %collective-permute-start.13 = (bf16[320,640]{1,0:T(8,128)(2,1)S(1)}, bf16[320,640]{1,0:T(8,128)(2,1)S(1)}, u32[]{:S(2)}, u32[]{:S(2)}) collective-permute-start(bf16[320,640]{1,0:T(8,128)(2,1)S(1)} %collective-permute-done.9.refs_1_), channel_id=1, source_target_pairs={{0,32},{8,232},{32,64},{40,8},{64,96},{72,40},{96,128},{104,72},{1... | collective-permute-start | bytes 1228808 | tf_op jit(solution)/shard_map/ppermute | solution.py:75
  51.1 1.3 %collective-permute-start.14 = (bf16[320,640]{1,0:T(8,128)(2,1)S(1)}, bf16[320,640]{1,0:T(8,128)(2,1)S(1)}, u32[]{:S(2)}, u32[]{:S(2)}) collective-permute-start(bf16[320,640]{1,0:T(8,128)(2,1)S(1)} %collective-permute-done.4.refs_2_), channel_id=1, source_target_pairs={{0,16},{16,0},{1,17},{17,1},{2,18},{18,2},{3,19},{19,3},{4,20},{20... | collective-permute-start | bytes 1228808 | tf_op jit(solution)/shard_map/ppermute | solution.py:81
  52.5 4.3 %project_early.5 = (f32[768,640]{1,0:T(8,128)S(1)}, f32[768,640]{1,0:T(8,128)S(1)}) custom-call(s32[3]{0:T(128)S(1)} %pad_add_fusion.place_ref, bf16[320,640]{1,0:T(8,128)(2,1)S(1)} %collective-permute-done.1.refs_0_, bf16[320,640]{1,0:T(8,128)(2,1)S(1)} %collective-permute-done.9.refs_1_, ...), custom_call_target="tpu_custom_call", output_to_operand_aliasing={{0}: (7, {}), {1}: (8, {})} | custom-call | flops 2516582400 | bytes 18874368 | tf_op jit(solution)/shard_map/project_early/pallas_call | solution.py:191
  56.7 2.5 %collective-permute-done.8.refs_2_ = bf16[320,640]{1,0:T(8,128)(2,1)S(1)} collective-permute-done((bf16[320,640]{1,0:T(8,128)(2,1)S(1)}, bf16[320,640]{1,0:T(8,128)(2,1)S(1)}, u32[]{:S(2)}, u32[]{:S(2)}) %collective-permute-start.8) | collective-permute-done | bytes 409632 | tf_op jit(solution)/shard_map/ppermute | solution.py:78
  59.3 3.1 %collective-permute-start.12 = (bf16[320,640]{1,0:T(8,128)(2,1)S(1)}, bf16[320,640]{1,0:T(8,128)(2,1)S(1)}, u32[]{:S(2)}, u32[]{:S(2)}) collective-permute-start(bf16[320,640]{1,0:T(8,128)(2,1)S(1)} %collective-permute-done.8.refs_2_), channel_id=1, source_target_pairs={{0,16},{16,0},{1,17},{17,1},{2,18},{18,2},{3,19},{19,3},{4,20},{20... | collective-permute-start | bytes 1228808 | tf_op jit(solution)/shard_map/ppermute | solution.py:81
  62.4 1.3 %collective-permute-done.13.refs_1_ = bf16[320,640]{1,0:T(8,128)(2,1)S(1)} collective-permute-done((bf16[320,640]{1,0:T(8,128)(2,1)S(1)}, bf16[320,640]{1,0:T(8,128)(2,1)S(1)}, u32[]{:S(2)}, u32[]{:S(2)}) %collective-permute-start.13) | collective-permute-done | bytes 409632 | tf_op jit(solution)/shard_map/ppermute | solution.py:75
  63.7 1.7 %collective-permute-start.16 = (bf16[320,640]{1,0:T(8,128)(2,1)S(1)}, bf16[320,640]{1,0:T(8,128)(2,1)S(1)}, u32[]{:S(2)}, u32[]{:S(2)}) collective-permute-start(bf16[320,640]{1,0:T(8,128)(2,1)S(1)} %collective-permute-done.13.refs_1_), channel_id=1, source_target_pairs={{0,32},{8,232},{32,64},{40,8},{64,96},{72,40},{96,128},{104,72},{1... | collective-permute-start | bytes 1228808 | tf_op jit(solution)/shard_map/ppermute | solution.py:75
  65.4 4.3 %project_early.6 = (f32[768,640]{1,0:T(8,128)S(1)}, f32[768,640]{1,0:T(8,128)S(1)}) custom-call(s32[3]{0:T(128)S(1)} %pad_add_fusion.place_ref, bf16[320,640]{1,0:T(8,128)(2,1)S(1)} %collective-permute-done.3.refs_0_, bf16[320,640]{1,0:T(8,128)(2,1)S(1)} %collective-permute-done.13.refs_1_, ...), custom_call_target="tpu_custom_call", output_to_operand_aliasing={{0}: (7, {}), {1}: (8, {})} | custom-call | flops 2516582400 | bytes 18874368 | tf_op jit(solution)/shard_map/project_early/pallas_call | solution.py:191
  70.1 1.4 %collective-permute-start.15 = (bf16[320,640]{1,0:T(8,128)(2,1)S(1)}, bf16[320,640]{1,0:T(8,128)(2,1)S(1)}, u32[]{:S(2)}, u32[]{:S(2)}) collective-permute-start(bf16[320,640]{1,0:T(8,128)(2,1)S(1)} %collective-permute-done.12.refs_3_), channel_id=1, source_target_pairs={{32,0},{232,8},{64,32},{8,40},{96,64},{40,72},{128,96},{72,104},{1... | collective-permute-start | bytes 1228808 | tf_op jit(solution)/shard_map/ppermute | solution.py:78
  71.4 4.3 %project_early.7 = (f32[768,640]{1,0:T(8,128)S(1)}, f32[768,640]{1,0:T(8,128)S(1)}) custom-call(s32[3]{0:T(128)S(1)} %pad_add_fusion.place_ref, bf16[320,640]{1,0:T(8,128)(2,1)S(1)} %collective-permute-done.7.refs_0_, bf16[320,640]{1,0:T(8,128)(2,1)S(1)} %collective-permute-done.16.refs_1_, ...), custom_call_target="tpu_custom_call", output_to_operand_aliasing={{0}: (7, {}), {1}: (8, {})} | custom-call | flops 2516582400 | bytes 18874368 | tf_op jit(solution)/shard_map/project_early/pallas_call | solution.py:191
  75.7 7.1 %collective-permute-done.15.refs_1_ = bf16[320,640]{1,0:T(8,128)(2,1)S(1)} collective-permute-done((bf16[320,640]{1,0:T(8,128)(2,1)S(1)}, bf16[320,640]{1,0:T(8,128)(2,1)S(1)}, u32[]{:S(2)}, u32[]{:S(2)}) %collective-permute-start.15) | collective-permute-done | bytes 409632 | tf_op jit(solution)/shard_map/ppermute | solution.py:78
  82.8 2.5 %project_late.2 = (bf16[768,640]{1,0:T(8,128)(2,1)S(1)}, bf16[640,640]{1,0:T(8,128)(2,1)S(1)}) custom-call(s32[3]{0:T(128)S(1)} %pad_add_fusion.place_ref, bf16[320,640]{1,0:T(8,128)(2,1)S(1)} %collective-permute-done.11.refs_0_, bf16[320,640]{1,0:T(8,128)(2,1)S(1)} %collective-permute-done.15.refs_1_, ...), custom_call_target="tpu_custom_call" | custom-call | flops 629145600 | bytes 9437184 | tf_op jit(solution)/shard_map/project_late/pallas_call | solution.py:250
  85.3 1.1 %collective-permute-start.17 = (bf16[768,640]{1,0:T(8,128)(2,1)S(1)}, bf16[768,640]{1,0:T(8,128)(2,1)S(1)}, u32[]{:S(2)}, u32[]{:S(2)}) collective-permute-start(bf16[768,640]{1,0:T(8,128)(2,1)S(1)} %get-tuple-element.74), channel_id=1, source_target_pairs={{0,8},{8,0},{1,9},{9,1},{2,10},{10,2},{3,11},{11,3},{4,12},{12,4},... | collective-permute-start | bytes 2949128 | tf_op jit(solution)/shard_map/ppermute | solution.py:349
  86.6 2.4 %project_late.3.own_ref = bf16[768,640]{1,0:T(8,128)(2,1)S(1)} custom-call(s32[3]{0:T(128)S(1)} %pad_add_fusion.place_ref, bf16[640,640]{1,0:T(8,128)(2,1)S(1)} %get-tuple-element.70.refs_0_, bf16[8,768,640]{2,1,0:T(8,128)(2,1)S(1)} %hold_tokens.2.refs_2_.refs_4_.refs_1_, f32[768,640]{1,0:T(8,128)S(1)} %get-tuple-element.71.refs_2_, ...), custom_call_target="tpu_custom_call" | custom-call | flops 629145600 | bytes 9437184 | tf_op jit(solution)/shard_map/project_late/pallas_call | solution.py:250
  89.1 4.9 %attend.1 = bf16[768,1024]{1,0:T(8,128)(2,1)} custom-call(s32[3]{0:T(128)S(1)} %pad_add_fusion.place_ref, bf16[768,640]{1,0:T(8,128)(2,1)S(1)} %project_late.3.own_ref, bf16[768,640]{1,0:T(8,128)(2,1)S(1)} %collective-permute-done.17.received_ref, s32[768,1]{1,0:T(8,128)S(1)} %reduce_max.23.start_ref), custom_call_target="tpu_custom_call" | custom-call | flops 1610612736 | bytes 4194304 | tf_op jit(solution)/shard_map/attend/pallas_call | solution.py:309
  (39 shorter events, 3.1 us)
Async XLA Ops:
  0.0 39.1 %collective-permute-start.6 = (bf16[768,5120]{1,0:T(8,128)(2,1)}, bf16[768,5120]{1,0:T(8,128)(2,1)}, u32[]{:S(2)}, u32[]{:S(2)}) collective-permute-start(bf16[768,5120]{1,0:T(8,128)(2,1)} %token_ref.1), channel_id=1, source_target_pairs={{0,8},{8,0},{1,9},{9,1},{2,10},{10,2},{3,11},{11,3},{4,12},{12,4},... | collective-permute-start | bytes 23592968 | tf_op jit(solution)/shard_map/ppermute | solution.py:332
  3.2 6.4 %collective-permute-start = (s32[1,8]{1,0:T(1,128)}, s32[1,8]{1,0:T(1,128)S(1)}, u32[]{:S(2)}, u32[]{:S(2)}) collective-permute-start(s32[1,8]{1,0:T(1,128)} %param.6), channel_id=1, source_target_pairs={{0,8},{8,0},{1,9},{9,1},{2,10},{10,2},{3,11},{11,3},{4,12},{12,4},... | collective-permute-start | bytes 104 | tf_op jit(solution)/shard_map/ppermute | solution.py:333
  3.2 1.0 %copy-start = (bf16[20,10240]{1,0:T(8,128)(2,1)S(1)}, bf16[20,10240]{1,0:T(8,128)(2,1)}, u32[]{:S(2)}) copy-start(bf16[20,10240]{1,0:T(8,128)(2,1)} %weight_ref.1) | copy-start | bytes 1228804
  4.3 5.0 %copy-start.3 = (s32[1,8]{1,0:T(1,128)S(1)}, s32[1,8]{1,0:T(1,128)}, u32[]{:S(2)}) copy-start(s32[1,8]{1,0:T(1,128)} %param.6) | copy-start | bytes 100
  5.1 13.2 %all-to-all-start = ((bf16[16,20,640]{2,1,0:T(8,128)(2,1)}), bf16[16,20,640]{2,1,0:T(8,128)(2,1)S(1)}, u32[]{:S(2)}, u32[]{:S(2)}) async-start(bf16[16,20,640]{2,1,0:T(8,128)(2,1)} %regroup.1), calls=%async_computation | async-start | bytes 983040 | tf_op jit(solution)/shard_map/all_to_all | solution.py:335
  18.4 13.2 %collective-permute-start.1 = (bf16[320,640]{1,0:T(8,128)(2,1)S(1)}, bf16[320,640]{1,0:T(8,128)(2,1)S(1)}, u32[]{:S(2)}, u32[]{:S(2)}) collective-permute-start(bf16[320,640]{1,0:T(8,128)(2,1)S(1)} %reshape.42.refs_0_), channel_id=1, source_target_pairs={{0,32},{8,232},{32,64},{40,8},{64,96},{72,40},{96,128},{104,72},{1... | collective-permute-start | bytes 1228808 | tf_op jit(solution)/shard_map/ppermute | solution.py:75
  24.0 11.3 %collective-permute-start.2 = (bf16[320,640]{1,0:T(8,128)(2,1)S(1)}, bf16[320,640]{1,0:T(8,128)(2,1)S(1)}, u32[]{:S(2)}, u32[]{:S(2)}) collective-permute-start(bf16[320,640]{1,0:T(8,128)(2,1)S(1)} %reshape.42.refs_0_), channel_id=1, source_target_pairs={{32,0},{232,8},{64,32},{8,40},{96,64},{40,72},{128,96},{72,104},{1... | collective-permute-start | bytes 1228808 | tf_op jit(solution)/shard_map/ppermute | solution.py:78
  24.0 12.7 %collective-permute-start.5 = (bf16[320,640]{1,0:T(8,128)(2,1)S(1)}, bf16[320,640]{1,0:T(8,128)(2,1)S(1)}, u32[]{:S(2)}, u32[]{:S(2)}) collective-permute-start(bf16[320,640]{1,0:T(8,128)(2,1)S(1)} %reshape.42.refs_0_), channel_id=1, source_target_pairs={{0,16},{16,0},{1,17},{17,1},{2,18},{18,2},{3,19},{19,3},{4,20},{20... | collective-permute-start | bytes 1228808 | tf_op jit(solution)/shard_map/ppermute | solution.py:81
  35.3 11.4 %collective-permute-start.3 = (bf16[320,640]{1,0:T(8,128)(2,1)S(1)}, bf16[320,640]{1,0:T(8,128)(2,1)S(1)}, u32[]{:S(2)}, u32[]{:S(2)}) collective-permute-start(bf16[320,640]{1,0:T(8,128)(2,1)S(1)} %collective-permute-done.1.refs_0_), channel_id=1, source_target_pairs={{0,32},{8,232},{32,64},{40,8},{64,96},{72,40},{96,128},{104,72},{1... | collective-permute-start | bytes 1228808 | tf_op jit(solution)/shard_map/ppermute | solution.py:75
  35.4 11.9 %collective-permute-start.4 = (bf16[320,640]{1,0:T(8,128)(2,1)S(1)}, bf16[320,640]{1,0:T(8,128)(2,1)S(1)}, u32[]{:S(2)}, u32[]{:S(2)}) collective-permute-start(bf16[320,640]{1,0:T(8,128)(2,1)S(1)} %collective-permute-done.2.refs_2_), channel_id=1, source_target_pairs={{32,0},{232,8},{64,32},{8,40},{96,64},{40,72},{128,96},{72,104},{1... | collective-permute-start | bytes 1228808 | tf_op jit(solution)/shard_map/ppermute | solution.py:78
  36.8 12.1 %collective-permute-start.9 = (bf16[320,640]{1,0:T(8,128)(2,1)S(1)}, bf16[320,640]{1,0:T(8,128)(2,1)S(1)}, u32[]{:S(2)}, u32[]{:S(2)}) collective-permute-start(bf16[320,640]{1,0:T(8,128)(2,1)S(1)} %collective-permute-done.1.refs_0_), channel_id=1, source_target_pairs={{0,16},{16,0},{1,17},{17,1},{2,18},{18,2},{3,19},{19,3},{4,20},{20... | collective-permute-start | bytes 1228808 | tf_op jit(solution)/shard_map/ppermute | solution.py:81
  39.0 13.4 %collective-permute-start.10 = (bf16[320,640]{1,0:T(8,128)(2,1)S(1)}, bf16[320,640]{1,0:T(8,128)(2,1)S(1)}, u32[]{:S(2)}, u32[]{:S(2)}) collective-permute-start(bf16[320,640]{1,0:T(8,128)(2,1)S(1)} %collective-permute-done.5.refs_1_), channel_id=1, source_target_pairs={{32,0},{232,8},{64,32},{8,40},{96,64},{40,72},{128,96},{72,104},{1... | collective-permute-start | bytes 1228808 | tf_op jit(solution)/shard_map/ppermute | solution.py:78
  47.4 9.4 %collective-permute-start.7 = (bf16[320,640]{1,0:T(8,128)(2,1)S(1)}, bf16[320,640]{1,0:T(8,128)(2,1)S(1)}, u32[]{:S(2)}, u32[]{:S(2)}) collective-permute-start(bf16[320,640]{1,0:T(8,128)(2,1)S(1)} %collective-permute-done.3.refs_0_), channel_id=1, source_target_pairs={{0,32},{8,232},{32,64},{40,8},{64,96},{72,40},{96,128},{104,72},{1... | collective-permute-start | bytes 1228808 | tf_op jit(solution)/shard_map/ppermute | solution.py:75
  48.5 10.8 %collective-permute-start.8 = (bf16[320,640]{1,0:T(8,128)(2,1)S(1)}, bf16[320,640]{1,0:T(8,128)(2,1)S(1)}, u32[]{:S(2)}, u32[]{:S(2)}) collective-permute-start(bf16[320,640]{1,0:T(8,128)(2,1)S(1)} %collective-permute-done.4.refs_2_), channel_id=1, source_target_pairs={{32,0},{232,8},{64,32},{8,40},{96,64},{40,72},{128,96},{72,104},{1... | collective-permute-start | bytes 1228808 | tf_op jit(solution)/shard_map/ppermute | solution.py:78
  48.8 14.9 %collective-permute-start.13 = (bf16[320,640]{1,0:T(8,128)(2,1)S(1)}, bf16[320,640]{1,0:T(8,128)(2,1)S(1)}, u32[]{:S(2)}, u32[]{:S(2)}) collective-permute-start(bf16[320,640]{1,0:T(8,128)(2,1)S(1)} %collective-permute-done.9.refs_1_), channel_id=1, source_target_pairs={{0,32},{8,232},{32,64},{40,8},{64,96},{72,40},{96,128},{104,72},{1... | collective-permute-start | bytes 1228808 | tf_op jit(solution)/shard_map/ppermute | solution.py:75
  51.1 14.3 %collective-permute-start.14 = (bf16[320,640]{1,0:T(8,128)(2,1)S(1)}, bf16[320,640]{1,0:T(8,128)(2,1)S(1)}, u32[]{:S(2)}, u32[]{:S(2)}) collective-permute-start(bf16[320,640]{1,0:T(8,128)(2,1)S(1)} %collective-permute-done.4.refs_2_), channel_id=1, source_target_pairs={{0,16},{16,0},{1,17},{17,1},{2,18},{18,2},{3,19},{19,3},{4,20},{20... | collective-permute-start | bytes 1228808 | tf_op jit(solution)/shard_map/ppermute | solution.py:81
  59.3 10.8 %collective-permute-start.12 = (bf16[320,640]{1,0:T(8,128)(2,1)S(1)}, bf16[320,640]{1,0:T(8,128)(2,1)S(1)}, u32[]{:S(2)}, u32[]{:S(2)}) collective-permute-start(bf16[320,640]{1,0:T(8,128)(2,1)S(1)} %collective-permute-done.8.refs_2_), channel_id=1, source_target_pairs={{0,16},{16,0},{1,17},{17,1},{2,18},{18,2},{3,19},{19,3},{4,20},{20... | collective-permute-start | bytes 1228808 | tf_op jit(solution)/shard_map/ppermute | solution.py:81
  63.7 7.7 %collective-permute-start.16 = (bf16[320,640]{1,0:T(8,128)(2,1)S(1)}, bf16[320,640]{1,0:T(8,128)(2,1)S(1)}, u32[]{:S(2)}, u32[]{:S(2)}) collective-permute-start(bf16[320,640]{1,0:T(8,128)(2,1)S(1)} %collective-permute-done.13.refs_1_), channel_id=1, source_target_pairs={{0,32},{8,232},{32,64},{40,8},{64,96},{72,40},{96,128},{104,72},{1... | collective-permute-start | bytes 1228808 | tf_op jit(solution)/shard_map/ppermute | solution.py:75
  65.4 10.3 %collective-permute-start.11 = (bf16[320,640]{1,0:T(8,128)(2,1)S(1)}, bf16[320,640]{1,0:T(8,128)(2,1)S(1)}, u32[]{:S(2)}, u32[]{:S(2)}) collective-permute-start(bf16[320,640]{1,0:T(8,128)(2,1)S(1)} %collective-permute-done.7.refs_0_), channel_id=1, source_target_pairs={{0,32},{8,232},{32,64},{40,8},{64,96},{72,40},{96,128},{104,72},{1... | collective-permute-start | bytes 1228808 | tf_op jit(solution)/shard_map/ppermute | solution.py:75
  70.1 12.8 %copy-start.1 = (f32[128]{0:T(128)S(1)}, f32[128]{0:T(128)}, u32[]{:S(2)}) copy-start(f32[128]{0:T(128)} %param.8) | copy-start | bytes 1540
  70.1 12.8 %copy-start.2 = (f32[128]{0:T(128)S(1)}, f32[128]{0:T(128)}, u32[]{:S(2)}) copy-start(f32[128]{0:T(128)} %param.9) | copy-start | bytes 1540
  70.1 12.8 %collective-permute-start.15 = (bf16[320,640]{1,0:T(8,128)(2,1)S(1)}, bf16[320,640]{1,0:T(8,128)(2,1)S(1)}, u32[]{:S(2)}, u32[]{:S(2)}) collective-permute-start(bf16[320,640]{1,0:T(8,128)(2,1)S(1)} %collective-permute-done.12.refs_3_), channel_id=1, source_target_pairs={{32,0},{232,8},{64,32},{8,40},{96,64},{40,72},{128,96},{72,104},{1... | collective-permute-start | bytes 1228808 | tf_op jit(solution)/shard_map/ppermute | solution.py:78
  85.3 3.7 %collective-permute-start.17 = (bf16[768,640]{1,0:T(8,128)(2,1)S(1)}, bf16[768,640]{1,0:T(8,128)(2,1)S(1)}, u32[]{:S(2)}, u32[]{:S(2)}) collective-permute-start(bf16[768,640]{1,0:T(8,128)(2,1)S(1)} %get-tuple-element.74), channel_id=1, source_target_pairs={{0,8},{8,0},{1,9},{9,1},{2,10},{10,2},{3,11},{11,3},{4,12},{12,4},... | collective-permute-start | bytes 2949128 | tf_op jit(solution)/shard_map/ppermute | solution.py:349
